TPU v7x, 256 devices: a whole 4x4x8 slice. The times are simulated.
256 devices in a mesh: dp: 32 (over z_lo, y, core), cout: 8 (over z_hi, x).
Axes of the slice: x: 4, y: 4, z: 8 (z_hi: 2, z_lo: 4; z = z_hi * 4 + z_lo), core: 2. Of those that a mesh axis runs over, the one named last changes fastest.
Arguments:
- images: bfloat16 [128, 512, 1024], P('dp', 'cout'), may hold values from -6 to 6
- styles: float32 [128, 512], P('dp'), may hold values from -5 to 5
- weight: bfloat16 [9, 512, 512], P(None, 'cout', 'dp'), may hold values from -0.09375 to 0.09375
- cotangent: bfloat16 [128, 512, 1024], P('dp', 'cout'), may hold values from -6 to 6
Outputs:
- output: bfloat16 [128, 512, 1024], P('dp', 'cout')
- input_grad: bfloat16 [128, 512, 1024], P('dp', 'cout')
- style_grad: float32 [128, 512], P('dp', 'cout')
- weight_grad: float32 [9, 512, 512], P(None, 'cout', 'dp')
All inputs are finite; a program needn't handle non-finite values.
Results may differ from a plain program's by a relative error of at most 0.013.
Values may be sent and summed in bfloat16 or wider, within the bound.
No kernel may reach another device: no remote copies, remote signals or barrier semaphores. Data moves between devices by JAX's collectives and lax.ppermute only.
A program may use at most 192 MiB of HBM per device.

v0:
```python
import jax
import jax.numpy as jnp
from jax import lax
from jax.sharding import PartitionSpec as P

RES = 32


epsilon = 1e-08
tap_steps = [(-1, -1), (-1, 0), (-1, 1), (0, -1), (0, 0), (0, 1), (1, -1), (1, 0), (1, 1)]


def displace(source, row_step, col_step, grid_side):
    length = source.shape[-1]
    margin = grid_side + 1
    offset = row_step * grid_side + col_step
    widths = [(0, 0)] * (source.ndim - 1) + [(margin, margin)]
    padded = jnp.pad(source, widths)
    moved = lax.slice_in_dim(
        padded, margin + offset, margin + offset + length, axis=source.ndim - 1
    )
    column = jnp.arange(length) % grid_side + col_step
    inside = (column >= 0) & (column < grid_side)
    return jnp.where(inside, moved, jnp.zeros_like(moved))


def forward_taps(kernel, source, running):
    for tap_index, (row_step, col_step) in enumerate(tap_steps):
        product = jnp.einsum(
            "oi,bip->bop", kernel[tap_index], source, preferred_element_type=jnp.float32
        )
        running = running + displace(product, row_step, col_step, RES)
    return running


def weight_taps(moved, source):
    return jnp.stack(
        [
            jnp.einsum("bop,bip->oi", moved[tap_index], source, preferred_element_type=jnp.float32)
            for tap_index in range(len(tap_steps))
        ]
    )


def on_device(images, styles, weight, cotangent):
    local_inputs = images.shape[1]
    first_channel = lax.axis_index("cout") * local_inputs
    local_styles = lax.dynamic_slice_in_dim(styles, first_channel, local_inputs, 1)
    modulated = (images.astype(jnp.float32) * local_styles[:, :, None]).astype(jnp.bfloat16)
    kernel = lax.all_gather(weight, "dp", axis=2, tiled=True)
    kernel_energy = jnp.sum(jnp.square(kernel.astype(jnp.float32)), axis=0)
    style_square = styles * styles
    energy = jnp.dot(style_square, kernel_energy.T, precision=lax.Precision.HIGHEST)
    demodulation = lax.rsqrt(energy + epsilon)
    empty = jnp.zeros((images.shape[0], weight.shape[1], images.shape[2]), jnp.float32)
    gathered = lax.all_gather(modulated, "cout", axis=1, tiled=True)
    convolved = forward_taps(kernel, gathered, empty)
    factor = demodulation[:, :, None]
    output = (factor * convolved).astype(jnp.bfloat16)
    upstream = cotangent.astype(jnp.float32)
    scaled = (upstream * factor).astype(jnp.bfloat16)
    norm_grad = jnp.sum(upstream * convolved, axis=2)
    energy_grad = -0.5 * norm_grad * demodulation**3
    moved = [displace(scaled, -row_step, -col_step, RES) for row_step, col_step in tap_steps]
    back_terms = jnp.einsum("oi,bop->bip", kernel[0], moved[0], preferred_element_type=jnp.float32)
    for tap_index in range(1, len(tap_steps)):
        back_terms = back_terms + jnp.einsum(
            "oi,bop->bip", kernel[tap_index], moved[tap_index], preferred_element_type=jnp.float32
        )
    style_terms = (
        2.0 * styles * jnp.dot(energy_grad, kernel_energy, precision=lax.Precision.HIGHEST)
    )
    back_mine, style_mine = (
        lax.psum_scatter(
            back_terms.astype(jnp.bfloat16), "cout", scatter_dimension=1, tiled=True
        ).astype(jnp.float32),
        lax.psum_scatter(
            style_terms.astype(jnp.bfloat16), "cout", scatter_dimension=1, tiled=True
        ).astype(jnp.float32),
    )
    input_grad = (back_mine * local_styles[:, :, None]).astype(jnp.bfloat16)
    style_grad = jnp.sum(back_mine * images.astype(jnp.float32), axis=2) + style_mine
    weight_terms = weight_taps(moved, gathered)
    radial = (
        2.0
        * kernel.astype(jnp.float32)
        * jnp.dot(energy_grad.T, style_square, precision=lax.Precision.HIGHEST)[None]
    )
    weight_total = lax.psum_scatter(weight_terms + radial, "dp", scatter_dimension=2, tiled=True)
    image_count = images.shape[0] * lax.axis_size("dp")
    weight_grad = weight_total * (1.0 / image_count)
    return (output, input_grad, style_grad, weight_grad)


def solution(mesh):
    return jax.shard_map(
        on_device,
        mesh=mesh,
        in_specs=(
            P("dp", "cout", None),
            P("dp", None),
            P(None, "cout", "dp"),
            P("dp", "cout", None),
        ),
        out_specs=(
            P("dp", "cout", None),
            P("dp", "cout", None),
            P("dp", "cout"),
            P(None, "cout", "dp"),
        ),
        check_vma=False,
    )
```

profile of v0, /device:TPU:32, one launch (start us, length us, event | category | flops | bytes accessed | tf_op | source)
XLA Modules:
  0.0 535.4 jit_solution(9627659840545433735)
XLA Ops:
  8.0 2.0 fusion.31
  10.1 42.9 %all_gather.6 = bf16[9,64,512]{1,2,0:T(8,128)(2,1)S(1)} all-gather(bf16[9,64,16]{1,2,0:T(8,128)(2,1)} %param.6), channel_id=1, replica_groups=mesh['dp'=32,'cout'=8] {'dp'}, dimensions={2}, use_global_device_ids=true | all-gather | bytes 608256 | tf_op jit(solution)/shard_map/all_gather | solution.py:50
  53.9 66.8 %all-gather.2.cloned.1.call-done = bf16[4,512,1024]{2,1,0:T(8,128)(2,1)} async-done(((bf16[4,64,1024]{2,1,0:T(8,128)(2,1)}), bf16[4,512,1024]{2,1,0:T(8,128)(2,1)}) %all-gather.2.cloned.1.call-update) | async-done | bytes 4194320 | tf_op jit(solution)/shard_map/all_gather | solution.py:56
  120.7 3.2 convolution_bitcast_fusion
  130.1 3.4 fusion.33
  134.1 4.7 fusion.38
  138.7 4.6 fusion.39
  143.3 4.7 fusion.40
  148.0 4.8 fusion.41
  152.8 4.8 fusion.42
  157.5 4.7 fusion.37
  162.2 4.8 fusion.43
  166.9 4.5 fusion.36
  172.6 3.7 fusion.17
  179.1 1.4 fusion.14
  180.5 1.4 fusion.13
  181.9 1.4 fusion.12
  183.3 1.4 fusion.11
  187.8 3.7 copy.38
  191.5 24.1 %fusion = bf16[4,512,1024]{2,1,0:T(8,128)(2,1)} fusion(f32[4,1024,512]{1,2,0:T(8,128)} %fusion.43, f32[4,1024,512]{1,2,0:T(8,128)} %fusion.42, f32[4,1024,512]{1,2,0:T(8,128)} %fusion.41, f32[4,1024,512]{1,2,0:T(8,128)} %fusion.36, f32[4,1024,512]{1,2,0:T(8,128)} %fusion.40, f32[4,1024,512]{1,2,0:T(8,128)} %fusion.39, f32[4,1024,512]{1,2,0:T(8,128)} %fusion.37, ...), kind=kOutput, calls=%fused_computation.1 | convolution fusion | flops 287571968 | bytes 71894016 | tf_op jit(solution)/shard_map/oi,bop->bip/dot_general | solution.py:67
  215.7 33.8 %reduce-scatter.10.cloned.1.call-done = bf16[64,4]{1,0:T(8,128)(2,1)} async-done(((bf16[512,4]{1,0:T(8,128)(2,1)}), bf16[64,4]{1,0:T(8,128)(2,1)}) %reduce-scatter.10.cloned.1.call-update) | async-done | bytes 528
  250.3 128.9 %reduce-scatter.8.cloned.1.call-done = f32[9,64,16]{1,0,2:T(8,128)} async-done(((f32[9,64,512]{1,0,2:T(8,128)}), f32[9,64,16]{1,0,2:T(8,128)}) %reduce-scatter.8.cloned.1.call-update) | async-done | bytes 36880 | tf_op jit(solution)/shard_map/reduce_scatter | solution.py:89
  380.8 145.4 %reduce-scatter.6.cloned.1.call-done = bf16[4,64,1024]{2,1,0:T(8,128)(2,1)} async-done(((bf16[4,512,1024]{2,1,0:T(8,128)(2,1)}), bf16[4,64,1024]{2,1,0:T(8,128)(2,1)}) %reduce-scatter.6.cloned.1.call-update) | async-done | bytes 524304 | tf_op jit(solution)/shard_map/reduce_scatter | solution.py:74
  526.1 2.1 fusion.35
  (43 shorter events, 18.3 us)
Async XLA Ops:
  7.2 46.5 %copy-start.3 = (f32[4,512]{1,0:T(4,128)S(1)}, f32[4,512]{1,0:T(4,128)}, u32[]{:S(2)}) copy-start(f32[4,512]{1,0:T(4,128)} %param.5) | copy-start | bytes 24580
  7.2 113.5 %all-gather.2.cloned.1.call-start = ((), (), s32[]{:S(2)}) async-start(), calls=%async_computation.3 | async-start | bytes 4718592 | tf_op jit(solution)/shard_map/all_gather | solution.py:56
  10.0 239.5 %reduce-scatter.10.cloned.1.call-start = ((), (), s32[]{:S(2)}) async-start(), calls=%async_computation.6 | async-start | bytes 147456
  120.7 3.4 copy-start
  128.4 1.7 copy-start.4
  172.3 206.9 %reduce-scatter.8.cloned.1.call-start = ((), (), s32[]{:S(2)}) async-start(), calls=%async_computation.5 | async-start | bytes 4325376 | tf_op jit(solution)/shard_map/reduce_scatter | solution.py:89
  172.6 3.7 copy-start.1
  191.5 334.7 %reduce-scatter.6.cloned.1.call-start = ((), (), s32[]{:S(2)}) async-start(), calls=%async_computation.4 | async-start | bytes 4718592 | tf_op jit(solution)/shard_map/reduce_scatter | solution.py:74
  215.6 310.5 %copy-start.2 = (bf16[4,64,1024]{2,1,0:T(8,128)(2,1)S(1)}, bf16[4,64,1024]{2,1,0:T(8,128)(2,1)}, u32[]{:S(2)}) copy-start(bf16[4,64,1024]{2,1,0:T(8,128)(2,1)} %param.4) | copy-start | bytes 1572868
Sparse Core Ops, SparseCore 0:
  11.2 109.4 all-gather.1
  172.4 77.0 reduce-scatter.9
  252.0 127.1 reduce-scatter.7
  383.2 142.8 reduce-scatter.5
where the time goes:
time: 537 us; the launch traced here: 535 us
  waiting for transfers between devices  375 us (70%)
  matrix products  89.6 us (17%)
  blocking collectives  42.9 us (8%)
  between operations  14 us (3%)
  local copies, waits for them, and re-layouts  7.55 us (1%)
  other arithmetic  5.96 us (1%)
    reduce_scatter x1, waiting for transfers between devices, on_device(): lax.psum_scatter(back_terms.astype(jnp.bfloat16), 'cout', scatter_dimensi...  145 us
    reduce_scatter x1, waiting for transfers between devices, on_device(): lax.psum_scatter(weight_terms + radial, 'dp', scatter_dimension=2, tiled=...  129 us
    all_gather x1, waiting for transfers between devices, on_device(): gathered = lax.all_gather(modulated, 'cout', axis=1, tiled=True)  66.8 us
    dot_general x8, matrix products, on_device(): jnp.einsum('oi,bop->bip', kernel[tap_index], moved[tap_index], preferred_...  56.8 us
    all_gather x1, blocking collectives, on_device(): kernel = lax.all_gather(weight, 'dp', axis=2, tiled=True)  42.9 us
    unnamed x5, waiting for transfers between devices  33.9 us
    dot_general x9, matrix products, weight_taps(): jnp.einsum('bop,bip->oi', moved[tap_index], source, preferred_element_typ...  14.9 us
    dot_general x9, matrix products, forward_taps(): jnp.einsum('oi,bip->bop', kernel[tap_index], source, preferred_element_ty...  12.5 us
  transfers between devices with their start and end apart: 4, of which 4 were waited for; matrix products, arithmetic and copies ran while one was open for 9% of the time, Pallas kernels for 0%

commit v1 on v0

v1 whole, which is shorter than its diff:
```python
import jax
import jax.numpy as jnp
from jax import lax
from jax.experimental import pallas as pl
from jax.experimental.pallas import tpu as pltpu
from jax.sharding import PartitionSpec as P

RES = 32
epsilon = 1e-08
tap_steps = [(-1, -1), (-1, 0), (-1, 1), (0, -1), (0, 0), (0, 1), (1, -1), (1, 0), (1, 1)]
F32 = jnp.float32
BF16 = jnp.bfloat16
HIGH = lax.Precision.HIGHEST
BOTH = ("dp", "cout")
SIZES = {"l": 4, "y": 4, "c": 2, "h": 2, "x": 4}
MIB = 1 << 20


def flat_index(at):
    return ((at["l"] * 4 + at["y"]) * 2 + at["c"]) * 8 + at["h"] * 4 + at["x"]


def places(names):
    if not names:
        return [{}]
    return [{**rest, names[0]: v} for v in range(SIZES[names[0]]) for rest in places(names[1:])]


def exchange(blocks, along):
    others = [name for name in "lychx" if name not in along]
    groups = [[flat_index({**fixed, **at}) for at in places(along)] for fixed in places(others)]
    return lax.all_to_all(blocks, BOTH, 0, 0, axis_index_groups=groups, tiled=True)


def moved_by(value, name, step):
    pairs = []
    for at in places("lychx"):
        to = {**at, name: (at[name] + step) % SIZES[name]}
        pairs.append((flat_index(at), flat_index(to)))
    return lax.ppermute(value, BOTH, pairs)


def inside(row_step, col_step):
    pixel = lax.broadcasted_iota(jnp.int32, (1, RES * RES), 1)
    row = pixel // RES + row_step
    col = pixel % RES + col_step
    return (row >= 0) & (row < RES) & (col >= 0) & (col < RES)


def shifted(value, row_step, col_step):
    offset = row_step * RES + col_step
    if offset == 0:
        return value
    rolled = pltpu.roll(value, (-offset) % (RES * RES), 1)
    return jnp.where(inside(row_step, col_step), rolled, 0.0)


def back_body(place, style, cot, own, other, back, kernel_t, moved, energy_t, demod, scaled):
    y, core = place[0], place[1]

    @pl.loop(0, 16)
    def _(step):
        k, l = step // 4, step % 4
        for source, at_core in ((own, core), (other, 1 - core)):
            row = pl.multiple_of(((l * 4 + (y + k) % 4) * 2 + at_core) * 16, 16)
            piece = source[k, l]
            kernel_t[pl.ds(row, 16), :] = piece
            wide = piece.astype(F32)
            total = jnp.zeros((16, 256), F32)
            for t in range(9):
                part = wide[:, t * 256 : (t + 1) * 256]
                total = total + part * part
            energy_t[pl.ds(row, 16), :] = total

    row_style = style[...]
    energy = jnp.dot(row_style * row_style, energy_t[...], precision=HIGH, preferred_element_type=F32)
    demod_row = lax.rsqrt(energy + epsilon)
    demod[...] = jnp.transpose(jnp.broadcast_to(demod_row[:1], (128, 256)))
    for j in range(8):
        lanes = slice(j * 128, (j + 1) * 128)
        scaled[:, lanes] = (cot[:, lanes].astype(F32) * demod[...]).astype(BF16).astype(F32)

    @pl.loop(0, 8)
    def _(step):
        row = pl.multiple_of(step * 32, 32)
        value = scaled[pl.ds(row, 32), :]
        for t, (a, c) in enumerate(tap_steps):
            moved[pl.ds(t * 256 + row, 32), :] = shifted(value, -a, -c).astype(BF16)

    @pl.loop(0, 4)
    def _(step):
        lanes = pl.ds(pl.multiple_of(step * 256, 256), 256)
        back[:, lanes] = jnp.dot(
            kernel_t[...], moved[:, lanes], preferred_element_type=F32
        ).astype(BF16)


def main_body(
    place, style, cot, images, kernel_t, moved, energy_t, demod,
    out, send, keep, style_part, products, terms, radial, slope,
):
    y, core = place[0], place[1]

    @pl.loop(0, 4)
    def _(step):
        lanes = pl.ds(pl.multiple_of(step * 256, 256), 256)
        products[:, lanes] = lax.dot_general(
            kernel_t[...], images[:, lanes], (((0,), (0,)), ((), ())), preferred_element_type=F32
        )

    @pl.loop(0, 8)
    def _(step):
        row = pl.multiple_of(step * 32, 32)
        total = products[pl.ds(4 * 256 + row, 32), :]
        for t, (a, c) in enumerate(tap_steps):
            if t != 4:
                total = total + shifted(products[pl.ds(t * 256 + row, 32), :], a, c)
        factor = demod[pl.ds(row, 32), :]
        upstream = cot[pl.ds(row, 32), :].astype(F32)
        norm = jnp.sum(upstream * total, axis=1, keepdims=True)
        slope[pl.ds(row, 32), :] = -0.5 * norm * (factor * factor * factor)
        for j in range(8):
            lanes = slice(j * 128, (j + 1) * 128)
            out[pl.ds(row, 32), lanes] = (factor * total[:, lanes]).astype(BF16)

    slope_row = jnp.transpose(slope[...])
    row_style = style[...]
    style_part[...] = (2.0 * row_style) * lax.dot_general(
        slope_row[:8], energy_t[...], (((1,), (1,)), ((), ())),
        precision=HIGH, preferred_element_type=F32,
    )
    square = jnp.transpose(jnp.broadcast_to((row_style * row_style)[:1], (128, 512)))
    for j in range(2):
        lanes = slice(j * 128, (j + 1) * 128)
        radial[:, lanes] = 2.0 * square * slope_row[:1, lanes]

    @pl.loop(0, 9)
    def _(t):
        lanes = pl.ds(pl.multiple_of(t * 256, 256), 256)
        terms[...] = lax.dot_general(
            images[...], moved[lanes, :], (((1,), (1,)), ((), ())), preferred_element_type=F32
        ) + radial[...] * kernel_t[:, lanes].astype(F32)
        for k in range(4):
            for l in range(4):
                row = (l * 4 + (y + k) % 4) * 32
                mine = pl.multiple_of(row + core * 16, 16)
                theirs = pl.multiple_of(row + (1 - core) * 16, 16)
                keep[k, l, :, lanes] = terms[pl.ds(mine, 16), :]
                send[k, l, :, lanes] = terms[pl.ds(theirs, 16), :].astype(BF16)


def vmem(count):
    return [pl.BlockSpec(memory_space=pltpu.VMEM)] * count


def back_call(place, style, cot, own, other):
    shape = jax.ShapeDtypeStruct
    return pl.pallas_call(
        back_body,
        out_shape=(
            shape((512, 1024), BF16),
            shape((512, 2304), BF16),
            shape((2304, 1024), BF16),
            shape((512, 256), F32),
            shape((256, 128), F32),
        ),
        in_specs=[pl.BlockSpec(memory_space=pltpu.SMEM)] + vmem(4),
        out_specs=tuple(vmem(5)),
        scratch_shapes=[pltpu.VMEM((256, 1024), F32)],
        compiler_params=pltpu.CompilerParams(vmem_limit_bytes=28 * MIB),
        cost_estimate=pl.CostEstimate(
            flops=2 * 512 * 2304 * 1024, bytes_accessed=12 * MIB, transcendentals=256
        ),
        name="back",
    )(place, style, cot, own, other)


def main_call(place, style, cot, images, kernel_t, moved, energy_t, demod):
    shape = jax.ShapeDtypeStruct
    return pl.pallas_call(
        main_body,
        out_shape=(
            shape((256, 1024), BF16),
            shape((4, 4, 16, 2304), BF16),
            shape((4, 4, 16, 2304), F32),
            shape((8, 512), F32),
        ),
        in_specs=[pl.BlockSpec(memory_space=pltpu.SMEM)] + vmem(7),
        out_specs=tuple(vmem(4)),
        scratch_shapes=[
            pltpu.VMEM((2304, 1024), F32),
            pltpu.VMEM((512, 256), F32),
            pltpu.VMEM((512, 256), F32),
            pltpu.VMEM((256, 128), F32),
        ],
        compiler_params=pltpu.CompilerParams(vmem_limit_bytes=40 * MIB),
        cost_estimate=pl.CostEstimate(
            flops=4 * 512 * 2304 * 1024, bytes_accessed=16 * MIB, transcendentals=256
        ),
        name="main",
    )(place, style, cot, images, kernel_t, moved, energy_t, demod)


def on_device(images, styles, weight, cotangent):
    seat = lax.axis_index("cout")
    spot = lax.axis_index("dp")
    place = jnp.stack([(spot // 2) % 4, spot % 2]).astype(jnp.int32)
    local_styles = lax.dynamic_slice_in_dim(styles, seat * 64, 64, 1)
    style = jnp.broadcast_to(lax.dynamic_slice_in_dim(styles, seat % 4, 1, 0), (8, 512))

    packed = jnp.transpose(weight, (2, 0, 1)).reshape(16, 576)
    near = exchange(jnp.broadcast_to(packed[None], (16, 16, 576)), "lx")
    near = near.reshape(4, 4, 16, 9, 64).transpose(0, 2, 3, 1, 4).reshape(4, 16, 2304)
    own = jnp.stack([near] + [moved_by(near, "y", -k) for k in (1, 2, 3)])
    other = moved_by(own, "c", 1)

    cot = exchange(cotangent, "x").reshape(256, 1024)
    modulated = (images.astype(F32) * local_styles[:, :, None]).astype(BF16)
    whole = exchange(jnp.concatenate([modulated, modulated]), "hx").reshape(512, 1024)

    back, kernel_t, moved, energy_t, demod = back_call(place, style, cot, own, other)
    back_parts = exchange(back.reshape(8, 64, 1024), "hx").reshape(2, 4, 64, 1024)

    out, send, keep, style_part = main_call(
        place, style, cot, whole, kernel_t, moved, energy_t, demod
    )
    received = moved_by(send, "c", 1)
    output = exchange(out.reshape(4, 64, 1024), "x")
    style_parts = exchange(style_part[0].reshape(8, 1, 64), "hx").reshape(2, 4, 64)

    halves = (keep + received.astype(F32)).astype(BF16)
    quarters = halves[0].astype(F32)
    for k in (1, 2, 3):
        quarters = quarters + moved_by(halves[k], "y", k).astype(F32)
    blocks = quarters.astype(BF16).reshape(4, 16, 9, 4, 64).transpose(0, 3, 1, 2, 4)
    blocks = exchange(blocks.reshape(16, 16, 576), "lx")
    total = jnp.sum(blocks.astype(F32), axis=0) * (1.0 / 128)
    weight_grad = total.reshape(16, 9, 64).transpose(1, 2, 0)

    back_sum = back_parts[0].astype(F32) + back_parts[1].astype(F32)
    input_grad = (back_sum * local_styles[:, :, None]).astype(BF16)
    style_grad = jnp.sum(back_sum * images.astype(F32), axis=2) + style_parts[0] + style_parts[1]
    return (output, input_grad, style_grad, weight_grad)


def solution(mesh):
    return jax.shard_map(
        on_device,
        mesh=mesh,
        in_specs=(
            P("dp", "cout", None),
            P("dp", None),
            P(None, "cout", "dp"),
            P("dp", "cout", None),
        ),
        out_specs=(
            P("dp", "cout", None),
            P("dp", "cout", None),
            P("dp", "cout"),
            P(None, "cout", "dp"),
        ),
        check_vma=False,
    )
```

time: 537 us -> 194 us (0.36)
  waiting for transfers between devices: 375 us -> 63.7 us
  matrix products: 89.6 us -> 0 us
  starting transfers between devices: 0.38 us -> 28.7 us
  Pallas kernels: 0 us -> 20.7 us
  blocking collectives: 42.9 us -> 62.2 us
  between operations: 14 us -> 0.79 us
    reduce_scatter x2 -> x0, waiting for transfers between devices: 274 us -> none  [the longest x1 145 us: on_device(): lax.psum_scatter(back_terms.astype(jnp.bfloat16), 'cout', scatter_dimensi...]
    dot_general x30 -> x0, matrix products: 89.6 us -> none  [the longest x8 56.8 us: on_device(): jnp.einsum('oi,bop->bip', kernel[tap_index], moved[tap_index], preferred_...]
    all_gather x1 -> x0, waiting for transfers between devices: 66.8 us -> none  [on_device(): gathered = lax.all_gather(modulated, 'cout', axis=1, tiled=True)]
    all_to_all x0 -> x3, blocking collectives: none -> 62.2 us  [exchange(): lax.all_to_all(blocks, BOTH, 0, 0, axis_index_groups=groups, tiled=True)]
    all_to_all x0 -> x4, waiting for transfers between devices: none -> 51.8 us  [exchange(): lax.all_to_all(blocks, BOTH, 0, 0, axis_index_groups=groups, tiled=True)]
    all_gather x1 -> x0, blocking collectives: 42.9 us -> none  [on_device(): kernel = lax.all_gather(weight, 'dp', axis=2, tiled=True)]
    unnamed x5 -> x0, waiting for transfers between devices: 33.9 us -> none
    pallas_call x0 -> x2, Pallas kernels: none -> 20.7 us  [the longest x1 13.3 us: main_call(): pl.pallas_call(main_body, out_shape=(shape((256, 1024), BF16), shape((4,...]
  transfers between devices with their start and end apart: 4 -> 12, of which waited for: 4 -> 7; matrix products, arithmetic and copies ran while one was open for 9% -> 2% of each run, Pallas kernels for 0% -> 0%
where the time goes in v1:
time: 194 us; the launch traced here: 192 us
  waiting for transfers between devices  63.7 us (33%)
  blocking collectives  62.2 us (32%)
  starting transfers between devices  28.7 us (15%)
  Pallas kernels  20.7 us (11%)
  local copies, waits for them, and re-layouts  12.3 us (6%)
  other arithmetic  3.49 us (2%)
    all_to_all x3, blocking collectives, exchange(): lax.all_to_all(blocks, BOTH, 0, 0, axis_index_groups=groups, tiled=True)  62.2 us
    all_to_all x4, waiting for transfers between devices, exchange(): lax.all_to_all(blocks, BOTH, 0, 0, axis_index_groups=groups, tiled=True)  51.8 us
    all_to_all x4, starting transfers between devices, exchange(): lax.all_to_all(blocks, BOTH, 0, 0, axis_index_groups=groups, tiled=True)  18 us
    pallas_call x1, Pallas kernels, main_call(): pl.pallas_call(main_body, out_shape=(shape((256, 1024), BF16), shape((4,...  13.3 us
    ppermute x8, waiting for transfers between devices, moved_by(): return lax.ppermute(value, BOTH, pairs)  11.9 us
    ppermute x8, starting transfers between devices, moved_by(): return lax.ppermute(value, BOTH, pairs)  10.7 us
    pallas_call x1, Pallas kernels, back_call(): pl.pallas_call(back_body, out_shape=(shape((512, 1024), BF16), shape((512...  7.42 us
    unnamed x18, local copies, waits for them, and re-layouts  7.35 us
  transfers between devices with their start and end apart: 12, of which 7 were waited for; matrix products, arithmetic and copies ran while one was open for 2% of the time, Pallas kernels for 0%

profile of v1, /device:TPU:32, one launch (start us, length us, event | category | flops | bytes accessed | tf_op | source)
XLA Modules:
  0.0 191.9 jit_solution(16080623390452625271)
XLA Ops:
  1.6 19.0 %all_to_all.35 = bf16[16,16,576]{2,1,0:T(8,128)(2,1)S(1)} all-to-all(bf16[16,16,576]{2,1,0:T(8,128)(2,1)S(1)} %broadcast_in_dim.19), channel_id=1, replica_groups={{0,1,2,3,64,65,66,67,128,129,130,131,192,193,194,195},{4,5,6,7,68,69,70..., dimensions={0} | all-to-all | bytes 589824 | tf_op jit(solution)/shard_map/all_to_all | solution.py:32
  22.2 1.7 collective-permute-start.2
  23.8 2.9 %collective-permute-start.1 = (bf16[4,16,2304]{2,1,0:T(8,128)(2,1)S(1)}, bf16[4,16,2304]{2,1,0:T(8,128)(2,1)S(1)}, u32[]{:S(2)}, u32[]{:S(2)}) collective-permute-start(bf16[4,16,2304]{2,1,0:T(8,128)(2,1)S(1)} %reshape.53), channel_id=1, source_target_pairs={{0,32},{1,33},{2,34},{3,35},{4,36},{5,37},{6,38},{7,39},{8,40},{9,... | collective-permute-start | bytes 884744 | tf_op jit(solution)/shard_map/ppermute | solution.py:40
  26.7 1.3 collective-permute-start
  28.4 4.3 %collective-permute-done.2 = bf16[4,16,2304]{2,1,0:T(8,128)(2,1)S(1)} collective-permute-done((bf16[4,16,2304]{2,1,0:T(8,128)(2,1)S(1)}, bf16[4,16,2304]{2,1,0:T(8,128)(2,1)S(1)}, u32[]{:S(2)}, u32[]{:S(2)}) %collective-permute-start.2) | collective-permute-done | bytes 294944 | tf_op jit(solution)/shard_map/ppermute | solution.py:40
  32.7 4.7 %collective-permute-done.1 = bf16[4,16,2304]{2,1,0:T(8,128)(2,1)S(1)} collective-permute-done((bf16[4,16,2304]{2,1,0:T(8,128)(2,1)S(1)}, bf16[4,16,2304]{2,1,0:T(8,128)(2,1)S(1)}, u32[]{:S(2)}, u32[]{:S(2)}) %collective-permute-start.1) | collective-permute-done | bytes 294944 | tf_op jit(solution)/shard_map/ppermute | solution.py:40
  37.7 4.1 %all-to-all-start = ((bf16[4,64,1024]{2,1,0:T(8,128)(2,1)}), bf16[4,64,1024]{2,1,0:T(8,128)(2,1)S(1)}, u32[]{:S(2)}, u32[]{:S(2)}) async-start(bf16[4,64,1024]{2,1,0:T(8,128)(2,1)} %param.7), calls=%async_computation | async-start | bytes 1048576 | tf_op jit(solution)/shard_map/all_to_all | solution.py:32
  41.9 10.0 %all-to-all-done = bf16[4,64,1024]{2,1,0:T(8,128)(2,1)S(1)} async-done(((bf16[4,64,1024]{2,1,0:T(8,128)(2,1)}), bf16[4,64,1024]{2,1,0:T(8,128)(2,1)S(1)}, u32[]{:S(2)}, u32[]{:S(2)}) %all-to-all-start) | async-done | bytes 524320 | tf_op jit(solution)/shard_map/all_to_all | solution.py:32
  51.9 7.4 %back.1 = (bf16[512,1024]{1,0:T(8,128)(2,1)}, bf16[512,2304]{1,0:T(8,128)(2,1)S(1)}, bf16[2304,1024]{1,0:T(8,128)(2,1)S(1)}, f32[512,256]{1,0:T(8,128)S(1)}, f32[256,128]{1,0:T(8,128)S(1)}) custom-call(s32[2]{0:T(128)S(1)} %pad_add_fusion.place, f32[8,512]{1,0:T(8,128)S(1)} %broadcast_in_dim.17.style, bf16[256,1024]{1,0:T(8,128)(2,1)S(1)} %bitcast.35, ...), custom_call_target="tpu_custom_call" | custom-call | flops 2415919104 | bytes 12582912 | tf_op jit(solution)/shard_map/back/pallas_call | solution.py:158
  59.3 2.1 %copy-done.1 = bf16[2304,1024]{1,0:T(8,128)(2,1)} copy-done((bf16[2304,1024]{1,0:T(8,128)(2,1)}, bf16[2304,1024]{1,0:T(8,128)(2,1)S(1)}, u32[]{:S(2)}) %copy-start.1) | copy-done | bytes 4718616
  61.4 1.4 copy-done.3
  63.5 6.5 %all-to-all-start.4 = ((bf16[8,64,1024]{2,1,0:T(8,128)(2,1)}), bf16[8,64,1024]{2,1,0:T(8,128)(2,1)S(1)}, u32[]{:S(2)}, u32[]{:S(2)}) async-start(bf16[8,64,1024]{2,1,0:T(8,128)(2,1)} %bitcast.11), calls=%async_computation.4 | async-start | bytes 2097152 | tf_op jit(solution)/shard_map/all_to_all | solution.py:32
  70.1 28.9 %all-to-all-done.4 = bf16[8,64,1024]{2,1,0:T(8,128)(2,1)S(1)} async-done(((bf16[8,64,1024]{2,1,0:T(8,128)(2,1)}), bf16[8,64,1024]{2,1,0:T(8,128)(2,1)S(1)}, u32[]{:S(2)}, u32[]{:S(2)}) %all-to-all-start.4) | async-done | bytes 1048608 | tf_op jit(solution)/shard_map/all_to_all | solution.py:32
  100.3 30.8 %all_to_all.36 = bf16[8,64,1024]{2,1,0:T(8,128)(2,1)S(1)} all-to-all(bf16[8,64,1024]{2,1,0:T(8,128)(2,1)S(1)} %pad_maximum_fusion.1), channel_id=1, replica_groups={{0,1,2,3,4,5,6,7},{8,9,10,11,12,13,14,15},{16,17,18,19,20,21,22,23},{24..., dimensions={0} | all-to-all | bytes 2097152 | tf_op jit(solution)/shard_map/all_to_all | solution.py:32
  131.2 1.7 copy-done.4
  132.8 13.3 %main.1 = (bf16[256,1024]{1,0:T(8,128)(2,1)}, bf16[4,4,16,2304]{3,2,1,0:T(8,128)(2,1)S(1)}, f32[4,4,16,2304]{3,2,1,0:T(8,128)S(1)}, f32[8,512]{1,0:T(8,128)S(1)}) custom-call(s32[2]{0:T(128)S(1)} %pad_add_fusion.place, f32[8,512]{1,0:T(8,128)S(1)} %broadcast_in_dim.17.style, bf16[256,1024]{1,0:T(8,128)(2,1)S(1)} %bitcast.36, bf16[512,1024]{1,0:T(8,128)(2,1)S(1)} %bitcast.34, ...), custom_call_target="tpu_custom_call" | custom-call | flops 4831838208 | bytes 16777216 | tf_op jit(solution)/shard_map/main/pallas_call | solution.py:180
  146.1 2.8 %collective-permute-done.4 = bf16[4,4,16,2304]{3,2,1,0:T(8,128)(2,1)S(1)} collective-permute-done((bf16[4,4,16,2304]{3,2,1,0:T(8,128)(2,1)S(1)}, bf16[4,4,16,2304]{3,2,1,0:T(8,128)(2,1)S(1)}, u32[]{:S(2)}, u32[]{:S(2)}) %collective-permute-start.4) | collective-permute-done | bytes 1179680 | tf_op jit(solution)/shard_map/ppermute | solution.py:40
  150.6 2.0 %collective-permute-start.7 = (bf16[4,16,2304]{2,1,0:T(8,128)(2,1)S(1)}, bf16[4,16,2304]{2,1,0:T(8,128)(2,1)S(1)}, u32[]{:S(2)}, u32[]{:S(2)}) collective-permute-start(bf16[4,16,2304]{2,1,0:T(8,128)(2,1)S(1)} %get-tuple-element.31), channel_id=1, source_target_pairs={{0,48},{1,49},{2,50},{3,51},{4,52},{5,53},{6,54},{7,55},{8,56},{9,... | collective-permute-start | bytes 884744 | tf_op jit(solution)/shard_map/ppermute | solution.py:40
  152.6 1.4 collective-permute-start.6
  154.1 12.4 %all_to_all.37 = f32[8,1,64]{2,1,0:T(1,128)S(1)} all-to-all(f32[8,1,64]{2,1,0:T(1,128)S(1)} %bitcast.44), channel_id=1, replica_groups={{0,1,2,3,4,5,6,7},{8,9,10,11,12,13,14,15},{16,17,18,19,20,21,22,23},{24..., dimensions={0} | all-to-all | bytes 4096 | tf_op jit(solution)/shard_map/all_to_all | solution.py:32
  166.5 3.5 %all-to-all-start.3 = ((bf16[4,64,1024]{2,1,0:T(8,128)(2,1)}), bf16[4,64,1024]{2,1,0:T(8,128)(2,1)S(1)}, u32[]{:S(2)}, u32[]{:S(2)}) async-start(bf16[4,64,1024]{2,1,0:T(8,128)(2,1)} %bitcast.10), calls=%async_computation.3 | async-start | bytes 1048576 | tf_op jit(solution)/shard_map/all_to_all | solution.py:32
  172.9 5.1 %all-to-all-done.3 = bf16[4,64,1024]{2,1,0:T(8,128)(2,1)S(1)} async-done(((bf16[4,64,1024]{2,1,0:T(8,128)(2,1)}), bf16[4,64,1024]{2,1,0:T(8,128)(2,1)S(1)}, u32[]{:S(2)}, u32[]{:S(2)}) %all-to-all-start.3) | async-done | bytes 524320 | tf_op jit(solution)/shard_map/all_to_all | solution.py:32
  178.0 4.0 %all-to-all-start.6 = ((bf16[16,16,576]{2,1,0:T(8,128)(2,1)}), bf16[16,16,576]{2,1,0:T(8,128)(2,1)S(1)}, u32[]{:S(2)}, u32[]{:S(2)}) async-start(bf16[16,16,576]{2,1,0:T(8,128)(2,1)} %reshape.57), calls=%async_computation.6 | async-start | bytes 655360 | tf_op jit(solution)/shard_map/all_to_all | solution.py:32
  182.5 7.8 %all-to-all-done.6 = bf16[16,16,576]{2,1,0:T(8,128)(2,1)S(1)} async-done(((bf16[16,16,576]{2,1,0:T(8,128)(2,1)}), bf16[16,16,576]{2,1,0:T(8,128)(2,1)S(1)}, u32[]{:S(2)}, u32[]{:S(2)}) %all-to-all-start.6) | async-done | bytes 294944 | tf_op jit(solution)/shard_map/all_to_all | solution.py:32
  (50 shorter events, 12.0 us)
Async XLA Ops:
  0.6 41.2 %copy-start = (f32[4,512]{1,0:T(4,128)S(1)}, f32[4,512]{1,0:T(4,128)}, u32[]{:S(2)}) copy-start(f32[4,512]{1,0:T(4,128)} %param.5) | copy-start | bytes 24580
  22.2 10.6 %collective-permute-start.2 = (bf16[4,16,2304]{2,1,0:T(8,128)(2,1)S(1)}, bf16[4,16,2304]{2,1,0:T(8,128)(2,1)S(1)}, u32[]{:S(2)}, u32[]{:S(2)}) collective-permute-start(bf16[4,16,2304]{2,1,0:T(8,128)(2,1)S(1)} %reshape.53), channel_id=1, source_target_pairs={{0,16},{1,17},{2,18},{3,19},{4,20},{5,21},{6,22},{7,23},{8,24},{9,... | collective-permute-start | bytes 884744 | tf_op jit(solution)/shard_map/ppermute | solution.py:40
  23.8 13.6 %collective-permute-start.1 = (bf16[4,16,2304]{2,1,0:T(8,128)(2,1)S(1)}, bf16[4,16,2304]{2,1,0:T(8,128)(2,1)S(1)}, u32[]{:S(2)}, u32[]{:S(2)}) collective-permute-start(bf16[4,16,2304]{2,1,0:T(8,128)(2,1)S(1)} %reshape.53), channel_id=1, source_target_pairs={{0,32},{1,33},{2,34},{3,35},{4,36},{5,37},{6,38},{7,39},{8,40},{9,... | collective-permute-start | bytes 884744 | tf_op jit(solution)/shard_map/ppermute | solution.py:40
  26.7 10.7 %collective-permute-start = (bf16[4,16,2304]{2,1,0:T(8,128)(2,1)S(1)}, bf16[4,16,2304]{2,1,0:T(8,128)(2,1)S(1)}, u32[]{:S(2)}, u32[]{:S(2)}) collective-permute-start(bf16[4,16,2304]{2,1,0:T(8,128)(2,1)S(1)} %reshape.53), channel_id=1, source_target_pairs={{0,48},{1,49},{2,50},{3,51},{4,52},{5,53},{6,54},{7,55},{8,56},{9,... | collective-permute-start | bytes 884744 | tf_op jit(solution)/shard_map/ppermute | solution.py:40
  37.6 14.3 %collective-permute-start.3 = (bf16[4,4,16,2304]{3,2,1,0:T(8,128)(2,1)S(1)}, bf16[4,4,16,2304]{3,2,1,0:T(8,128)(2,1)S(1)}, u32[]{:S(2)}, u32[]{:S(2)}) collective-permute-start(bf16[4,4,16,2304]{3,2,1,0:T(8,128)(2,1)S(1)} %pad_maximum_fusion.own), channel_id=1, source_target_pairs={{0,8},{1,9},{2,10},{3,11},{4,12},{5,13},{6,14},{7,15},{8,0},{9,1},... | collective-permute-start | bytes 3538952 | tf_op jit(solution)/shard_map/ppermute | solution.py:40
  37.7 14.2 %all-to-all-start = ((bf16[4,64,1024]{2,1,0:T(8,128)(2,1)}), bf16[4,64,1024]{2,1,0:T(8,128)(2,1)S(1)}, u32[]{:S(2)}, u32[]{:S(2)}) async-start(bf16[4,64,1024]{2,1,0:T(8,128)(2,1)} %param.7), calls=%async_computation | async-start | bytes 1048576 | tf_op jit(solution)/shard_map/all_to_all | solution.py:32
  59.3 2.1 %copy-start.1 = (bf16[2304,1024]{1,0:T(8,128)(2,1)}, bf16[2304,1024]{1,0:T(8,128)(2,1)S(1)}, u32[]{:S(2)}) copy-start(bf16[2304,1024]{1,0:T(8,128)(2,1)S(1)} %get-tuple-element.14.moved) | copy-start | bytes 14155780
  61.4 1.4 copy-start.3
  62.9 0.7 copy-start.5
  63.5 35.5 %copy-start.7 = (bf16[4,64,1024]{2,1,0:T(8,128)(2,1)S(1)}, bf16[4,64,1024]{2,1,0:T(8,128)(2,1)}, u32[]{:S(2)}) copy-start(bf16[4,64,1024]{2,1,0:T(8,128)(2,1)} %param.4) | copy-start | bytes 1572868
  63.5 35.5 %all-to-all-start.4 = ((bf16[8,64,1024]{2,1,0:T(8,128)(2,1)}), bf16[8,64,1024]{2,1,0:T(8,128)(2,1)S(1)}, u32[]{:S(2)}, u32[]{:S(2)}) async-start(bf16[8,64,1024]{2,1,0:T(8,128)(2,1)} %bitcast.11), calls=%async_computation.4 | async-start | bytes 2097152 | tf_op jit(solution)/shard_map/all_to_all | solution.py:32
  99.1 32.1 %copy-start.2 = (bf16[2304,1024]{1,0:T(8,128)(2,1)S(1)}, bf16[2304,1024]{1,0:T(8,128)(2,1)}, u32[]{:S(2)}) copy-start(bf16[2304,1024]{1,0:T(8,128)(2,1)} %copy-done.1) | copy-start | bytes 14155780
  100.3 30.8 %copy-start.6 = (f32[256,128]{1,0:T(8,128)S(1)}, f32[256,128]{1,0:T(8,128)}, u32[]{:S(2)}) copy-start(f32[256,128]{1,0:T(8,128)} %copy-done.5) | copy-start | bytes 393220
  131.2 1.7 copy-start.4
  146.1 2.8 %collective-permute-start.4 = (bf16[4,4,16,2304]{3,2,1,0:T(8,128)(2,1)S(1)}, bf16[4,4,16,2304]{3,2,1,0:T(8,128)(2,1)S(1)}, u32[]{:S(2)}, u32[]{:S(2)}) collective-permute-start(bf16[4,4,16,2304]{3,2,1,0:T(8,128)(2,1)S(1)} %get-tuple-element.21), channel_id=1, source_target_pairs={{0,8},{1,9},{2,10},{3,11},{4,12},{5,13},{6,14},{7,15},{8,0},{9,1},... | collective-permute-start | bytes 3538952 | tf_op jit(solution)/shard_map/ppermute | solution.py:40
  149.3 20.7 %collective-permute-start.5 = (bf16[4,16,2304]{2,1,0:T(8,128)(2,1)S(1)}, bf16[4,16,2304]{2,1,0:T(8,128)(2,1)S(1)}, u32[]{:S(2)}, u32[]{:S(2)}) collective-permute-start(bf16[4,16,2304]{2,1,0:T(8,128)(2,1)S(1)} %get-tuple-element.30), channel_id=1, source_target_pairs={{0,16},{1,17},{2,18},{3,19},{4,20},{5,21},{6,22},{7,23},{8,24},{9,... | collective-permute-start | bytes 884744 | tf_op jit(solution)/shard_map/ppermute | solution.py:40
  150.6 19.4 %collective-permute-start.7 = (bf16[4,16,2304]{2,1,0:T(8,128)(2,1)S(1)}, bf16[4,16,2304]{2,1,0:T(8,128)(2,1)S(1)}, u32[]{:S(2)}, u32[]{:S(2)}) collective-permute-start(bf16[4,16,2304]{2,1,0:T(8,128)(2,1)S(1)} %get-tuple-element.31), channel_id=1, source_target_pairs={{0,48},{1,49},{2,50},{3,51},{4,52},{5,53},{6,54},{7,55},{8,56},{9,... | collective-permute-start | bytes 884744 | tf_op jit(solution)/shard_map/ppermute | solution.py:40
  152.6 17.4 %collective-permute-start.6 = (bf16[4,16,2304]{2,1,0:T(8,128)(2,1)S(1)}, bf16[4,16,2304]{2,1,0:T(8,128)(2,1)}, u32[]{:S(2)}, u32[]{:S(2)}) collective-permute-start(bf16[4,16,2304]{2,1,0:T(8,128)(2,1)S(1)} %get-tuple-element.32), channel_id=1, source_target_pairs={{0,32},{1,33},{2,34},{3,35},{4,36},{5,37},{6,38},{7,39},{8,40},{9,... | collective-permute-start | bytes 884744 | tf_op jit(solution)/shard_map/ppermute | solution.py:40
  166.5 11.5 %all-to-all-start.3 = ((bf16[4,64,1024]{2,1,0:T(8,128)(2,1)}), bf16[4,64,1024]{2,1,0:T(8,128)(2,1)S(1)}, u32[]{:S(2)}, u32[]{:S(2)}) async-start(bf16[4,64,1024]{2,1,0:T(8,128)(2,1)} %bitcast.10), calls=%async_computation.3 | async-start | bytes 1048576 | tf_op jit(solution)/shard_map/all_to_all | solution.py:32
  178.0 12.3 %all-to-all-start.6 = ((bf16[16,16,576]{2,1,0:T(8,128)(2,1)}), bf16[16,16,576]{2,1,0:T(8,128)(2,1)S(1)}, u32[]{:S(2)}, u32[]{:S(2)}) async-start(bf16[16,16,576]{2,1,0:T(8,128)(2,1)} %reshape.57), calls=%async_computation.6 | async-start | bytes 655360 | tf_op jit(solution)/shard_map/all_to_all | solution.py:32

commit v2 on v1

v2 whole, which is shorter than its diff:
```python
import jax
import jax.numpy as jnp
from jax import lax
from jax.experimental import pallas as pl
from jax.experimental.pallas import tpu as pltpu
from jax.sharding import PartitionSpec as P

RES = 32
epsilon = 1e-08
tap_steps = [(-1, -1), (-1, 0), (-1, 1), (0, -1), (0, 0), (0, 1), (1, -1), (1, 0), (1, 1)]
F32 = jnp.float32
BF16 = jnp.bfloat16
HIGH = lax.Precision.HIGHEST
BOTH = ("dp", "cout")
SIZES = {"l": 4, "y": 4, "c": 2, "h": 2, "x": 4}
MIB = 1 << 20


def flat_index(at):
    return ((at["l"] * 4 + at["y"]) * 2 + at["c"]) * 8 + at["h"] * 4 + at["x"]


def places(names):
    if not names:
        return [{}]
    return [{**rest, names[0]: v} for v in range(SIZES[names[0]]) for rest in places(names[1:])]


def exchange(blocks, along):
    others = [name for name in "lychx" if name not in along]
    groups = [[flat_index({**fixed, **at}) for at in places(along)] for fixed in places(others)]
    return lax.all_to_all(blocks, BOTH, 0, 0, axis_index_groups=groups, tiled=True)


def moved_by(value, name, step):
    pairs = []
    for at in places("lychx"):
        to = {**at, name: (at[name] + step) % SIZES[name]}
        pairs.append((flat_index(at), flat_index(to)))
    return lax.ppermute(value, BOTH, pairs)


def inside(row_step, col_step):
    pixel = lax.broadcasted_iota(jnp.int32, (1, RES * RES), 1)
    row = pixel // RES + row_step
    col = pixel % RES + col_step
    return (row >= 0) & (row < RES) & (col >= 0) & (col < RES)


def shifted(value, row_step, col_step):
    offset = row_step * RES + col_step
    if offset == 0:
        return value
    rolled = pltpu.roll(value, (-offset) % (RES * RES), 1)
    return jnp.where(inside(row_step, col_step), rolled, 0.0)


def rows_of(place, k, l):
    return (((place[0] + l) % 4) * 4 + (place[1] + k) % 4) * 32


def image_grad_body(
    place, cot0, cot1, cot2, cot3, whole, moved_out, grad_out, moved, grad, images, sems
):
    bring = pltpu.make_async_copy(whole, images, sems.at[10])
    bring.start()
    for k, source in enumerate((cot0, cot1, cot2, cot3)):
        block = ((place[3] + 4 - k) % 4) * 64

        @pl.loop(0, 2)
        def _(half):
            value = source[pl.ds(pl.multiple_of(half * 32, 32), 32), :].astype(F32)
            for t, (a, c) in enumerate(tap_steps):
                row = pl.multiple_of(t * 256 + block + half * 32, 32)
                moved[pl.ds(row, 32), :] = shifted(value, -a, -c).astype(BF16)

    pltpu.make_async_copy(moved, moved_out, sems.at[9]).start()
    bring.wait()

    def leave(t):
        lanes = pl.ds(pl.multiple_of(t * 256, 256), 256)
        return pltpu.make_async_copy(grad.at[:, lanes], grad_out.at[:, lanes], sems.at[t])

    @pl.loop(0, 9)
    def _(t):
        lanes = pl.ds(pl.multiple_of(t * 256, 256), 256)
        grad[:, lanes] = lax.dot_general(
            images[...], moved[lanes, :], (((1,), (1,)), ((), ())), preferred_element_type=F32
        )
        leave(t).start()

    @pl.loop(0, 9)
    def _(t):
        leave(t).wait()

    pltpu.make_async_copy(moved, moved_out, sems.at[9]).wait()


def gradient_body(
    place, style, moved_in, grad_in, own0, own1, own2, own3, other0, other1, other2, other3,
    demod_out, send_out, keep_out, back_out, kernel_out,
    moved, grad, kernel_t, scaled_t, energy_t, inner, demod, send, keep, back, sems,
):
    core = place[2]
    sources = []
    for k, (own, other) in enumerate(
        ((own0, other0), (own1, other1), (own2, other2), (own3, other3))
    ):
        sources += [(k, own, core), (k, other, 1 - core)]

    def copy(index, source, target):
        return pltpu.make_async_copy(source, target, sems.at[index])

    copy(4, grad_in, grad).start()
    copy(5, moved_in, moved).start()
    for k, source, at_core in sources:

        @pl.loop(0, 4)
        def _(l):
            row = pl.multiple_of(rows_of(place, k, l) + at_core * 16, 16)
            piece = source[l]
            kernel_t[pl.ds(row, 16), :] = piece
            wide = piece.astype(F32)
            total = jnp.zeros((16, 256), F32)
            for t in range(9):
                part = wide[:, t * 256 : (t + 1) * 256]
                total = total + part * part
            energy_t[pl.ds(row, 16), :] = total

    row_style = style[...]
    square_row = row_style * row_style
    energy = jnp.dot(square_row, energy_t[...], precision=HIGH, preferred_element_type=F32)
    factor = lax.rsqrt(energy + epsilon)
    demod[...] = jnp.transpose(jnp.broadcast_to(factor[:1], (128, 256)))
    copy(0, demod, demod_out).start()
    copy(6, kernel_t, kernel_out).start()

    copy(4, grad_in, grad).wait()
    inner[...] = jnp.zeros((16, 256), F32)

    @pl.loop(0, 32)
    def _(step):
        row = pl.multiple_of(step * 16, 16)
        dots = jnp.zeros((16, 256), F32)
        for t in range(9):
            lanes = slice(t * 256, (t + 1) * 256)
            dots = dots + kernel_t[pl.ds(row, 16), lanes].astype(F32) * grad[pl.ds(row, 16), lanes]
        inner[...] += dots

    norm = jnp.sum(inner[...], axis=0, keepdims=True)
    slope = -0.5 * norm * (factor * factor * factor)
    style_col = jnp.transpose(jnp.broadcast_to(row_style[:1], (128, 512)))
    style_sum = jnp.sum(energy_t[...] * slope[:1], axis=1, keepdims=True)
    back[:, 1024:1152] = (2.0 * style_col * style_sum).astype(BF16)
    for j in range(2):
        lanes = slice(j * 128, (j + 1) * 128)
        energy_t[:, lanes] = 2.0 * (style_col * style_col) * slope[:1, lanes]

    @pl.loop(0, 16)
    def _(step):
        k, l = step // 4, step % 4
        for target, at_core in ((keep, core), (send, 1 - core)):
            row = pl.multiple_of(rows_of(place, k, l) + at_core * 16, 16)
            radial = energy_t[pl.ds(row, 16), :]
            for t in range(9):
                lanes = slice(t * 256, (t + 1) * 256)
                part = kernel_t[pl.ds(row, 16), lanes].astype(F32)
                term = grad[pl.ds(row, 16), lanes] * factor[:1] + part * radial
                target[k, l, :, lanes] = term.astype(target.dtype)
                scaled_t[pl.ds(row, 16), lanes] = (part * factor[:1]).astype(BF16)

    copy(1, send, send_out).start()
    copy(2, keep, keep_out).start()
    copy(5, moved_in, moved).wait()
    side = slice(1024, 1152)
    copy(3, back.at[:, side], back_out.at[:, side]).start()

    def back_copy(step):
        lanes = pl.ds(pl.multiple_of(step * 256, 256), 256)
        return copy(7 + step, back.at[:, lanes], back_out.at[:, lanes])

    @pl.loop(0, 4)
    def _(step):
        lanes = pl.ds(pl.multiple_of(step * 256, 256), 256)
        back[:, lanes] = jnp.dot(
            scaled_t[...], moved[:, lanes], preferred_element_type=F32
        ).astype(BF16)
        back_copy(step).start()

    copy(0, demod, demod_out).wait()
    copy(1, send, send_out).wait()
    copy(2, keep, keep_out).wait()
    copy(3, back.at[:, side], back_out.at[:, side]).wait()
    copy(6, kernel_t, kernel_out).wait()

    @pl.loop(0, 4)
    def _(step):
        back_copy(step).wait()


def forward_body(place, whole, kernel_in, demod_in, out, products, kernel_t, images, demod, sems):
    copies = [
        pltpu.make_async_copy(source, target, sems.at[index])
        for index, (source, target) in enumerate(
            ((kernel_in, kernel_t), (whole, images), (demod_in, demod))
        )
    ]
    for copy in copies:
        copy.start()
    for copy in copies:
        copy.wait()

    @pl.loop(0, 4)
    def _(step):
        lanes = pl.ds(pl.multiple_of(step * 256, 256), 256)
        products[:, lanes] = lax.dot_general(
            kernel_t[...], images[:, lanes], (((0,), (0,)), ((), ())), preferred_element_type=F32
        )

    @pl.loop(0, 8)
    def _(step):
        k, half = step // 2, step % 2
        row = pl.multiple_of(((place[3] + k) % 4) * 64 + half * 32, 32)
        total = products[pl.ds(4 * 256 + row, 32), :]
        for t, (a, c) in enumerate(tap_steps):
            if t != 4:
                total = total + shifted(products[pl.ds(t * 256 + row, 32), :], a, c)
        factor = demod[pl.ds(row, 32), :]
        for j in range(8):
            lanes = slice(j * 128, (j + 1) * 128)
            place_at = pl.ds(pl.multiple_of(half * 32, 32), 32)
            out[k, place_at, lanes] = (factor * total[:, lanes]).astype(BF16)


def pair_body(keep, received, *outs):
    for k, out in enumerate(outs):

        @pl.loop(0, 4)
        def _(l):
            out[l] = (keep[k, l] + received[k, l].astype(F32)).astype(BF16)


def quarter_body(place, part0, part1, part2, part3, out0, out1, out2, out3, sums):
    @pl.loop(0, 4)
    def _(l):
        total = part0[l].astype(F32)
        for part in (part1, part2, part3):
            total = total + part[l].astype(F32)
        sums[...] = total
        for k, out in enumerate((out0, out1, out2, out3)):
            pair = ((place[3] + k) % 4) // 2
            for t in range(9):
                start = pl.multiple_of(t * 256 + pair * 128, 128)
                out[l, t * 16 : (t + 1) * 16, :] = sums[:, pl.ds(start, 128)].astype(BF16)


def output_body(place, part0, part1, part2, part3, out, sems):
    copies = []
    for k, part in enumerate((part0, part1, part2, part3)):
        slot = (place[3] + 4 - k) % 4
        copies.append(pltpu.make_async_copy(part, out.at[slot], sems.at[k]))
    for copy in copies:
        copy.start()
    for copy in copies:
        copy.wait()


PRODUCT = 2 * 512 * 2304 * 1024
VM = pltpu.VMEM
HB = pltpu.HBM


def run(body, name, outs, out_space, scratch, mib, flops, *args, far=()):
    def space(index, arg):
        if arg.dtype == jnp.int32:
            return pltpu.SMEM
        return HB if index in far else VM

    return pl.pallas_call(
        body,
        out_shape=tuple(jax.ShapeDtypeStruct(*one) for one in outs),
        in_specs=[pl.BlockSpec(memory_space=space(*one)) for one in enumerate(args)],
        out_specs=tuple(pl.BlockSpec(memory_space=out_space) for _ in outs),
        scratch_shapes=scratch,
        compiler_params=pltpu.CompilerParams(vmem_limit_bytes=mib * MIB),
        cost_estimate=pl.CostEstimate(flops=flops, bytes_accessed=MIB, transcendentals=256),
        name=name,
    )(*args)


def ring_take(parts, start):
    return lax.dynamic_slice_in_dim(jnp.concatenate([parts, parts]), start, 4, 0)


def on_device(images, styles, weight, cotangent):
    seat = lax.axis_index("cout")
    spot = lax.axis_index("dp")
    column = seat % 4
    place = jnp.stack([spot // 8, (spot // 2) % 4, spot % 2, column]).astype(jnp.int32)
    local_styles = lax.dynamic_slice_in_dim(styles, seat * 64, 64, 1)
    style = jnp.broadcast_to(lax.dynamic_slice_in_dim(styles, column, 1, 0), (8, 512))

    packed = jnp.transpose(weight, (2, 0, 1)).reshape(9, 1024)
    stages = [packed] + [moved_by(packed, "l", -k) for k in (1, 2, 3)]
    rows = jnp.pad(jnp.concatenate(stages), ((0, 4), (0, 0)))
    modulated = (images.astype(F32) * local_styles[:, :, None]).astype(BF16)
    rows, twice = lax.optimization_barrier((rows, jnp.concatenate([modulated, modulated])))
    whole = exchange(twice, "hx").reshape(512, 1024)

    turned = [lax.dynamic_index_in_dim(cotangent, (column + k) % 4, 0, False) for k in range(4)]
    cots = [turned[0]] + [
        moved_by(jnp.concatenate([turned[k], rows]), "x", k) for k in (1, 2, 3)
    ]
    taps = jnp.stack([rows[:36]] + [cots[k][64:100] for k in (3, 2, 1)])
    taps = ring_take(taps, (4 - column) % 4)
    near = taps.reshape(4, 4, 16, 9, 64).transpose(1, 2, 3, 0, 4).reshape(4, 16, 2304)
    own = [near] + [moved_by(near, "y", -k) for k in (1, 2, 3)]
    kernels = own + [moved_by(one, "c", 1) for one in own]

    moved, grad = run(
        image_grad_body,
        "image_grad",
        [((2304, 1024), BF16), ((512, 2304), F32)],
        HB,
        [
            VM((2304, 1024), BF16),
            VM((512, 2304), F32),
            VM((512, 1024), BF16),
            pltpu.SemaphoreType.DMA((11,)),
        ],
        16,
        12 * PRODUCT,
        place,
        *cots,
        whole,
        far=(5,),
    )
    blocks = (4, 4, 16, 2304)
    demod, send, keep, back, kernel_t = run(
        gradient_body,
        "gradient",
        [
            ((256, 128), F32),
            (blocks, BF16),
            (blocks, F32),
            ((512, 1152), BF16),
            ((512, 2304), BF16),
        ],
        HB,
        [
            VM((2304, 1024), BF16),
            VM((512, 2304), F32),
            VM((512, 2304), BF16),
            VM((512, 2304), BF16),
            VM((512, 256), F32),
            VM((16, 256), F32),
            VM((256, 128), F32),
            VM(blocks, BF16),
            VM(blocks, F32),
            VM((512, 1152), BF16),
            pltpu.SemaphoreType.DMA((11,)),
        ],
        30,
        2 * PRODUCT,
        place,
        style,
        moved,
        grad,
        *kernels,
        far=(2, 3),
    )
    received = moved_by(send, "c", 1)
    (out,) = run(
        forward_body,
        "forward",
        [((4, 64, 1024), BF16)],
        VM,
        [
            VM((2304, 1024), F32),
            VM((512, 2304), BF16),
            VM((512, 1024), BF16),
            VM((256, 128), F32),
            pltpu.SemaphoreType.DMA((3,)),
        ],
        18,
        PRODUCT,
        place,
        whole,
        kernel_t,
        demod,
        far=(1, 2, 3),
    )
    outs = [out[0]] + [moved_by(out[k], "x", k) for k in (1, 2, 3)]
    (output,) = run(
        output_body, "output", [((4, 64, 1024), BF16)], HB, [pltpu.SemaphoreType.DMA((4,))],
        4, 10**6, place, *outs,
    )

    halves = run(
        pair_body, "pair_sum", [((4, 16, 2304), BF16)] * 4, VM, [], 8, 10**7, keep, received
    )
    halves, back = lax.optimization_barrier((halves, back))
    back_parts = exchange(back.reshape(8, 64, 1152), "hx").reshape(2, 4, 64, 1152)
    quarters = [halves[0]] + [moved_by(halves[k], "y", k) for k in (1, 2, 3)]
    pieces = run(
        quarter_body, "quarter_sum", [((4, 144, 128), BF16)] * 4, VM, [VM((16, 2304), F32)],
        6, 10**7, place, *quarters,
    )
    total = pieces[0].astype(F32)
    for k in (1, 2, 3):
        total = total + moved_by(pieces[k], "x", k).astype(F32)
    pieces = total.astype(BF16)
    total = pieces[0].astype(F32)
    for k in (1, 2, 3):
        total = total + moved_by(pieces[k], "l", k).astype(F32)
    total = lax.dynamic_slice_in_dim(total * (1.0 / 128), (column % 2) * 64, 64, 1)
    weight_grad = total.reshape(9, 16, 64).transpose(0, 2, 1)

    back_sum = back_parts[0].astype(F32) + back_parts[1].astype(F32)
    input_grad = (back_sum[:, :, :1024] * local_styles[:, :, None]).astype(BF16)
    style_grad = jnp.sum(back_sum[:, :, :1024] * images.astype(F32), axis=2) + back_sum[:, :, 1024]
    return (output, input_grad, style_grad, weight_grad)


def solution(mesh):
    return jax.shard_map(
        on_device,
        mesh=mesh,
        in_specs=(
            P("dp", "cout", None),
            P("dp", None),
            P(None, "cout", "dp"),
            P("dp", "cout", None),
        ),
        out_specs=(
            P("dp", "cout", None),
            P("dp", "cout", None),
            P("dp", "cout"),
            P(None, "cout", "dp"),
        ),
        check_vma=False,
    )
```

time: 194 us -> 136 us (0.70)
  the two profiles are of different devices: /device:TPU:32 before, /device:TPU:8 now
where the time goes in v2:
time: 136 us; the launch traced here: 135 us
  starting transfers between devices  52.8 us (39%)
  waiting for transfers between devices  43.6 us (32%)
  Pallas kernels  27.1 us (20%)
  other arithmetic  6.33 us (5%)
  local copies, waits for them, and re-layouts  4.53 us (3%)
    ppermute x26, waiting for transfers between devices, moved_by(): return lax.ppermute(value, BOTH, pairs)  43.6 us
    ppermute x26, starting transfers between devices, moved_by(): return lax.ppermute(value, BOTH, pairs)  35.7 us
    pallas_call x6, Pallas kernels, run(): pl.pallas_call(body, out_shape=tuple((jax.ShapeDtypeStruct(*one) for one...  27.1 us
    all_to_all x2, starting transfers between devices, exchange(): lax.all_to_all(blocks, BOTH, 0, 0, axis_index_groups=groups, tiled=True)  17.1 us
  transfers between devices with their start and end apart: 28, of which 13 were waited for; matrix products, arithmetic and copies ran while one was open for 4% of the time, Pallas kernels for 13%

profile of v2, /device:TPU:8, one launch (start us, length us, event | category | flops | bytes accessed | tf_op | source)
XLA Modules:
  0.0 135.4 jit_solution(18282657455196062507)
XLA Ops:
  1.5 2.0 %collective-permute-start.2 = (bf16[9,1024]{1,0:T(8,128)(2,1)S(1)}, bf16[9,1024]{1,0:T(8,128)(2,1)S(1)}, u32[]{:S(2)}, u32[]{:S(2)}) collective-permute-start(bf16[9,1024]{1,0:T(8,128)(2,1)S(1)} %reshape.34), channel_id=1, source_target_pairs={{0,64},{1,65},{2,66},{3,67},{4,68},{5,69},{6,70},{7,71},{8,72},{9,... | collective-permute-start | bytes 55304 | tf_op jit(solution)/shard_map/ppermute | solution.py:40
  3.5 3.3 %collective-permute-start.1 = (bf16[9,1024]{1,0:T(8,128)(2,1)S(1)}, bf16[9,1024]{1,0:T(8,128)(2,1)S(1)}, u32[]{:S(2)}, u32[]{:S(2)}) collective-permute-start(bf16[9,1024]{1,0:T(8,128)(2,1)S(1)} %reshape.34), channel_id=1, source_target_pairs={{0,128},{1,129},{2,130},{3,131},{4,132},{5,133},{6,134},{7,135},{8... | collective-permute-start | bytes 55304 | tf_op jit(solution)/shard_map/ppermute | solution.py:40
  10.8 8.7 %all-to-all-start = ((bf16[8,64,1024]{2,1,0:T(8,128)(2,1)}), bf16[8,64,1024]{2,1,0:T(8,128)(2,1)S(1)}, u32[]{:S(2)}, u32[]{:S(2)}) async-start(bf16[8,64,1024]{2,1,0:T(8,128)(2,1)} %pad_maximum_fusion), calls=%async_computation | async-start | bytes 2097152 | tf_op jit(solution)/shard_map/all_to_all | solution.py:32
  19.6 3.3 %collective-permute-start.5 = (bf16[104,1024]{1,0:T(8,128)(2,1)S(1)}, bf16[104,1024]{1,0:T(8,128)(2,1)S(1)}, u32[]{:S(2)}, u32[]{:S(2)}) collective-permute-start(bf16[104,1024]{1,0:T(8,128)(2,1)S(1)} %get-tuple-element.70), channel_id=1, source_target_pairs={{0,3},{1,0},{2,1},{3,2},{4,7},{5,4},{6,5},{7,6},{8,11},{9,8},{10,9... | collective-permute-start | bytes 638984 | tf_op jit(solution)/shard_map/ppermute | solution.py:40
  24.6 14.5 %collective-permute-done.5.cot3 = bf16[104,1024]{1,0:T(8,128)(2,1)S(1)} collective-permute-done((bf16[104,1024]{1,0:T(8,128)(2,1)S(1)}, bf16[104,1024]{1,0:T(8,128)(2,1)S(1)}, u32[]{:S(2)}, u32[]{:S(2)}) %collective-permute-start.5) | collective-permute-done | bytes 213024 | tf_op jit(solution)/shard_map/ppermute | solution.py:40
  40.6 1.9 %collective-permute-done.3.cot1 = bf16[104,1024]{1,0:T(8,128)(2,1)S(1)} collective-permute-done((bf16[104,1024]{1,0:T(8,128)(2,1)S(1)}, bf16[104,1024]{1,0:T(8,128)(2,1)S(1)}, u32[]{:S(2)}, u32[]{:S(2)}) %collective-permute-start.3) | collective-permute-done | bytes 213024 | tf_op jit(solution)/shard_map/ppermute | solution.py:40
  46.9 2.4 %collective-permute-start.6 = (bf16[4,16,2304]{2,1,0:T(8,128)(2,1)S(1)}, bf16[4,16,2304]{2,1,0:T(8,128)(2,1)S(1)}, u32[]{:S(2)}, u32[]{:S(2)}) collective-permute-start(bf16[4,16,2304]{2,1,0:T(8,128)(2,1)S(1)} %reshape.37.own0), channel_id=1, source_target_pairs={{0,48},{1,49},{2,50},{3,51},{4,52},{5,53},{6,54},{7,55},{8,56},{9,... | collective-permute-start | bytes 884744 | tf_op jit(solution)/shard_map/ppermute | solution.py:40
  49.5 4.9 %collective-permute-done.8.own3 = bf16[4,16,2304]{2,1,0:T(8,128)(2,1)S(1)} collective-permute-done((bf16[4,16,2304]{2,1,0:T(8,128)(2,1)S(1)}, bf16[4,16,2304]{2,1,0:T(8,128)(2,1)S(1)}, u32[]{:S(2)}, u32[]{:S(2)}) %collective-permute-start.8) | collective-permute-done | bytes 294944 | tf_op jit(solution)/shard_map/ppermute | solution.py:40
  54.3 3.1 %collective-permute-done.7.own2 = bf16[4,16,2304]{2,1,0:T(8,128)(2,1)S(1)} collective-permute-done((bf16[4,16,2304]{2,1,0:T(8,128)(2,1)S(1)}, bf16[4,16,2304]{2,1,0:T(8,128)(2,1)S(1)}, u32[]{:S(2)}, u32[]{:S(2)}) %collective-permute-start.7) | collective-permute-done | bytes 294944 | tf_op jit(solution)/shard_map/ppermute | solution.py:40
  57.4 3.5 %collective-permute-done.6.own1 = bf16[4,16,2304]{2,1,0:T(8,128)(2,1)S(1)} collective-permute-done((bf16[4,16,2304]{2,1,0:T(8,128)(2,1)S(1)}, bf16[4,16,2304]{2,1,0:T(8,128)(2,1)S(1)}, u32[]{:S(2)}, u32[]{:S(2)}) %collective-permute-start.6) | collective-permute-done | bytes 294944 | tf_op jit(solution)/shard_map/ppermute | solution.py:40
  60.9 7.5 %image_grad.1 = (bf16[2304,1024]{1,0:T(8,128)(2,1)S(1)}, f32[512,2304]{1,0:T(8,128)S(1)}) custom-call(s32[4]{0:T(128)S(1)} %pad_add_fusion.place, bf16[64,1024]{1,0:T(8,128)(2,1)S(1)} %get-tuple-element.64.cot0, bf16[104,1024]{1,0:T(8,128)(2,1)S(1)} %collective-permute-done.3.cot1, bf16[104,1024]{1,0:T(8,128)(2,1)S(1)} %collective-permute-done.4.cot2, ...), custom_call_target="tpu_custom_call" | custom-call | flops 28991029248 | bytes 1048576 | tf_op jit(solution)/shard_map/image_grad/pallas_call | solution.py:279
  68.5 9.8 %gradient.1 = (f32[256,128]{1,0:T(8,128)S(1)}, bf16[4,4,16,2304]{3,2,1,0:T(8,128)(2,1)S(1)}, f32[4,4,16,2304]{3,2,1,0:T(8,128)S(1)}, bf16[512,1152]{1,0:T(8,128)(2,1)}, bf16[512,2304]{1,0:T(8,128)(2,1)S(1)}) custom-call(s32[4]{0:T(128)S(1)} %pad_add_fusion.place, f32[8,512]{1,0:T(8,128)S(1)} %broadcast_in_dim.10.style, ...), custom_call_target="tpu_custom_call" | custom-call | flops 4831838208 | bytes 1048576 | tf_op jit(solution)/shard_map/gradient/pallas_call | solution.py:279
  78.9 2.5 %collective-permute-done.16.received = bf16[4,4,16,2304]{3,2,1,0:T(8,128)(2,1)S(1)} collective-permute-done((bf16[4,4,16,2304]{3,2,1,0:T(8,128)(2,1)S(1)}, bf16[4,4,16,2304]{3,2,1,0:T(8,128)(2,1)S(1)}, u32[]{:S(2)}, u32[]{:S(2)}) %collective-permute-start.16) | collective-permute-done | bytes 1179680 | tf_op jit(solution)/shard_map/ppermute | solution.py:40
  81.7 8.3 %all-to-all-start.1 = ((bf16[8,64,1152]{2,1,0:T(8,128)(2,1)}), bf16[8,64,1152]{2,1,0:T(8,128)(2,1)}, u32[]{:S(2)}, u32[]{:S(2)}) async-start(bf16[8,64,1152]{2,1,0:T(8,128)(2,1)} %bitcast.20), calls=%async_computation.1 | async-start | bytes 2359296 | tf_op jit(solution)/shard_map/all_to_all | solution.py:32
  91.3 1.9 %collective-permute-start.18 = (bf16[4,16,2304]{2,1,0:T(8,128)(2,1)S(1)}, bf16[4,16,2304]{2,1,0:T(8,128)(2,1)S(1)}, u32[]{:S(2)}, u32[]{:S(2)}) collective-permute-start(bf16[4,16,2304]{2,1,0:T(8,128)(2,1)S(1)} %get-tuple-element.42), channel_id=1, source_target_pairs={{0,32},{1,33},{2,34},{3,35},{4,36},{5,37},{6,38},{7,39},{8,40},{9,... | collective-permute-start | bytes 884744 | tf_op jit(solution)/shard_map/ppermute | solution.py:40
  94.4 1.7 %copy-done.2 = bf16[512,2304]{1,0:T(8,128)(2,1)S(1)} copy-done((bf16[512,2304]{1,0:T(8,128)(2,1)S(1)}, bf16[512,2304]{1,0:T(8,128)(2,1)}, u32[]{:S(2)}) %copy-start.2) | copy-done | bytes 2359320
  96.1 7.3 %forward.1 = bf16[4,64,1024]{2,1,0:T(8,128)(2,1)S(1)} custom-call(s32[4]{0:T(128)S(1)} %pad_add_fusion.place, bf16[512,1024]{1,0:T(8,128)(2,1)S(1)} %bitcast.59, bf16[512,2304]{1,0:T(8,128)(2,1)S(1)} %copy-done.2, f32[256,128]{1,0:T(8,128)S(1)} %get-tuple-element.31.demod_in), custom_call_target="tpu_custom_call" | custom-call | flops 2415919104 | bytes 1048576 | tf_op jit(solution)/shard_map/forward/pallas_call | solution.py:279
  103.4 4.3 %collective-permute-done.19.part3 = bf16[4,16,2304]{2,1,0:T(8,128)(2,1)S(1)} collective-permute-done((bf16[4,16,2304]{2,1,0:T(8,128)(2,1)S(1)}, bf16[4,16,2304]{2,1,0:T(8,128)(2,1)S(1)}, u32[]{:S(2)}, u32[]{:S(2)}) %collective-permute-start.19) | collective-permute-done | bytes 294944 | tf_op jit(solution)/shard_map/ppermute | solution.py:40
  108.7 1.8 %collective-permute-start.20 = (bf16[4,144,128]{2,1,0:T(8,128)(2,1)S(1)}, bf16[4,144,128]{2,1,0:T(8,128)(2,1)S(1)}, u32[]{:S(2)}, u32[]{:S(2)}) collective-permute-start(bf16[4,144,128]{2,1,0:T(8,128)(2,1)S(1)} %get-tuple-element.45), channel_id=1, source_target_pairs={{0,1},{1,2},{2,3},{3,0},{4,5},{5,6},{6,7},{7,4},{8,9},{9,10},{10,1... | collective-permute-start | bytes 442376 | tf_op jit(solution)/shard_map/ppermute | solution.py:40
  110.5 2.7 %collective-permute-start.21 = (bf16[4,144,128]{2,1,0:T(8,128)(2,1)S(1)}, bf16[4,144,128]{2,1,0:T(8,128)(2,1)S(1)}, u32[]{:S(2)}, u32[]{:S(2)}) collective-permute-start(bf16[4,144,128]{2,1,0:T(8,128)(2,1)S(1)} %get-tuple-element.46), channel_id=1, source_target_pairs={{0,2},{1,3},{2,0},{3,1},{4,6},{5,7},{6,4},{7,5},{8,10},{9,11},{10,... | collective-permute-start | bytes 442376 | tf_op jit(solution)/shard_map/ppermute | solution.py:40
  114.8 2.6 %collective-permute-start.14 = (bf16[64,1024]{1,0:T(8,128)(2,1)S(1)}, bf16[64,1024]{1,0:T(8,128)(2,1)S(1)}, u32[]{:S(2)}, u32[]{:S(2)}) collective-permute-start(bf16[64,1024]{1,0:T(8,128)(2,1)S(1)} %get-tuple-element.59), channel_id=1, source_target_pairs={{0,2},{1,3},{2,0},{3,1},{4,6},{5,7},{6,4},{7,5},{8,10},{9,11},{10,... | collective-permute-start | bytes 393224 | tf_op jit(solution)/shard_map/ppermute | solution.py:40
  118.9 3.8 %collective-permute-done.21 = bf16[4,144,128]{2,1,0:T(8,128)(2,1)S(1)} collective-permute-done((bf16[4,144,128]{2,1,0:T(8,128)(2,1)S(1)}, bf16[4,144,128]{2,1,0:T(8,128)(2,1)S(1)}, u32[]{:S(2)}, u32[]{:S(2)}) %collective-permute-start.21) | collective-permute-done | bytes 147488 | tf_op jit(solution)/shard_map/ppermute | solution.py:40
  124.1 2.5 %collective-permute-start.25 = (bf16[144,128]{1,0:T(8,128)(2,1)S(1)}, bf16[144,128]{1,0:T(8,128)(2,1)S(1)}, u32[]{:S(2)}, u32[]{:S(2)}) collective-permute-start(bf16[144,128]{1,0:T(8,128)(2,1)S(1)} %get-tuple-element.67), channel_id=1, source_target_pairs={{0,192},{1,193},{2,194},{3,195},{4,196},{5,197},{6,198},{7,199},{8... | collective-permute-start | bytes 110600 | tf_op jit(solution)/shard_map/ppermute | solution.py:40
  128.8 2.7 %collective-permute-done.24 = bf16[144,128]{1,0:T(8,128)(2,1)S(1)} collective-permute-done((bf16[144,128]{1,0:T(8,128)(2,1)S(1)}, bf16[144,128]{1,0:T(8,128)(2,1)S(1)}, u32[]{:S(2)}, u32[]{:S(2)}) %collective-permute-start.24) | collective-permute-done | bytes 36896 | tf_op jit(solution)/shard_map/ppermute | solution.py:40
  (79 shorter events, 27.4 us)
Async XLA Ops:
  1.5 8.7 %collective-permute-start.2 = (bf16[9,1024]{1,0:T(8,128)(2,1)S(1)}, bf16[9,1024]{1,0:T(8,128)(2,1)S(1)}, u32[]{:S(2)}, u32[]{:S(2)}) collective-permute-start(bf16[9,1024]{1,0:T(8,128)(2,1)S(1)} %reshape.34), channel_id=1, source_target_pairs={{0,64},{1,65},{2,66},{3,67},{4,68},{5,69},{6,70},{7,71},{8,72},{9,... | collective-permute-start | bytes 55304 | tf_op jit(solution)/shard_map/ppermute | solution.py:40
  3.5 6.8 %collective-permute-start.1 = (bf16[9,1024]{1,0:T(8,128)(2,1)S(1)}, bf16[9,1024]{1,0:T(8,128)(2,1)S(1)}, u32[]{:S(2)}, u32[]{:S(2)}) collective-permute-start(bf16[9,1024]{1,0:T(8,128)(2,1)S(1)} %reshape.34), channel_id=1, source_target_pairs={{0,128},{1,129},{2,130},{3,131},{4,132},{5,133},{6,134},{7,135},{8... | collective-permute-start | bytes 55304 | tf_op jit(solution)/shard_map/ppermute | solution.py:40
  10.8 50.2 %all-to-all-start = ((bf16[8,64,1024]{2,1,0:T(8,128)(2,1)}), bf16[8,64,1024]{2,1,0:T(8,128)(2,1)S(1)}, u32[]{:S(2)}, u32[]{:S(2)}) async-start(bf16[8,64,1024]{2,1,0:T(8,128)(2,1)} %pad_maximum_fusion), calls=%async_computation | async-start | bytes 2097152 | tf_op jit(solution)/shard_map/all_to_all | solution.py:32
  19.6 19.5 %collective-permute-start.5 = (bf16[104,1024]{1,0:T(8,128)(2,1)S(1)}, bf16[104,1024]{1,0:T(8,128)(2,1)S(1)}, u32[]{:S(2)}, u32[]{:S(2)}) collective-permute-start(bf16[104,1024]{1,0:T(8,128)(2,1)S(1)} %get-tuple-element.70), channel_id=1, source_target_pairs={{0,3},{1,0},{2,1},{3,2},{4,7},{5,4},{6,5},{7,6},{8,11},{9,8},{10,9... | collective-permute-start | bytes 638984 | tf_op jit(solution)/shard_map/ppermute | solution.py:40
  22.9 17.8 %collective-permute-start.4 = (bf16[104,1024]{1,0:T(8,128)(2,1)S(1)}, bf16[104,1024]{1,0:T(8,128)(2,1)S(1)}, u32[]{:S(2)}, u32[]{:S(2)}) collective-permute-start(bf16[104,1024]{1,0:T(8,128)(2,1)S(1)} %get-tuple-element.71), channel_id=1, source_target_pairs={{0,2},{1,3},{2,0},{3,1},{4,6},{5,7},{6,4},{7,5},{8,10},{9,11},{10,... | collective-permute-start | bytes 638984 | tf_op jit(solution)/shard_map/ppermute | solution.py:40
  23.7 18.9 %collective-permute-start.3 = (bf16[104,1024]{1,0:T(8,128)(2,1)S(1)}, bf16[104,1024]{1,0:T(8,128)(2,1)S(1)}, u32[]{:S(2)}, u32[]{:S(2)}) collective-permute-start(bf16[104,1024]{1,0:T(8,128)(2,1)S(1)} %get-tuple-element.72), channel_id=1, source_target_pairs={{0,1},{1,2},{2,3},{3,0},{4,5},{5,6},{6,7},{7,4},{8,9},{9,10},{10,1... | collective-permute-start | bytes 638984 | tf_op jit(solution)/shard_map/ppermute | solution.py:40
  44.3 10.0 %collective-permute-start.8 = (bf16[4,16,2304]{2,1,0:T(8,128)(2,1)S(1)}, bf16[4,16,2304]{2,1,0:T(8,128)(2,1)S(1)}, u32[]{:S(2)}, u32[]{:S(2)}) collective-permute-start(bf16[4,16,2304]{2,1,0:T(8,128)(2,1)S(1)} %reshape.37.own0), channel_id=1, source_target_pairs={{0,16},{1,17},{2,18},{3,19},{4,20},{5,21},{6,22},{7,23},{8,24},{9,... | collective-permute-start | bytes 884744 | tf_op jit(solution)/shard_map/ppermute | solution.py:40
  46.0 11.4 %collective-permute-start.7 = (bf16[4,16,2304]{2,1,0:T(8,128)(2,1)S(1)}, bf16[4,16,2304]{2,1,0:T(8,128)(2,1)S(1)}, u32[]{:S(2)}, u32[]{:S(2)}) collective-permute-start(bf16[4,16,2304]{2,1,0:T(8,128)(2,1)S(1)} %reshape.37.own0), channel_id=1, source_target_pairs={{0,32},{1,33},{2,34},{3,35},{4,36},{5,37},{6,38},{7,39},{8,40},{9,... | collective-permute-start | bytes 884744 | tf_op jit(solution)/shard_map/ppermute | solution.py:40
  46.9 14.0 %collective-permute-start.6 = (bf16[4,16,2304]{2,1,0:T(8,128)(2,1)S(1)}, bf16[4,16,2304]{2,1,0:T(8,128)(2,1)S(1)}, u32[]{:S(2)}, u32[]{:S(2)}) collective-permute-start(bf16[4,16,2304]{2,1,0:T(8,128)(2,1)S(1)} %reshape.37.own0), channel_id=1, source_target_pairs={{0,48},{1,49},{2,50},{3,51},{4,52},{5,53},{6,54},{7,55},{8,56},{9,... | collective-permute-start | bytes 884744 | tf_op jit(solution)/shard_map/ppermute | solution.py:40
  49.4 19.1 %collective-permute-start.9 = (bf16[4,16,2304]{2,1,0:T(8,128)(2,1)S(1)}, bf16[4,16,2304]{2,1,0:T(8,128)(2,1)S(1)}, u32[]{:S(2)}, u32[]{:S(2)}) collective-permute-start(bf16[4,16,2304]{2,1,0:T(8,128)(2,1)S(1)} %reshape.37.own0), channel_id=1, source_target_pairs={{0,8},{1,9},{2,10},{3,11},{4,12},{5,13},{6,14},{7,15},{8,0},{9,1},... | collective-permute-start | bytes 884744 | tf_op jit(solution)/shard_map/ppermute | solution.py:40
  54.3 14.1 %collective-permute-start.12 = (bf16[4,16,2304]{2,1,0:T(8,128)(2,1)S(1)}, bf16[4,16,2304]{2,1,0:T(8,128)(2,1)}, u32[]{:S(2)}, u32[]{:S(2)}) collective-permute-start(bf16[4,16,2304]{2,1,0:T(8,128)(2,1)S(1)} %collective-permute-done.8.own3), channel_id=1, source_target_pairs={{0,8},{1,9},{2,10},{3,11},{4,12},{5,13},{6,14},{7,15},{8,0},{9,1},... | collective-permute-start | bytes 884744 | tf_op jit(solution)/shard_map/ppermute | solution.py:40
  57.4 11.1 %collective-permute-start.11 = (bf16[4,16,2304]{2,1,0:T(8,128)(2,1)S(1)}, bf16[4,16,2304]{2,1,0:T(8,128)(2,1)}, u32[]{:S(2)}, u32[]{:S(2)}) collective-permute-start(bf16[4,16,2304]{2,1,0:T(8,128)(2,1)S(1)} %collective-permute-done.7.own2), channel_id=1, source_target_pairs={{0,8},{1,9},{2,10},{3,11},{4,12},{5,13},{6,14},{7,15},{8,0},{9,1},... | collective-permute-start | bytes 884744 | tf_op jit(solution)/shard_map/ppermute | solution.py:40
  60.9 7.6 %collective-permute-start.10 = (bf16[4,16,2304]{2,1,0:T(8,128)(2,1)S(1)}, bf16[4,16,2304]{2,1,0:T(8,128)(2,1)}, u32[]{:S(2)}, u32[]{:S(2)}) collective-permute-start(bf16[4,16,2304]{2,1,0:T(8,128)(2,1)S(1)} %collective-permute-done.6.own1), channel_id=1, source_target_pairs={{0,8},{1,9},{2,10},{3,11},{4,12},{5,13},{6,14},{7,15},{8,0},{9,1},... | collective-permute-start | bytes 884744 | tf_op jit(solution)/shard_map/ppermute | solution.py:40
  81.7 50.5 %all-to-all-start.1 = ((bf16[8,64,1152]{2,1,0:T(8,128)(2,1)}), bf16[8,64,1152]{2,1,0:T(8,128)(2,1)}, u32[]{:S(2)}, u32[]{:S(2)}) async-start(bf16[8,64,1152]{2,1,0:T(8,128)(2,1)} %bitcast.20), calls=%async_computation.1 | async-start | bytes 2359296 | tf_op jit(solution)/shard_map/all_to_all | solution.py:32
  90.0 13.4 %collective-permute-start.17 = (bf16[4,16,2304]{2,1,0:T(8,128)(2,1)S(1)}, bf16[4,16,2304]{2,1,0:T(8,128)(2,1)S(1)}, u32[]{:S(2)}, u32[]{:S(2)}) collective-permute-start(bf16[4,16,2304]{2,1,0:T(8,128)(2,1)S(1)} %get-tuple-element.41), channel_id=1, source_target_pairs={{0,16},{1,17},{2,18},{3,19},{4,20},{5,21},{6,22},{7,23},{8,24},{9,... | collective-permute-start | bytes 884744 | tf_op jit(solution)/shard_map/ppermute | solution.py:40
  91.3 12.1 %collective-permute-start.18 = (bf16[4,16,2304]{2,1,0:T(8,128)(2,1)S(1)}, bf16[4,16,2304]{2,1,0:T(8,128)(2,1)S(1)}, u32[]{:S(2)}, u32[]{:S(2)}) collective-permute-start(bf16[4,16,2304]{2,1,0:T(8,128)(2,1)S(1)} %get-tuple-element.42), channel_id=1, source_target_pairs={{0,32},{1,33},{2,34},{3,35},{4,36},{5,37},{6,38},{7,39},{8,40},{9,... | collective-permute-start | bytes 884744 | tf_op jit(solution)/shard_map/ppermute | solution.py:40
  93.2 14.5 %collective-permute-start.19 = (bf16[4,16,2304]{2,1,0:T(8,128)(2,1)S(1)}, bf16[4,16,2304]{2,1,0:T(8,128)(2,1)S(1)}, u32[]{:S(2)}, u32[]{:S(2)}) collective-permute-start(bf16[4,16,2304]{2,1,0:T(8,128)(2,1)S(1)} %get-tuple-element.43), channel_id=1, source_target_pairs={{0,48},{1,49},{2,50},{3,51},{4,52},{5,53},{6,54},{7,55},{8,56},{9,... | collective-permute-start | bytes 884744 | tf_op jit(solution)/shard_map/ppermute | solution.py:40
  108.7 8.7 %collective-permute-start.20 = (bf16[4,144,128]{2,1,0:T(8,128)(2,1)S(1)}, bf16[4,144,128]{2,1,0:T(8,128)(2,1)S(1)}, u32[]{:S(2)}, u32[]{:S(2)}) collective-permute-start(bf16[4,144,128]{2,1,0:T(8,128)(2,1)S(1)} %get-tuple-element.45), channel_id=1, source_target_pairs={{0,1},{1,2},{2,3},{3,0},{4,5},{5,6},{6,7},{7,4},{8,9},{9,10},{10,1... | collective-permute-start | bytes 442376 | tf_op jit(solution)/shard_map/ppermute | solution.py:40
  110.5 12.1 %collective-permute-start.21 = (bf16[4,144,128]{2,1,0:T(8,128)(2,1)S(1)}, bf16[4,144,128]{2,1,0:T(8,128)(2,1)S(1)}, u32[]{:S(2)}, u32[]{:S(2)}) collective-permute-start(bf16[4,144,128]{2,1,0:T(8,128)(2,1)S(1)} %get-tuple-element.46), channel_id=1, source_target_pairs={{0,2},{1,3},{2,0},{3,1},{4,6},{5,7},{6,4},{7,5},{8,10},{9,11},{10,... | collective-permute-start | bytes 442376 | tf_op jit(solution)/shard_map/ppermute | solution.py:40
  113.2 9.4 %collective-permute-start.22 = (bf16[4,144,128]{2,1,0:T(8,128)(2,1)S(1)}, bf16[4,144,128]{2,1,0:T(8,128)(2,1)S(1)}, u32[]{:S(2)}, u32[]{:S(2)}) collective-permute-start(bf16[4,144,128]{2,1,0:T(8,128)(2,1)S(1)} %get-tuple-element.47), channel_id=1, source_target_pairs={{0,3},{1,0},{2,1},{3,2},{4,7},{5,4},{6,5},{7,6},{8,11},{9,8},{10,9... | collective-permute-start | bytes 442376 | tf_op jit(solution)/shard_map/ppermute | solution.py:40
  114.7 12.0 %collective-permute-start.15 = (bf16[64,1024]{1,0:T(8,128)(2,1)S(1)}, bf16[64,1024]{1,0:T(8,128)(2,1)S(1)}, u32[]{:S(2)}, u32[]{:S(2)}) collective-permute-start(bf16[64,1024]{1,0:T(8,128)(2,1)S(1)} %get-tuple-element.58), channel_id=1, source_target_pairs={{0,3},{1,0},{2,1},{3,2},{4,7},{5,4},{6,5},{7,6},{8,11},{9,8},{10,9... | collective-permute-start | bytes 393224 | tf_op jit(solution)/shard_map/ppermute | solution.py:40
  114.8 12.2 %collective-permute-start.14 = (bf16[64,1024]{1,0:T(8,128)(2,1)S(1)}, bf16[64,1024]{1,0:T(8,128)(2,1)S(1)}, u32[]{:S(2)}, u32[]{:S(2)}) collective-permute-start(bf16[64,1024]{1,0:T(8,128)(2,1)S(1)} %get-tuple-element.59), channel_id=1, source_target_pairs={{0,2},{1,3},{2,0},{3,1},{4,6},{5,7},{6,4},{7,5},{8,10},{9,11},{10,... | collective-permute-start | bytes 393224 | tf_op jit(solution)/shard_map/ppermute | solution.py:40
  117.4 9.9 %collective-permute-start.13 = (bf16[64,1024]{1,0:T(8,128)(2,1)S(1)}, bf16[64,1024]{1,0:T(8,128)(2,1)S(1)}, u32[]{:S(2)}, u32[]{:S(2)}) collective-permute-start(bf16[64,1024]{1,0:T(8,128)(2,1)S(1)} %get-tuple-element.60), channel_id=1, source_target_pairs={{0,1},{1,2},{2,3},{3,0},{4,5},{5,6},{6,7},{7,4},{8,9},{9,10},{10,1... | collective-permute-start | bytes 393224 | tf_op jit(solution)/shard_map/ppermute | solution.py:40
  122.7 5.9 %collective-permute-start.23 = (bf16[144,128]{1,0:T(8,128)(2,1)S(1)}, bf16[144,128]{1,0:T(8,128)(2,1)S(1)}, u32[]{:S(2)}, u32[]{:S(2)}) collective-permute-start(bf16[144,128]{1,0:T(8,128)(2,1)S(1)} %get-tuple-element.66), channel_id=1, source_target_pairs={{0,64},{1,65},{2,66},{3,67},{4,68},{5,69},{6,70},{7,71},{8,72},{9,... | collective-permute-start | bytes 110600 | tf_op jit(solution)/shard_map/ppermute | solution.py:40
  (9 other events, 32.7 us)

commit v3 on v2

--- a/solution.py
+++ b/solution.py
@@ -59,47 +59,16 @@
     return (((place[0] + l) % 4) * 4 + (place[1] + k) % 4) * 32
 
 
-def image_grad_body(
-    place, cot0, cot1, cot2, cot3, whole, moved_out, grad_out, moved, grad, images, sems
-):
-    bring = pltpu.make_async_copy(whole, images, sems.at[10])
-    bring.start()
-    for k, source in enumerate((cot0, cot1, cot2, cot3)):
-        block = ((place[3] + 4 - k) % 4) * 64
-
-        @pl.loop(0, 2)
-        def _(half):
-            value = source[pl.ds(pl.multiple_of(half * 32, 32), 32), :].astype(F32)
-            for t, (a, c) in enumerate(tap_steps):
-                row = pl.multiple_of(t * 256 + block + half * 32, 32)
-                moved[pl.ds(row, 32), :] = shifted(value, -a, -c).astype(BF16)
-
-    pltpu.make_async_copy(moved, moved_out, sems.at[9]).start()
-    bring.wait()
-
-    def leave(t):
-        lanes = pl.ds(pl.multiple_of(t * 256, 256), 256)
-        return pltpu.make_async_copy(grad.at[:, lanes], grad_out.at[:, lanes], sems.at[t])
-
-    @pl.loop(0, 9)
-    def _(t):
-        lanes = pl.ds(pl.multiple_of(t * 256, 256), 256)
-        grad[:, lanes] = lax.dot_general(
-            images[...], moved[lanes, :], (((1,), (1,)), ((), ())), preferred_element_type=F32
-        )
-        leave(t).start()
-
-    @pl.loop(0, 9)
-    def _(t):
-        leave(t).wait()
-
-    pltpu.make_async_copy(moved, moved_out, sems.at[9]).wait()
+def ready_body(place, whole, out):
+    del whole
+    for index in range(4):
+        out[index] = place[index]
 
 
 def gradient_body(
-    place, style, moved_in, grad_in, own0, own1, own2, own3, other0, other1, other2, other3,
+    place, style, cot0, cot1, cot2, cot3, whole, own0, own1, own2, own3, other0, other1, other2, other3,
     demod_out, send_out, keep_out, back_out, kernel_out,
-    moved, grad, kernel_t, scaled_t, energy_t, inner, demod, send, keep, back, sems,
+    moved, grad, images, kernel_t, scaled_t, energy_t, inner, demod, send, keep, back, sems,
 ):
     core = place[2]
     sources = []
@@ -111,8 +80,17 @@
     def copy(index, source, target):
         return pltpu.make_async_copy(source, target, sems.at[index])
 
-    copy(4, grad_in, grad).start()
-    copy(5, moved_in, moved).start()
+    copy(4, whole, images).start()
+    for k, source in enumerate((cot0, cot1, cot2, cot3)):
+        block = ((place[3] + 4 - k) % 4) * 64
+
+        @pl.loop(0, 2)
+        def _(half):
+            value = source[pl.ds(pl.multiple_of(half * 32, 32), 32), :].astype(F32)
+            for t, (a, c) in enumerate(tap_steps):
+                row = pl.multiple_of(t * 256 + block + half * 32, 32)
+                moved[pl.ds(row, 32), :] = shifted(value, -a, -c).astype(BF16)
+
     for k, source, at_core in sources:
 
         @pl.loop(0, 4)
@@ -128,14 +106,29 @@
             energy_t[pl.ds(row, 16), :] = total
 
     row_style = style[...]
-    square_row = row_style * row_style
-    energy = jnp.dot(square_row, energy_t[...], precision=HIGH, preferred_element_type=F32)
+    style_col = jnp.transpose(jnp.broadcast_to(row_style[:1], (128, 512)))
+    square = style_col * style_col
+    energy = jnp.concatenate(
+        [
+            jnp.sum(energy_t[:, j * 128 : (j + 1) * 128] * square, axis=0, keepdims=True)
+            for j in range(2)
+        ],
+        axis=1,
+    )
     factor = lax.rsqrt(energy + epsilon)
-    demod[...] = jnp.transpose(jnp.broadcast_to(factor[:1], (128, 256)))
+    demod[...] = jnp.transpose(jnp.broadcast_to(factor, (128, 256)))
     copy(0, demod, demod_out).start()
     copy(6, kernel_t, kernel_out).start()
 
-    copy(4, grad_in, grad).wait()
+    copy(4, whole, images).wait()
+
+    @pl.loop(0, 9)
+    def _(t):
+        lanes = pl.ds(pl.multiple_of(t * 256, 256), 256)
+        grad[:, lanes] = lax.dot_general(
+            images[...], moved[lanes, :], (((1,), (1,)), ((), ())), preferred_element_type=F32
+        )
+
     inner[...] = jnp.zeros((16, 256), F32)
 
     @pl.loop(0, 32)
@@ -144,40 +137,31 @@
         dots = jnp.zeros((16, 256), F32)
         for t in range(9):
             lanes = slice(t * 256, (t + 1) * 256)
-            dots = dots + kernel_t[pl.ds(row, 16), lanes].astype(F32) * grad[pl.ds(row, 16), lanes]
+            part = kernel_t[pl.ds(row, 16), lanes].astype(F32)
+            dots = dots + part * grad[pl.ds(row, 16), lanes]
+            scaled_t[pl.ds(row, 16), lanes] = (part * factor).astype(BF16)
         inner[...] += dots
 
     norm = jnp.sum(inner[...], axis=0, keepdims=True)
     slope = -0.5 * norm * (factor * factor * factor)
-    style_col = jnp.transpose(jnp.broadcast_to(row_style[:1], (128, 512)))
     style_sum = jnp.sum(energy_t[...] * slope[:1], axis=1, keepdims=True)
     back[:, 1024:1152] = (2.0 * style_col * style_sum).astype(BF16)
     for j in range(2):
         lanes = slice(j * 128, (j + 1) * 128)
-        energy_t[:, lanes] = 2.0 * (style_col * style_col) * slope[:1, lanes]
-
-    @pl.loop(0, 16)
-    def _(step):
-        k, l = step // 4, step % 4
-        for target, at_core in ((keep, core), (send, 1 - core)):
-            row = pl.multiple_of(rows_of(place, k, l) + at_core * 16, 16)
-            radial = energy_t[pl.ds(row, 16), :]
-            for t in range(9):
-                lanes = slice(t * 256, (t + 1) * 256)
-                part = kernel_t[pl.ds(row, 16), lanes].astype(F32)
-                term = grad[pl.ds(row, 16), lanes] * factor[:1] + part * radial
-                target[k, l, :, lanes] = term.astype(target.dtype)
-                scaled_t[pl.ds(row, 16), lanes] = (part * factor[:1]).astype(BF16)
-
-    copy(1, send, send_out).start()
-    copy(2, keep, keep_out).start()
-    copy(5, moved_in, moved).wait()
+        energy_t[:, lanes] = 2.0 * square * slope[:1, lanes]
+
     side = slice(1024, 1152)
     copy(3, back.at[:, side], back_out.at[:, side]).start()
 
     def back_copy(step):
         lanes = pl.ds(pl.multiple_of(step * 256, 256), 256)
         return copy(7 + step, back.at[:, lanes], back_out.at[:, lanes])
+
+    def terms_copy(step):
+        return copy(11 + step, send.at[step], send_out.at[step])
+
+    def keep_copy(step):
+        return copy(15 + step, keep.at[step], keep_out.at[step])
 
     @pl.loop(0, 4)
     def _(step):
@@ -185,17 +169,28 @@
         back[:, lanes] = jnp.dot(
             scaled_t[...], moved[:, lanes], preferred_element_type=F32
         ).astype(BF16)
+        for l in range(4):
+            for target, at_core in ((keep, core), (send, 1 - core)):
+                row = pl.multiple_of(rows_of(place, step, l) + at_core * 16, 16)
+                radial = energy_t[pl.ds(row, 16), :]
+                for t in range(9):
+                    taps = slice(t * 256, (t + 1) * 256)
+                    part = kernel_t[pl.ds(row, 16), taps].astype(F32)
+                    term = grad[pl.ds(row, 16), taps] * factor + part * radial
+                    target[step, l, :, taps] = term.astype(target.dtype)
         back_copy(step).start()
+        terms_copy(step).start()
+        keep_copy(step).start()
 
     copy(0, demod, demod_out).wait()
-    copy(1, send, send_out).wait()
-    copy(2, keep, keep_out).wait()
     copy(3, back.at[:, side], back_out.at[:, side]).wait()
     copy(6, kernel_t, kernel_out).wait()
 
     @pl.loop(0, 4)
     def _(step):
         back_copy(step).wait()
+        terms_copy(step).wait()
+        keep_copy(step).wait()
 
 
 def forward_body(place, whole, kernel_in, demod_in, out, products, kernel_t, images, demod, sems):
@@ -241,6 +236,8 @@
 
 
 def quarter_body(place, part0, part1, part2, part3, out0, out1, out2, out3, sums):
+    low = lax.broadcasted_iota(jnp.int32, (16, 128), 1) < 64
+
     @pl.loop(0, 4)
     def _(l):
         total = part0[l].astype(F32)
@@ -248,10 +245,23 @@
             total = total + part[l].astype(F32)
         sums[...] = total
         for k, out in enumerate((out0, out1, out2, out3)):
-            pair = ((place[3] + k) % 4) // 2
-            for t in range(9):
-                start = pl.multiple_of(t * 256 + pair * 128, 128)
-                out[l, t * 16 : (t + 1) * 16, :] = sums[:, pl.ds(start, 128)].astype(BF16)
+            column = (place[3] + k) % 4
+            even = column % 2 == 0
+
+            def block(t):
+                start = pl.multiple_of(t * 256 + (column // 2) * 128, 128)
+                value = sums[:, pl.ds(start, 128)]
+                return value, pltpu.roll(value, 64, 1)
+
+            for pair in range(5):
+                first, first_rolled = block(2 * pair)
+                left = jnp.where(even, first, first_rolled)
+                right = jnp.zeros((16, 128), F32)
+                if pair < 4:
+                    second, second_rolled = block(2 * pair + 1)
+                    right = jnp.where(even, second_rolled, second)
+                packed = jnp.where(low, left, right).astype(BF16)
+                out[l, pair * 16 : (pair + 1) * 16, :] = packed
 
 
 def output_body(place, part0, part1, part2, part3, out, sems):
@@ -307,33 +317,19 @@
     rows, twice = lax.optimization_barrier((rows, jnp.concatenate([modulated, modulated])))
     whole = exchange(twice, "hx").reshape(512, 1024)
 
-    turned = [lax.dynamic_index_in_dim(cotangent, (column + k) % 4, 0, False) for k in range(4)]
-    cots = [turned[0]] + [
-        moved_by(jnp.concatenate([turned[k], rows]), "x", k) for k in (1, 2, 3)
-    ]
-    taps = jnp.stack([rows[:36]] + [cots[k][64:100] for k in (3, 2, 1)])
+    sides = [rows] + [moved_by(rows, "x", k) for k in (1, 2, 3)]
+    taps = jnp.stack([sides[k][:36] for k in (0, 3, 2, 1)])
     taps = ring_take(taps, (4 - column) % 4)
     near = taps.reshape(4, 4, 16, 9, 64).transpose(1, 2, 3, 0, 4).reshape(4, 16, 2304)
+    turned = [lax.dynamic_index_in_dim(cotangent, (column + k) % 4, 0, False) for k in range(4)]
+    near, *turned = lax.optimization_barrier((near, *turned))
+    cots = [turned[0]] + [moved_by(turned[k], "x", k) for k in (1, 2, 3)]
     own = [near] + [moved_by(near, "y", -k) for k in (1, 2, 3)]
     kernels = own + [moved_by(one, "c", 1) for one in own]
 
-    moved, grad = run(
-        image_grad_body,
-        "image_grad",
-        [((2304, 1024), BF16), ((512, 2304), F32)],
-        HB,
-        [
-            VM((2304, 1024), BF16),
-            VM((512, 2304), F32),
-            VM((512, 1024), BF16),
-            pltpu.SemaphoreType.DMA((11,)),
-        ],
-        16,
-        12 * PRODUCT,
-        place,
-        *cots,
-        whole,
-        far=(5,),
+    (ready,) = run(
+        ready_body, "ready", [((4,), jnp.int32)], pltpu.SMEM, [], 1, 12 * PRODUCT, place, whole,
+        far=(1,),
     )
     blocks = (4, 4, 16, 2304)
     demod, send, keep, back, kernel_t = run(
@@ -350,6 +346,7 @@
         [
             VM((2304, 1024), BF16),
             VM((512, 2304), F32),
+            VM((512, 1024), BF16),
             VM((512, 2304), BF16),
             VM((512, 2304), BF16),
             VM((512, 256), F32),
@@ -358,16 +355,16 @@
             VM(blocks, BF16),
             VM(blocks, F32),
             VM((512, 1152), BF16),
-            pltpu.SemaphoreType.DMA((11,)),
+            pltpu.SemaphoreType.DMA((19,)),
         ],
-        30,
+        32,
         2 * PRODUCT,
-        place,
+        ready,
         style,
-        moved,
-        grad,
+        *cots,
+        whole,
         *kernels,
-        far=(2, 3),
+        far=(6,),
     )
     received = moved_by(send, "c", 1)
     (out,) = run(
@@ -383,42 +380,42 @@
             pltpu.SemaphoreType.DMA((3,)),
         ],
         18,
-        PRODUCT,
+        20 * PRODUCT,
         place,
         whole,
         kernel_t,
         demod,
         far=(1, 2, 3),
     )
+    halves = run(
+        pair_body, "pair_sum", [((4, 16, 2304), BF16)] * 4, VM, [], 8, 10**7, keep, received
+    )
+    halves, back = lax.optimization_barrier((halves, back))
+    back_parts = exchange(back.reshape(8, 64, 1152), "hx").reshape(2, 4, 64, 1152)
+    quarters = [halves[0]] + [moved_by(halves[k], "y", k) for k in (1, 2, 3)]
+    pieces = run(
+        quarter_body, "quarter_sum", [((4, 80, 128), BF16)] * 4, VM, [VM((16, 2304), F32)],
+        6, 10**7, place, *quarters,
+    )
+    total = pieces[0].astype(F32)
+    for k in (1, 2, 3):
+        total = total + moved_by(pieces[k], "x", k).astype(F32)
+    pieces = total.astype(BF16)
+    pieces, out = lax.optimization_barrier((pieces, out))
     outs = [out[0]] + [moved_by(out[k], "x", k) for k in (1, 2, 3)]
     (output,) = run(
         output_body, "output", [((4, 64, 1024), BF16)], HB, [pltpu.SemaphoreType.DMA((4,))],
         4, 10**6, place, *outs,
     )
 
-    halves = run(
-        pair_body, "pair_sum", [((4, 16, 2304), BF16)] * 4, VM, [], 8, 10**7, keep, received
-    )
-    halves, back = lax.optimization_barrier((halves, back))
-    back_parts = exchange(back.reshape(8, 64, 1152), "hx").reshape(2, 4, 64, 1152)
-    quarters = [halves[0]] + [moved_by(halves[k], "y", k) for k in (1, 2, 3)]
-    pieces = run(
-        quarter_body, "quarter_sum", [((4, 144, 128), BF16)] * 4, VM, [VM((16, 2304), F32)],
-        6, 10**7, place, *quarters,
-    )
-    total = pieces[0].astype(F32)
-    for k in (1, 2, 3):
-        total = total + moved_by(pieces[k], "x", k).astype(F32)
-    pieces = total.astype(BF16)
-    total = pieces[0].astype(F32)
-    for k in (1, 2, 3):
-        total = total + moved_by(pieces[k], "l", k).astype(F32)
-    total = lax.dynamic_slice_in_dim(total * (1.0 / 128), (column % 2) * 64, 64, 1)
-    weight_grad = total.reshape(9, 16, 64).transpose(0, 2, 1)
-
+    parts = [pieces[0]] + [moved_by(pieces[k], "l", k) for k in (1, 2, 3)]
     back_sum = back_parts[0].astype(F32) + back_parts[1].astype(F32)
     input_grad = (back_sum[:, :, :1024] * local_styles[:, :, None]).astype(BF16)
     style_grad = jnp.sum(back_sum[:, :, :1024] * images.astype(F32), axis=2) + back_sum[:, :, 1024]
+    input_grad, style_grad, *parts = lax.optimization_barrier((input_grad, style_grad, *parts))
+    total = sum((part.astype(F32) for part in parts[1:]), parts[0].astype(F32))
+    total = (total * (1.0 / 128)).reshape(5, 16, 2, 64)
+    weight_grad = total.transpose(0, 2, 3, 1).reshape(10, 64, 16)[:9]
     return (output, input_grad, style_grad, weight_grad)
 
 

time: 136 us -> 121 us (0.89)
  the two profiles are of different devices: /device:TPU:8 before, /device:TPU:32 now
where the time goes in v3:
time: 121 us; the launch traced here: 120 us
  starting transfers between devices  51.6 us (43%)
  waiting for transfers between devices  30.2 us (25%)
  Pallas kernels  25.9 us (21%)
  local copies, waits for them, and re-layouts  5.96 us (5%)
  other arithmetic  5.56 us (5%)
    ppermute x29, starting transfers between devices, moved_by(): return lax.ppermute(value, BOTH, pairs)  40.9 us
    pallas_call x6, Pallas kernels, run(): pl.pallas_call(body, out_shape=tuple((jax.ShapeDtypeStruct(*one) for one...  25.9 us
    ppermute x29, waiting for transfers between devices, moved_by(): return lax.ppermute(value, BOTH, pairs)  20.8 us
    all_to_all x2, starting transfers between devices, exchange(): lax.all_to_all(blocks, BOTH, 0, 0, axis_index_groups=groups, tiled=True)  10.7 us
    all_to_all x2, waiting for transfers between devices, exchange(): lax.all_to_all(blocks, BOTH, 0, 0, axis_index_groups=groups, tiled=True)  9.38 us
  transfers between devices with their start and end apart: 31, of which 9 were waited for; matrix products, arithmetic and copies ran while one was open for 7% of the time, Pallas kernels for 9%

profile of v3, /device:TPU:32, one launch (start us, length us, event | category | flops | bytes accessed | tf_op | source)
XLA Modules:
  0.0 120.3 jit_solution(15981733224225922093)
XLA Ops:
  1.5 2.0 %collective-permute-start.2 = (bf16[9,1024]{1,0:T(8,128)(2,1)S(1)}, bf16[9,1024]{1,0:T(8,128)(2,1)S(1)}, u32[]{:S(2)}, u32[]{:S(2)}) collective-permute-start(bf16[9,1024]{1,0:T(8,128)(2,1)S(1)} %reshape.35), channel_id=1, source_target_pairs={{0,64},{1,65},{2,66},{3,67},{4,68},{5,69},{6,70},{7,71},{8,72},{9,... | collective-permute-start | bytes 55304 | tf_op jit(solution)/shard_map/ppermute | solution.py:40
  3.5 2.3 %collective-permute-start.1 = (bf16[9,1024]{1,0:T(8,128)(2,1)S(1)}, bf16[9,1024]{1,0:T(8,128)(2,1)S(1)}, u32[]{:S(2)}, u32[]{:S(2)}) collective-permute-start(bf16[9,1024]{1,0:T(8,128)(2,1)S(1)} %reshape.35), channel_id=1, source_target_pairs={{0,128},{1,129},{2,130},{3,131},{4,132},{5,133},{6,134},{7,135},{8... | collective-permute-start | bytes 55304 | tf_op jit(solution)/shard_map/ppermute | solution.py:40
  11.7 2.7 %collective-permute-start.4 = (bf16[40,1024]{1,0:T(8,128)(2,1)S(1)}, bf16[40,1024]{1,0:T(8,128)(2,1)S(1)}, u32[]{:S(2)}, u32[]{:S(2)}) collective-permute-start(bf16[40,1024]{1,0:T(8,128)(2,1)S(1)} %fusion.8), channel_id=1, source_target_pairs={{0,2},{1,3},{2,0},{3,1},{4,6},{5,7},{6,4},{7,5},{8,10},{9,11},{10,... | collective-permute-start | bytes 245768 | tf_op jit(solution)/shard_map/ppermute | solution.py:40
  15.8 6.5 %all-to-all-start = ((bf16[8,64,1024]{2,1,0:T(8,128)(2,1)}), bf16[8,64,1024]{2,1,0:T(8,128)(2,1)S(1)}, u32[]{:S(2)}, u32[]{:S(2)}) async-start(bf16[8,64,1024]{2,1,0:T(8,128)(2,1)} %pad_maximum_fusion), calls=%async_computation | async-start | bytes 2097152 | tf_op jit(solution)/shard_map/all_to_all | solution.py:32
  24.1 1.7 %collective-permute-start.11 = (bf16[4,16,2304]{2,1,0:T(8,128)(2,1)S(1)}, bf16[4,16,2304]{2,1,0:T(8,128)(2,1)S(1)}, u32[]{:S(2)}, u32[]{:S(2)}) collective-permute-start(bf16[4,16,2304]{2,1,0:T(8,128)(2,1)S(1)} %reshape.38.own0), channel_id=1, source_target_pairs={{0,16},{1,17},{2,18},{3,19},{4,20},{5,21},{6,22},{7,23},{8,24},{9,... | collective-permute-start | bytes 884744 | tf_op jit(solution)/shard_map/ppermute | solution.py:40
  25.7 2.9 %collective-permute-start.10 = (bf16[4,16,2304]{2,1,0:T(8,128)(2,1)S(1)}, bf16[4,16,2304]{2,1,0:T(8,128)(2,1)S(1)}, u32[]{:S(2)}, u32[]{:S(2)}) collective-permute-start(bf16[4,16,2304]{2,1,0:T(8,128)(2,1)S(1)} %reshape.38.own0), channel_id=1, source_target_pairs={{0,32},{1,33},{2,34},{3,35},{4,36},{5,37},{6,38},{7,39},{8,40},{9,... | collective-permute-start | bytes 884744 | tf_op jit(solution)/shard_map/ppermute | solution.py:40
  30.0 2.0 %collective-permute-start.6 = (bf16[64,1024]{1,0:T(8,128)(2,1)S(1)}, bf16[64,1024]{1,0:T(8,128)(2,1)S(1)}, u32[]{:S(2)}, u32[]{:S(2)}) collective-permute-start(bf16[64,1024]{1,0:T(8,128)(2,1)S(1)} %get-tuple-element.40), channel_id=1, source_target_pairs={{0,1},{1,2},{2,3},{3,0},{4,5},{5,6},{6,7},{7,4},{8,9},{9,10},{10,1... | collective-permute-start | bytes 393224 | tf_op jit(solution)/shard_map/ppermute | solution.py:40
  32.0 2.7 %collective-permute-start.7 = (bf16[64,1024]{1,0:T(8,128)(2,1)S(1)}, bf16[64,1024]{1,0:T(8,128)(2,1)S(1)}, u32[]{:S(2)}, u32[]{:S(2)}) collective-permute-start(bf16[64,1024]{1,0:T(8,128)(2,1)S(1)} %get-tuple-element.41), channel_id=1, source_target_pairs={{0,2},{1,3},{2,0},{3,1},{4,6},{5,7},{6,4},{7,5},{8,10},{9,11},{10,... | collective-permute-start | bytes 393224 | tf_op jit(solution)/shard_map/ppermute | solution.py:40
  34.8 2.0 %collective-permute-done.6.cot1 = bf16[64,1024]{1,0:T(8,128)(2,1)S(1)} collective-permute-done((bf16[64,1024]{1,0:T(8,128)(2,1)S(1)}, bf16[64,1024]{1,0:T(8,128)(2,1)S(1)}, u32[]{:S(2)}, u32[]{:S(2)}) %collective-permute-start.6) | collective-permute-done | bytes 131104 | tf_op jit(solution)/shard_map/ppermute | solution.py:40
  36.8 2.3 %collective-permute-done.7.cot2 = bf16[64,1024]{1,0:T(8,128)(2,1)S(1)} collective-permute-done((bf16[64,1024]{1,0:T(8,128)(2,1)S(1)}, bf16[64,1024]{1,0:T(8,128)(2,1)S(1)}, u32[]{:S(2)}, u32[]{:S(2)}) %collective-permute-start.7) | collective-permute-done | bytes 131104 | tf_op jit(solution)/shard_map/ppermute | solution.py:40
  40.5 9.4 %all-to-all-done = bf16[8,64,1024]{2,1,0:T(8,128)(2,1)S(1)} async-done(((bf16[8,64,1024]{2,1,0:T(8,128)(2,1)}), bf16[8,64,1024]{2,1,0:T(8,128)(2,1)S(1)}, u32[]{:S(2)}, u32[]{:S(2)}) %all-to-all-start) | async-done | bytes 1048608 | tf_op jit(solution)/shard_map/all_to_all | solution.py:32
  51.1 14.7 %gradient.1 = (f32[256,128]{1,0:T(8,128)S(1)}, bf16[4,4,16,2304]{3,2,1,0:T(8,128)(2,1)S(1)}, f32[4,4,16,2304]{3,2,1,0:T(8,128)S(1)}, bf16[512,1152]{1,0:T(8,128)(2,1)}, bf16[512,2304]{1,0:T(8,128)(2,1)S(1)}) custom-call(s32[4]{0:T(128)S(1)} %ready.1.place, f32[8,512]{1,0:T(8,128)S(1)} %broadcast_in_dim.10.style, ...), custom_call_target="tpu_custom_call" | custom-call | flops 4831838208 | bytes 1048576 | tf_op jit(solution)/shard_map/gradient/pallas_call | solution.py:289
  65.9 2.8 %collective-permute-done.16.received = bf16[4,4,16,2304]{3,2,1,0:T(8,128)(2,1)S(1)} collective-permute-done((bf16[4,4,16,2304]{3,2,1,0:T(8,128)(2,1)S(1)}, bf16[4,4,16,2304]{3,2,1,0:T(8,128)(2,1)S(1)}, u32[]{:S(2)}, u32[]{:S(2)}) %collective-permute-start.16) | collective-permute-done | bytes 1179680 | tf_op jit(solution)/shard_map/ppermute | solution.py:40
  69.1 1.7 %collective-permute-start.17 = (bf16[4,16,2304]{2,1,0:T(8,128)(2,1)S(1)}, bf16[4,16,2304]{2,1,0:T(8,128)(2,1)S(1)}, u32[]{:S(2)}, u32[]{:S(2)}) collective-permute-start(bf16[4,16,2304]{2,1,0:T(8,128)(2,1)S(1)} %get-tuple-element.52), channel_id=1, source_target_pairs={{0,16},{1,17},{2,18},{3,19},{4,20},{5,21},{6,22},{7,23},{8,24},{9,... | collective-permute-start | bytes 884744 | tf_op jit(solution)/shard_map/ppermute | solution.py:40
  70.7 2.9 %collective-permute-start.18 = (bf16[4,16,2304]{2,1,0:T(8,128)(2,1)S(1)}, bf16[4,16,2304]{2,1,0:T(8,128)(2,1)S(1)}, u32[]{:S(2)}, u32[]{:S(2)}) collective-permute-start(bf16[4,16,2304]{2,1,0:T(8,128)(2,1)S(1)} %get-tuple-element.53), channel_id=1, source_target_pairs={{0,32},{1,33},{2,34},{3,35},{4,36},{5,37},{6,38},{7,39},{8,40},{9,... | collective-permute-start | bytes 884744 | tf_op jit(solution)/shard_map/ppermute | solution.py:40
  75.0 4.2 %all-to-all-start.1 = ((bf16[8,64,1152]{2,1,0:T(8,128)(2,1)}), bf16[8,64,1152]{2,1,0:T(8,128)(2,1)}, u32[]{:S(2)}, u32[]{:S(2)}) async-start(bf16[8,64,1152]{2,1,0:T(8,128)(2,1)} %bitcast.20), calls=%async_computation.1 | async-start | bytes 2359296 | tf_op jit(solution)/shard_map/all_to_all | solution.py:32
  79.5 7.5 %collective-permute-done.18.part2 = bf16[4,16,2304]{2,1,0:T(8,128)(2,1)S(1)} collective-permute-done((bf16[4,16,2304]{2,1,0:T(8,128)(2,1)S(1)}, bf16[4,16,2304]{2,1,0:T(8,128)(2,1)S(1)}, u32[]{:S(2)}, u32[]{:S(2)}) %collective-permute-start.18) | collective-permute-done | bytes 294944 | tf_op jit(solution)/shard_map/ppermute | solution.py:40
  89.0 2.7 %collective-permute-start.21 = (bf16[4,80,128]{2,1,0:T(8,128)(2,1)S(1)}, bf16[4,80,128]{2,1,0:T(8,128)(2,1)S(1)}, u32[]{:S(2)}, u32[]{:S(2)}) collective-permute-start(bf16[4,80,128]{2,1,0:T(8,128)(2,1)S(1)} %get-tuple-element.57), channel_id=1, source_target_pairs={{0,2},{1,3},{2,0},{3,1},{4,6},{5,7},{6,4},{7,5},{8,10},{9,11},{10,... | collective-permute-start | bytes 245768 | tf_op jit(solution)/shard_map/ppermute | solution.py:40
  93.3 1.7 %copy-done.2 = bf16[512,2304]{1,0:T(8,128)(2,1)S(1)} copy-done((bf16[512,2304]{1,0:T(8,128)(2,1)S(1)}, bf16[512,2304]{1,0:T(8,128)(2,1)}, u32[]{:S(2)}) %copy-start.2) | copy-done | bytes 2359320
  94.9 7.2 %forward.1 = bf16[4,64,1024]{2,1,0:T(8,128)(2,1)S(1)} custom-call(s32[4]{0:T(128)S(1)} %pad_add_fusion.place, bf16[512,1024]{1,0:T(8,128)(2,1)S(1)} %bitcast.58, bf16[512,2304]{1,0:T(8,128)(2,1)S(1)} %copy-done.2, f32[256,128]{1,0:T(8,128)S(1)} %copy-done.4), custom_call_target="tpu_custom_call" | custom-call | flops 48318382080 | bytes 1048576 | tf_op jit(solution)/shard_map/forward/pallas_call | solution.py:289
  102.4 2.5 %collective-permute-start.24 = (bf16[64,1024]{1,0:T(8,128)(2,1)S(1)}, bf16[64,1024]{1,0:T(8,128)(2,1)S(1)}, u32[]{:S(2)}, u32[]{:S(2)}) collective-permute-start(bf16[64,1024]{1,0:T(8,128)(2,1)S(1)} %get-tuple-element.81), channel_id=1, source_target_pairs={{0,2},{1,3},{2,0},{3,1},{4,6},{5,7},{6,4},{7,5},{8,10},{9,11},{10,... | collective-permute-start | bytes 393224 | tf_op jit(solution)/shard_map/ppermute | solution.py:40
  105.0 2.8 %collective-permute-start.27 = (bf16[80,128]{1,0:T(8,128)(2,1)S(1)}, bf16[80,128]{1,0:T(8,128)(2,1)S(1)}, u32[]{:S(2)}, u32[]{:S(2)}) collective-permute-start(bf16[80,128]{1,0:T(8,128)(2,1)S(1)} %get-tuple-element.89), channel_id=1, source_target_pairs={{0,128},{1,129},{2,130},{3,131},{4,132},{5,133},{6,134},{7,135},{8... | collective-permute-start | bytes 61448 | tf_op jit(solution)/shard_map/ppermute | solution.py:40
  110.0 2.4 %collective-permute-done.24.part2 = bf16[64,1024]{1,0:T(8,128)(2,1)S(1)} collective-permute-done((bf16[64,1024]{1,0:T(8,128)(2,1)S(1)}, bf16[64,1024]{1,0:T(8,128)(2,1)S(1)}, u32[]{:S(2)}, u32[]{:S(2)}) %collective-permute-start.24) | collective-permute-done | bytes 131104 | tf_op jit(solution)/shard_map/ppermute | solution.py:40
  112.3 2.7 %collective-permute-done.23.part1 = bf16[64,1024]{1,0:T(8,128)(2,1)S(1)} collective-permute-done((bf16[64,1024]{1,0:T(8,128)(2,1)S(1)}, bf16[64,1024]{1,0:T(8,128)(2,1)S(1)}, u32[]{:S(2)}, u32[]{:S(2)}) %collective-permute-start.23) | collective-permute-done | bytes 131104 | tf_op jit(solution)/shard_map/ppermute | solution.py:40
  (91 shorter events, 27.2 us)
Async XLA Ops:
  1.5 8.5 %collective-permute-start.2 = (bf16[9,1024]{1,0:T(8,128)(2,1)S(1)}, bf16[9,1024]{1,0:T(8,128)(2,1)S(1)}, u32[]{:S(2)}, u32[]{:S(2)}) collective-permute-start(bf16[9,1024]{1,0:T(8,128)(2,1)S(1)} %reshape.35), channel_id=1, source_target_pairs={{0,64},{1,65},{2,66},{3,67},{4,68},{5,69},{6,70},{7,71},{8,72},{9,... | collective-permute-start | bytes 55304 | tf_op jit(solution)/shard_map/ppermute | solution.py:40
  10.1 12.2 %collective-permute-start.5 = (bf16[40,1024]{1,0:T(8,128)(2,1)S(1)}, bf16[40,1024]{1,0:T(8,128)(2,1)S(1)}, u32[]{:S(2)}, u32[]{:S(2)}) collective-permute-start(bf16[40,1024]{1,0:T(8,128)(2,1)S(1)} %fusion.8), channel_id=1, source_target_pairs={{0,1},{1,2},{2,3},{3,0},{4,5},{5,6},{6,7},{7,4},{8,9},{9,10},{10,1... | collective-permute-start | bytes 245768 | tf_op jit(solution)/shard_map/ppermute | solution.py:40
  11.7 10.7 %collective-permute-start.4 = (bf16[40,1024]{1,0:T(8,128)(2,1)S(1)}, bf16[40,1024]{1,0:T(8,128)(2,1)S(1)}, u32[]{:S(2)}, u32[]{:S(2)}) collective-permute-start(bf16[40,1024]{1,0:T(8,128)(2,1)S(1)} %fusion.8), channel_id=1, source_target_pairs={{0,2},{1,3},{2,0},{3,1},{4,6},{5,7},{6,4},{7,5},{8,10},{9,11},{10,... | collective-permute-start | bytes 245768 | tf_op jit(solution)/shard_map/ppermute | solution.py:40
  15.8 34.0 %all-to-all-start = ((bf16[8,64,1024]{2,1,0:T(8,128)(2,1)}), bf16[8,64,1024]{2,1,0:T(8,128)(2,1)S(1)}, u32[]{:S(2)}, u32[]{:S(2)}) async-start(bf16[8,64,1024]{2,1,0:T(8,128)(2,1)} %pad_maximum_fusion), calls=%async_computation | async-start | bytes 2097152 | tf_op jit(solution)/shard_map/all_to_all | solution.py:32
  24.1 15.6 %collective-permute-start.11 = (bf16[4,16,2304]{2,1,0:T(8,128)(2,1)S(1)}, bf16[4,16,2304]{2,1,0:T(8,128)(2,1)S(1)}, u32[]{:S(2)}, u32[]{:S(2)}) collective-permute-start(bf16[4,16,2304]{2,1,0:T(8,128)(2,1)S(1)} %reshape.38.own0), channel_id=1, source_target_pairs={{0,16},{1,17},{2,18},{3,19},{4,20},{5,21},{6,22},{7,23},{8,24},{9,... | collective-permute-start | bytes 884744 | tf_op jit(solution)/shard_map/ppermute | solution.py:40
  25.7 14.0 %collective-permute-start.10 = (bf16[4,16,2304]{2,1,0:T(8,128)(2,1)S(1)}, bf16[4,16,2304]{2,1,0:T(8,128)(2,1)S(1)}, u32[]{:S(2)}, u32[]{:S(2)}) collective-permute-start(bf16[4,16,2304]{2,1,0:T(8,128)(2,1)S(1)} %reshape.38.own0), channel_id=1, source_target_pairs={{0,32},{1,33},{2,34},{3,35},{4,36},{5,37},{6,38},{7,39},{8,40},{9,... | collective-permute-start | bytes 884744 | tf_op jit(solution)/shard_map/ppermute | solution.py:40
  28.6 11.6 %collective-permute-start.9 = (bf16[4,16,2304]{2,1,0:T(8,128)(2,1)S(1)}, bf16[4,16,2304]{2,1,0:T(8,128)(2,1)S(1)}, u32[]{:S(2)}, u32[]{:S(2)}) collective-permute-start(bf16[4,16,2304]{2,1,0:T(8,128)(2,1)S(1)} %reshape.38.own0), channel_id=1, source_target_pairs={{0,48},{1,49},{2,50},{3,51},{4,52},{5,53},{6,54},{7,55},{8,56},{9,... | collective-permute-start | bytes 884744 | tf_op jit(solution)/shard_map/ppermute | solution.py:40
  36.8 14.3 %collective-permute-start.12 = (bf16[4,16,2304]{2,1,0:T(8,128)(2,1)S(1)}, bf16[4,16,2304]{2,1,0:T(8,128)(2,1)S(1)}, u32[]{:S(2)}, u32[]{:S(2)}) collective-permute-start(bf16[4,16,2304]{2,1,0:T(8,128)(2,1)S(1)} %reshape.38.own0), channel_id=1, source_target_pairs={{0,8},{1,9},{2,10},{3,11},{4,12},{5,13},{6,14},{7,15},{8,0},{9,1},... | collective-permute-start | bytes 884744 | tf_op jit(solution)/shard_map/ppermute | solution.py:40
  39.0 12.0 %collective-permute-start.8 = (bf16[64,1024]{1,0:T(8,128)(2,1)}, bf16[64,1024]{1,0:T(8,128)(2,1)}, u32[]{:S(2)}, u32[]{:S(2)}) collective-permute-start(bf16[64,1024]{1,0:T(8,128)(2,1)} %get-tuple-element.42), channel_id=1, source_target_pairs={{0,3},{1,0},{2,1},{3,2},{4,7},{5,4},{6,5},{7,6},{8,11},{9,8},{10,9... | collective-permute-start | bytes 393224 | tf_op jit(solution)/shard_map/ppermute | solution.py:40
  39.7 11.3 %collective-permute-start.15 = (bf16[4,16,2304]{2,1,0:T(8,128)(2,1)S(1)}, bf16[4,16,2304]{2,1,0:T(8,128)(2,1)S(1)}, u32[]{:S(2)}, u32[]{:S(2)}) collective-permute-start(bf16[4,16,2304]{2,1,0:T(8,128)(2,1)S(1)} %collective-permute-done.11.own3), channel_id=1, source_target_pairs={{0,8},{1,9},{2,10},{3,11},{4,12},{5,13},{6,14},{7,15},{8,0},{9,1},... | collective-permute-start | bytes 884744 | tf_op jit(solution)/shard_map/ppermute | solution.py:40
  39.7 11.3 %collective-permute-start.14 = (bf16[4,16,2304]{2,1,0:T(8,128)(2,1)S(1)}, bf16[4,16,2304]{2,1,0:T(8,128)(2,1)S(1)}, u32[]{:S(2)}, u32[]{:S(2)}) collective-permute-start(bf16[4,16,2304]{2,1,0:T(8,128)(2,1)S(1)} %collective-permute-done.10.own2), channel_id=1, source_target_pairs={{0,8},{1,9},{2,10},{3,11},{4,12},{5,13},{6,14},{7,15},{8,0},{9,1},... | collective-permute-start | bytes 884744 | tf_op jit(solution)/shard_map/ppermute | solution.py:40
  40.2 10.8 %collective-permute-start.13 = (bf16[4,16,2304]{2,1,0:T(8,128)(2,1)S(1)}, bf16[4,16,2304]{2,1,0:T(8,128)(2,1)}, u32[]{:S(2)}, u32[]{:S(2)}) collective-permute-start(bf16[4,16,2304]{2,1,0:T(8,128)(2,1)S(1)} %collective-permute-done.9.own1), channel_id=1, source_target_pairs={{0,8},{1,9},{2,10},{3,11},{4,12},{5,13},{6,14},{7,15},{8,0},{9,1},... | collective-permute-start | bytes 884744 | tf_op jit(solution)/shard_map/ppermute | solution.py:40
  69.1 10.4 %collective-permute-start.17 = (bf16[4,16,2304]{2,1,0:T(8,128)(2,1)S(1)}, bf16[4,16,2304]{2,1,0:T(8,128)(2,1)S(1)}, u32[]{:S(2)}, u32[]{:S(2)}) collective-permute-start(bf16[4,16,2304]{2,1,0:T(8,128)(2,1)S(1)} %get-tuple-element.52), channel_id=1, source_target_pairs={{0,16},{1,17},{2,18},{3,19},{4,20},{5,21},{6,22},{7,23},{8,24},{9,... | collective-permute-start | bytes 884744 | tf_op jit(solution)/shard_map/ppermute | solution.py:40
  70.7 16.2 %collective-permute-start.18 = (bf16[4,16,2304]{2,1,0:T(8,128)(2,1)S(1)}, bf16[4,16,2304]{2,1,0:T(8,128)(2,1)S(1)}, u32[]{:S(2)}, u32[]{:S(2)}) collective-permute-start(bf16[4,16,2304]{2,1,0:T(8,128)(2,1)S(1)} %get-tuple-element.53), channel_id=1, source_target_pairs={{0,32},{1,33},{2,34},{3,35},{4,36},{5,37},{6,38},{7,39},{8,40},{9,... | collective-permute-start | bytes 884744 | tf_op jit(solution)/shard_map/ppermute | solution.py:40
  73.6 13.3 %collective-permute-start.19 = (bf16[4,16,2304]{2,1,0:T(8,128)(2,1)S(1)}, bf16[4,16,2304]{2,1,0:T(8,128)(2,1)S(1)}, u32[]{:S(2)}, u32[]{:S(2)}) collective-permute-start(bf16[4,16,2304]{2,1,0:T(8,128)(2,1)S(1)} %get-tuple-element.54), channel_id=1, source_target_pairs={{0,48},{1,49},{2,50},{3,51},{4,52},{5,53},{6,54},{7,55},{8,56},{9,... | collective-permute-start | bytes 884744 | tf_op jit(solution)/shard_map/ppermute | solution.py:40
  75.0 41.4 %all-to-all-start.1 = ((bf16[8,64,1152]{2,1,0:T(8,128)(2,1)}), bf16[8,64,1152]{2,1,0:T(8,128)(2,1)}, u32[]{:S(2)}, u32[]{:S(2)}) async-start(bf16[8,64,1152]{2,1,0:T(8,128)(2,1)} %bitcast.20), calls=%async_computation.1 | async-start | bytes 2359296 | tf_op jit(solution)/shard_map/all_to_all | solution.py:32
  88.1 14.0 %collective-permute-start.20 = (bf16[4,80,128]{2,1,0:T(8,128)(2,1)S(1)}, bf16[4,80,128]{2,1,0:T(8,128)(2,1)S(1)}, u32[]{:S(2)}, u32[]{:S(2)}) collective-permute-start(bf16[4,80,128]{2,1,0:T(8,128)(2,1)S(1)} %get-tuple-element.56), channel_id=1, source_target_pairs={{0,1},{1,2},{2,3},{3,0},{4,5},{5,6},{6,7},{7,4},{8,9},{9,10},{10,1... | collective-permute-start | bytes 245768 | tf_op jit(solution)/shard_map/ppermute | solution.py:40
  89.0 13.1 %collective-permute-start.21 = (bf16[4,80,128]{2,1,0:T(8,128)(2,1)S(1)}, bf16[4,80,128]{2,1,0:T(8,128)(2,1)S(1)}, u32[]{:S(2)}, u32[]{:S(2)}) collective-permute-start(bf16[4,80,128]{2,1,0:T(8,128)(2,1)S(1)} %get-tuple-element.57), channel_id=1, source_target_pairs={{0,2},{1,3},{2,0},{3,1},{4,6},{5,7},{6,4},{7,5},{8,10},{9,11},{10,... | collective-permute-start | bytes 245768 | tf_op jit(solution)/shard_map/ppermute | solution.py:40
  91.7 10.5 %collective-permute-start.22 = (bf16[4,80,128]{2,1,0:T(8,128)(2,1)S(1)}, bf16[4,80,128]{2,1,0:T(8,128)(2,1)S(1)}, u32[]{:S(2)}, u32[]{:S(2)}) collective-permute-start(bf16[4,80,128]{2,1,0:T(8,128)(2,1)S(1)} %get-tuple-element.58), channel_id=1, source_target_pairs={{0,3},{1,0},{2,1},{3,2},{4,7},{5,4},{6,5},{7,6},{8,11},{9,8},{10,9... | collective-permute-start | bytes 245768 | tf_op jit(solution)/shard_map/ppermute | solution.py:40
  102.4 9.9 %collective-permute-start.24 = (bf16[64,1024]{1,0:T(8,128)(2,1)S(1)}, bf16[64,1024]{1,0:T(8,128)(2,1)S(1)}, u32[]{:S(2)}, u32[]{:S(2)}) collective-permute-start(bf16[64,1024]{1,0:T(8,128)(2,1)S(1)} %get-tuple-element.81), channel_id=1, source_target_pairs={{0,2},{1,3},{2,0},{3,1},{4,6},{5,7},{6,4},{7,5},{8,10},{9,11},{10,... | collective-permute-start | bytes 393224 | tf_op jit(solution)/shard_map/ppermute | solution.py:40
  104.9 10.1 %collective-permute-start.23 = (bf16[64,1024]{1,0:T(8,128)(2,1)S(1)}, bf16[64,1024]{1,0:T(8,128)(2,1)S(1)}, u32[]{:S(2)}, u32[]{:S(2)}) collective-permute-start(bf16[64,1024]{1,0:T(8,128)(2,1)S(1)} %get-tuple-element.82), channel_id=1, source_target_pairs={{0,1},{1,2},{2,3},{3,0},{4,5},{5,6},{6,7},{7,4},{8,9},{9,10},{10,1... | collective-permute-start | bytes 393224 | tf_op jit(solution)/shard_map/ppermute | solution.py:40
  104.9 14.6 %collective-permute-start.28 = (bf16[80,128]{1,0:T(8,128)(2,1)S(1)}, bf16[80,128]{1,0:T(8,128)(2,1)S(1)}, u32[]{:S(2)}, u32[]{:S(2)}) collective-permute-start(bf16[80,128]{1,0:T(8,128)(2,1)S(1)} %get-tuple-element.88), channel_id=1, source_target_pairs={{0,192},{1,193},{2,194},{3,195},{4,196},{5,197},{6,198},{7,199},{8... | collective-permute-start | bytes 61448 | tf_op jit(solution)/shard_map/ppermute | solution.py:40
  105.0 14.6 %collective-permute-start.27 = (bf16[80,128]{1,0:T(8,128)(2,1)S(1)}, bf16[80,128]{1,0:T(8,128)(2,1)S(1)}, u32[]{:S(2)}, u32[]{:S(2)}) collective-permute-start(bf16[80,128]{1,0:T(8,128)(2,1)S(1)} %get-tuple-element.89), channel_id=1, source_target_pairs={{0,128},{1,129},{2,130},{3,131},{4,132},{5,133},{6,134},{7,135},{8... | collective-permute-start | bytes 61448 | tf_op jit(solution)/shard_map/ppermute | solution.py:40
  108.8 10.8 %collective-permute-start.26 = (bf16[80,128]{1,0:T(8,128)(2,1)S(1)}, bf16[80,128]{1,0:T(8,128)(2,1)S(1)}, u32[]{:S(2)}, u32[]{:S(2)}) collective-permute-start(bf16[80,128]{1,0:T(8,128)(2,1)S(1)} %get-tuple-element.90), channel_id=1, source_target_pairs={{0,64},{1,65},{2,66},{3,67},{4,68},{5,69},{6,70},{7,71},{8,72},{9,... | collective-permute-start | bytes 61448 | tf_op jit(solution)/shard_map/ppermute | solution.py:40
  (14 other events, 74.2 us)

commit v4 on v3

--- a/solution.py
+++ b/solution.py
@@ -264,13 +264,29 @@
                 out[l, pair * 16 : (pair + 1) * 16, :] = packed
 
 
-def output_body(place, part0, part1, part2, part3, out, sems):
+def finish_body(
+    place, part0, part1, part2, part3, back, images, scale, out, input_grad, style_grad, sems
+):
     copies = []
     for k, part in enumerate((part0, part1, part2, part3)):
         slot = (place[3] + 4 - k) % 4
         copies.append(pltpu.make_async_copy(part, out.at[slot], sems.at[k]))
     for copy in copies:
         copy.start()
+    lane = lax.broadcasted_iota(jnp.int32, (64, 128), 1)
+    columns = jnp.zeros((64, 128), F32)
+    for b in range(4):
+        total = jnp.zeros((64, 128), F32)
+        for j in range(8):
+            lanes = slice(j * 128, (j + 1) * 128)
+            value = back[0, b, :, lanes].astype(F32) + back[1, b, :, lanes].astype(F32)
+            input_grad[b, :, lanes] = (value * scale[b]).astype(BF16)
+            total = total + value * images[b, :, lanes].astype(F32)
+        side = slice(1024, 1152)
+        side = back[0, b, :, side].astype(F32) + back[1, b, :, side].astype(F32)
+        column = jnp.sum(total, axis=1, keepdims=True) + side[:, :1]
+        columns = jnp.where(lane == b, column, columns)
+    style_grad[...] = jnp.transpose(columns)[:4]
     for copy in copies:
         copy.wait()
 
@@ -290,7 +306,10 @@
         body,
         out_shape=tuple(jax.ShapeDtypeStruct(*one) for one in outs),
         in_specs=[pl.BlockSpec(memory_space=space(*one)) for one in enumerate(args)],
-        out_specs=tuple(pl.BlockSpec(memory_space=out_space) for _ in outs),
+        out_specs=tuple(
+            pl.BlockSpec(memory_space=out_space[n] if isinstance(out_space, tuple) else out_space)
+            for n in range(len(outs))
+        ),
         scratch_shapes=scratch,
         compiler_params=pltpu.CompilerParams(vmem_limit_bytes=mib * MIB),
         cost_estimate=pl.CostEstimate(flops=flops, bytes_accessed=MIB, transcendentals=256),
@@ -313,6 +332,7 @@
     packed = jnp.transpose(weight, (2, 0, 1)).reshape(9, 1024)
     stages = [packed] + [moved_by(packed, "l", -k) for k in (1, 2, 3)]
     rows = jnp.pad(jnp.concatenate(stages), ((0, 4), (0, 0)))
+    scale = jnp.broadcast_to(local_styles[:, :, None], (4, 64, 128))
     modulated = (images.astype(F32) * local_styles[:, :, None]).astype(BF16)
     rows, twice = lax.optimization_barrier((rows, jnp.concatenate([modulated, modulated])))
     whole = exchange(twice, "hx").reshape(512, 1024)
@@ -403,15 +423,21 @@
     pieces = total.astype(BF16)
     pieces, out = lax.optimization_barrier((pieces, out))
     outs = [out[0]] + [moved_by(out[k], "x", k) for k in (1, 2, 3)]
-    (output,) = run(
-        output_body, "output", [((4, 64, 1024), BF16)], HB, [pltpu.SemaphoreType.DMA((4,))],
-        4, 10**6, place, *outs,
-    )
-
     parts = [pieces[0]] + [moved_by(pieces[k], "l", k) for k in (1, 2, 3)]
-    back_sum = back_parts[0].astype(F32) + back_parts[1].astype(F32)
-    input_grad = (back_sum[:, :, :1024] * local_styles[:, :, None]).astype(BF16)
-    style_grad = jnp.sum(back_sum[:, :, :1024] * images.astype(F32), axis=2) + back_sum[:, :, 1024]
+    output, input_grad, style_grad = run(
+        finish_body,
+        "finish",
+        [((4, 64, 1024), BF16), ((4, 64, 1024), BF16), ((4, 64), F32)],
+        (HB, VM, VM),
+        [pltpu.SemaphoreType.DMA((4,))],
+        8,
+        10**7,
+        place,
+        *outs,
+        back_parts,
+        images,
+        scale,
+    )
     input_grad, style_grad, *parts = lax.optimization_barrier((input_grad, style_grad, *parts))
     total = sum((part.astype(F32) for part in parts[1:]), parts[0].astype(F32))
     total = (total * (1.0 / 128)).reshape(5, 16, 2, 64)

time: 121 us -> 120 us (level)
  waiting for transfers between devices: 30.2 us -> 33.3 us
  other arithmetic: 5.56 us -> 2.55 us
  starting transfers between devices: 51.6 us -> 49.2 us
  Pallas kernels: 25.9 us -> 27.9 us
    ppermute x29, waiting for transfers between devices: 20.8 us -> 25 us  [moved_by(): return lax.ppermute(value, BOTH, pairs)]
    ppermute x29, starting transfers between devices: 40.9 us -> 37.7 us  [moved_by(): return lax.ppermute(value, BOTH, pairs)]
    add x2 -> x0, other arithmetic: 2.01 us -> none  [the longest x1 1.42 us: on_device(): back_sum = back_parts[0].astype(F32) + back_parts[1].astype(F32)]
    pallas_call x6, Pallas kernels: 25.9 us -> 27.9 us  [run(): pl.pallas_call(body, out_shape=tuple((jax.ShapeDtypeStruct(*one) for one...]
  transfers between devices with their start and end apart: 31 -> 31, of which waited for: 9 -> 9; matrix products, arithmetic and copies ran while one was open for 7% -> 4% of each run, Pallas kernels for 9% -> 10%
where the time goes in v4:
time: 120 us
  starting transfers between devices  49.2 us (41%)
  waiting for transfers between devices  33.3 us (28%)
  Pallas kernels  27.9 us (23%)
  local copies, waits for them, and re-layouts  5.98 us (5%)
  other arithmetic  2.55 us (2%)
    ppermute x29, starting transfers between devices, moved_by(): return lax.ppermute(value, BOTH, pairs)  37.7 us
    pallas_call x6, Pallas kernels, run(): pl.pallas_call(body, out_shape=tuple((jax.ShapeDtypeStruct(*one) for one...  27.9 us
    ppermute x29, waiting for transfers between devices, moved_by(): return lax.ppermute(value, BOTH, pairs)  25 us
    all_to_all x2, starting transfers between devices, exchange(): lax.all_to_all(blocks, BOTH, 0, 0, axis_index_groups=groups, tiled=True)  11.5 us
    all_to_all x2, waiting for transfers between devices, exchange(): lax.all_to_all(blocks, BOTH, 0, 0, axis_index_groups=groups, tiled=True)  8.22 us
  transfers between devices with their start and end apart: 31, of which 9 were waited for; matrix products, arithmetic and copies ran while one was open for 4% of the time, Pallas kernels for 10%

profile of v4, /device:TPU:32, one launch (start us, length us, event | category | flops | bytes accessed | tf_op | source)
XLA Modules:
  0.0 119.8 jit_solution(16938256886204544826)
XLA Ops:
  1.5 1.9 %collective-permute-start = (bf16[9,1024]{1,0:T(8,128)(2,1)S(1)}, bf16[9,1024]{1,0:T(8,128)(2,1)S(1)}, u32[]{:S(2)}, u32[]{:S(2)}) collective-permute-start(bf16[9,1024]{1,0:T(8,128)(2,1)S(1)} %reshape.33), channel_id=1, source_target_pairs={{0,192},{1,193},{2,194},{3,195},{4,196},{5,197},{6,198},{7,199},{8... | collective-permute-start | bytes 55304 | tf_op jit(solution)/shard_map/ppermute | solution.py:40
  5.0 2.8 %collective-permute-start.2 = (bf16[9,1024]{1,0:T(8,128)(2,1)S(1)}, bf16[9,1024]{1,0:T(8,128)(2,1)S(1)}, u32[]{:S(2)}, u32[]{:S(2)}) collective-permute-start(bf16[9,1024]{1,0:T(8,128)(2,1)S(1)} %reshape.33), channel_id=1, source_target_pairs={{0,64},{1,65},{2,66},{3,67},{4,68},{5,69},{6,70},{7,71},{8,72},{9,... | collective-permute-start | bytes 55304 | tf_op jit(solution)/shard_map/ppermute | solution.py:40
  11.1 2.8 %collective-permute-start.3 = (bf16[40,1024]{1,0:T(8,128)(2,1)S(1)}, bf16[40,1024]{1,0:T(8,128)(2,1)S(1)}, u32[]{:S(2)}, u32[]{:S(2)}) collective-permute-start(bf16[40,1024]{1,0:T(8,128)(2,1)S(1)} %fusion.6), channel_id=1, source_target_pairs={{0,3},{1,0},{2,1},{3,2},{4,7},{5,4},{6,5},{7,6},{8,11},{9,8},{10,9... | collective-permute-start | bytes 245768 | tf_op jit(solution)/shard_map/ppermute | solution.py:40
  15.6 7.6 %all-to-all-start = ((bf16[8,64,1024]{2,1,0:T(8,128)(2,1)}), bf16[8,64,1024]{2,1,0:T(8,128)(2,1)S(1)}, u32[]{:S(2)}, u32[]{:S(2)}) async-start(bf16[8,64,1024]{2,1,0:T(8,128)(2,1)} %pad_maximum_fusion), calls=%async_computation | async-start | bytes 2097152 | tf_op jit(solution)/shard_map/all_to_all | solution.py:32
  24.9 3.1 %collective-permute-start.9 = (bf16[4,16,2304]{2,1,0:T(8,128)(2,1)S(1)}, bf16[4,16,2304]{2,1,0:T(8,128)(2,1)S(1)}, u32[]{:S(2)}, u32[]{:S(2)}) collective-permute-start(bf16[4,16,2304]{2,1,0:T(8,128)(2,1)S(1)} %reshape.36.own0), channel_id=1, source_target_pairs={{0,48},{1,49},{2,50},{3,51},{4,52},{5,53},{6,54},{7,55},{8,56},{9,... | collective-permute-start | bytes 884744 | tf_op jit(solution)/shard_map/ppermute | solution.py:40
  29.6 2.0 %collective-permute-start.6 = (bf16[64,1024]{1,0:T(8,128)(2,1)}, bf16[64,1024]{1,0:T(8,128)(2,1)S(1)}, u32[]{:S(2)}, u32[]{:S(2)}) collective-permute-start(bf16[64,1024]{1,0:T(8,128)(2,1)} %get-tuple-element.43), channel_id=1, source_target_pairs={{0,1},{1,2},{2,3},{3,0},{4,5},{5,6},{6,7},{7,4},{8,9},{9,10},{10,1... | collective-permute-start | bytes 393224 | tf_op jit(solution)/shard_map/ppermute | solution.py:40
  31.7 2.7 %collective-permute-start.7 = (bf16[64,1024]{1,0:T(8,128)(2,1)S(1)}, bf16[64,1024]{1,0:T(8,128)(2,1)S(1)}, u32[]{:S(2)}, u32[]{:S(2)}) collective-permute-start(bf16[64,1024]{1,0:T(8,128)(2,1)S(1)} %get-tuple-element.44), channel_id=1, source_target_pairs={{0,2},{1,3},{2,0},{3,1},{4,6},{5,7},{6,4},{7,5},{8,10},{9,11},{10,... | collective-permute-start | bytes 393224 | tf_op jit(solution)/shard_map/ppermute | solution.py:40
  34.4 1.7 %collective-permute-done.6.cot1 = bf16[64,1024]{1,0:T(8,128)(2,1)S(1)} collective-permute-done((bf16[64,1024]{1,0:T(8,128)(2,1)}, bf16[64,1024]{1,0:T(8,128)(2,1)S(1)}, u32[]{:S(2)}, u32[]{:S(2)}) %collective-permute-start.6) | collective-permute-done | bytes 131104 | tf_op jit(solution)/shard_map/ppermute | solution.py:40
  36.1 3.0 %collective-permute-done.7.cot2 = bf16[64,1024]{1,0:T(8,128)(2,1)S(1)} collective-permute-done((bf16[64,1024]{1,0:T(8,128)(2,1)S(1)}, bf16[64,1024]{1,0:T(8,128)(2,1)S(1)}, u32[]{:S(2)}, u32[]{:S(2)}) %collective-permute-start.7) | collective-permute-done | bytes 131104 | tf_op jit(solution)/shard_map/ppermute | solution.py:40
  39.9 2.5 %collective-permute-done.11.own3 = bf16[4,16,2304]{2,1,0:T(8,128)(2,1)S(1)} collective-permute-done((bf16[4,16,2304]{2,1,0:T(8,128)(2,1)S(1)}, bf16[4,16,2304]{2,1,0:T(8,128)(2,1)S(1)}, u32[]{:S(2)}, u32[]{:S(2)}) %collective-permute-start.11) | collective-permute-done | bytes 294944 | tf_op jit(solution)/shard_map/ppermute | solution.py:40
  42.4 8.2 %all-to-all-done = bf16[8,64,1024]{2,1,0:T(8,128)(2,1)S(1)} async-done(((bf16[8,64,1024]{2,1,0:T(8,128)(2,1)}), bf16[8,64,1024]{2,1,0:T(8,128)(2,1)S(1)}, u32[]{:S(2)}, u32[]{:S(2)}) %all-to-all-start) | async-done | bytes 1048608 | tf_op jit(solution)/shard_map/all_to_all | solution.py:32
  51.8 14.7 %gradient.1 = (f32[256,128]{1,0:T(8,128)S(1)}, bf16[4,4,16,2304]{3,2,1,0:T(8,128)(2,1)S(1)}, f32[4,4,16,2304]{3,2,1,0:T(8,128)S(1)}, bf16[512,1152]{1,0:T(8,128)(2,1)}, bf16[512,2304]{1,0:T(8,128)(2,1)S(1)}) custom-call(s32[4]{0:T(128)S(1)} %ready.1.place, f32[8,512]{1,0:T(8,128)S(1)} %broadcast_in_dim.7.style, bf16[64,1024]{1,0:T(8,128)(2,1)S(1)} %get-tuple-element.42.cot0, ...), custom_call_target="tpu_custom_call" | custom-call | flops 4831838208 | bytes 1048576 | tf_op jit(solution)/shard_map/gradient/pallas_call | solution.py:305
  66.6 2.8 %collective-permute-done.16.received = bf16[4,4,16,2304]{3,2,1,0:T(8,128)(2,1)S(1)} collective-permute-done((bf16[4,4,16,2304]{3,2,1,0:T(8,128)(2,1)S(1)}, bf16[4,4,16,2304]{3,2,1,0:T(8,128)(2,1)S(1)}, u32[]{:S(2)}, u32[]{:S(2)}) %collective-permute-start.16) | collective-permute-done | bytes 1179680 | tf_op jit(solution)/shard_map/ppermute | solution.py:40
  70.7 1.6 %collective-permute-start.17 = (bf16[4,16,2304]{2,1,0:T(8,128)(2,1)}, bf16[4,16,2304]{2,1,0:T(8,128)(2,1)S(1)}, u32[]{:S(2)}, u32[]{:S(2)}) collective-permute-start(bf16[4,16,2304]{2,1,0:T(8,128)(2,1)} %get-tuple-element.55), channel_id=1, source_target_pairs={{0,16},{1,17},{2,18},{3,19},{4,20},{5,21},{6,22},{7,23},{8,24},{9,... | collective-permute-start | bytes 884744 | tf_op jit(solution)/shard_map/ppermute | solution.py:40
  72.2 2.9 %collective-permute-start.18 = (bf16[4,16,2304]{2,1,0:T(8,128)(2,1)}, bf16[4,16,2304]{2,1,0:T(8,128)(2,1)S(1)}, u32[]{:S(2)}, u32[]{:S(2)}) collective-permute-start(bf16[4,16,2304]{2,1,0:T(8,128)(2,1)} %get-tuple-element.56), channel_id=1, source_target_pairs={{0,32},{1,33},{2,34},{3,35},{4,36},{5,37},{6,38},{7,39},{8,40},{9,... | collective-permute-start | bytes 884744 | tf_op jit(solution)/shard_map/ppermute | solution.py:40
  76.5 4.0 %all-to-all-start.1 = ((bf16[8,64,1152]{2,1,0:T(8,128)(2,1)}), bf16[8,64,1152]{2,1,0:T(8,128)(2,1)S(1)}, u32[]{:S(2)}, u32[]{:S(2)}) async-start(bf16[8,64,1152]{2,1,0:T(8,128)(2,1)} %bitcast.20), calls=%async_computation.1 | async-start | bytes 2359296 | tf_op jit(solution)/shard_map/all_to_all | solution.py:32
  81.2 7.5 %collective-permute-done.18.part2 = bf16[4,16,2304]{2,1,0:T(8,128)(2,1)S(1)} collective-permute-done((bf16[4,16,2304]{2,1,0:T(8,128)(2,1)}, bf16[4,16,2304]{2,1,0:T(8,128)(2,1)S(1)}, u32[]{:S(2)}, u32[]{:S(2)}) %collective-permute-start.18) | collective-permute-done | bytes 294944 | tf_op jit(solution)/shard_map/ppermute | solution.py:40
  91.1 2.6 %collective-permute-start.21 = (bf16[4,80,128]{2,1,0:T(8,128)(2,1)S(1)}, bf16[4,80,128]{2,1,0:T(8,128)(2,1)S(1)}, u32[]{:S(2)}, u32[]{:S(2)}) collective-permute-start(bf16[4,80,128]{2,1,0:T(8,128)(2,1)S(1)} %get-tuple-element.60), channel_id=1, source_target_pairs={{0,2},{1,3},{2,0},{3,1},{4,6},{5,7},{6,4},{7,5},{8,10},{9,11},{10,... | collective-permute-start | bytes 245768 | tf_op jit(solution)/shard_map/ppermute | solution.py:40
  95.1 1.7 %copy-done.3 = bf16[512,2304]{1,0:T(8,128)(2,1)S(1)} copy-done((bf16[512,2304]{1,0:T(8,128)(2,1)S(1)}, bf16[512,2304]{1,0:T(8,128)(2,1)}, u32[]{:S(2)}) %copy-start.3) | copy-done | bytes 2359320
  96.8 7.2 %forward.1 = bf16[4,64,1024]{2,1,0:T(8,128)(2,1)S(1)} custom-call(s32[4]{0:T(128)S(1)} %pad_add_fusion.place, bf16[512,1024]{1,0:T(8,128)(2,1)S(1)} %bitcast.60, bf16[512,2304]{1,0:T(8,128)(2,1)S(1)} %copy-done.3, f32[256,128]{1,0:T(8,128)S(1)} %copy-done.5), custom_call_target="tpu_custom_call" | custom-call | flops 48318382080 | bytes 1048576 | tf_op jit(solution)/shard_map/forward/pallas_call | solution.py:305
  105.7 2.1 %collective-permute-start.25 = (bf16[64,1024]{1,0:T(8,128)(2,1)S(1)}, bf16[64,1024]{1,0:T(8,128)(2,1)S(1)}, u32[]{:S(2)}, u32[]{:S(2)}) collective-permute-start(bf16[64,1024]{1,0:T(8,128)(2,1)S(1)} %get-tuple-element.76), channel_id=1, source_target_pairs={{0,3},{1,0},{2,1},{3,2},{4,7},{5,4},{6,5},{7,6},{8,11},{9,8},{10,9... | collective-permute-start | bytes 393224 | tf_op jit(solution)/shard_map/ppermute | solution.py:40
  109.7 4.1 %collective-permute-done.23.part1 = bf16[64,1024]{1,0:T(8,128)(2,1)S(1)} collective-permute-done((bf16[64,1024]{1,0:T(8,128)(2,1)S(1)}, bf16[64,1024]{1,0:T(8,128)(2,1)S(1)}, u32[]{:S(2)}, u32[]{:S(2)}) %collective-permute-start.23) | collective-permute-done | bytes 131104 | tf_op jit(solution)/shard_map/ppermute | solution.py:40
  113.7 2.7 %collective-permute-done.24.part2 = bf16[64,1024]{1,0:T(8,128)(2,1)S(1)} collective-permute-done((bf16[64,1024]{1,0:T(8,128)(2,1)S(1)}, bf16[64,1024]{1,0:T(8,128)(2,1)S(1)}, u32[]{:S(2)}, u32[]{:S(2)}) %collective-permute-start.24) | collective-permute-done | bytes 131104 | tf_op jit(solution)/shard_map/ppermute | solution.py:40
  116.6 2.5 %finish.1 = (bf16[4,64,1024]{2,1,0:T(8,128)(2,1)}, bf16[4,64,1024]{2,1,0:T(8,128)(2,1)}, f32[4,64]{1,0:T(4,128)}) custom-call(s32[4]{0:T(128)S(1)} %pad_add_fusion.place, bf16[64,1024]{1,0:T(8,128)(2,1)S(1)} %get-tuple-element.79.part0, bf16[64,1024]{1,0:T(8,128)(2,1)S(1)} %collective-permute-done.23.part1, ...), custom_call_target="tpu_custom_call" | custom-call | flops 10000000 | bytes 1048576 | tf_op jit(solution)/shard_map/finish/pallas_call | solution.py:305
  (88 shorter events, 24.3 us)
Async XLA Ops:
  1.5 9.5 %collective-permute-start = (bf16[9,1024]{1,0:T(8,128)(2,1)S(1)}, bf16[9,1024]{1,0:T(8,128)(2,1)S(1)}, u32[]{:S(2)}, u32[]{:S(2)}) collective-permute-start(bf16[9,1024]{1,0:T(8,128)(2,1)S(1)} %reshape.33), channel_id=1, source_target_pairs={{0,192},{1,193},{2,194},{3,195},{4,196},{5,197},{6,198},{7,199},{8... | collective-permute-start | bytes 55304 | tf_op jit(solution)/shard_map/ppermute | solution.py:40
  11.1 12.1 %collective-permute-start.3 = (bf16[40,1024]{1,0:T(8,128)(2,1)S(1)}, bf16[40,1024]{1,0:T(8,128)(2,1)S(1)}, u32[]{:S(2)}, u32[]{:S(2)}) collective-permute-start(bf16[40,1024]{1,0:T(8,128)(2,1)S(1)} %fusion.6), channel_id=1, source_target_pairs={{0,3},{1,0},{2,1},{3,2},{4,7},{5,4},{6,5},{7,6},{8,11},{9,8},{10,9... | collective-permute-start | bytes 245768 | tf_op jit(solution)/shard_map/ppermute | solution.py:40
  13.9 9.3 %collective-permute-start.4 = (bf16[40,1024]{1,0:T(8,128)(2,1)S(1)}, bf16[40,1024]{1,0:T(8,128)(2,1)S(1)}, u32[]{:S(2)}, u32[]{:S(2)}) collective-permute-start(bf16[40,1024]{1,0:T(8,128)(2,1)S(1)} %fusion.6), channel_id=1, source_target_pairs={{0,2},{1,3},{2,0},{3,1},{4,6},{5,7},{6,4},{7,5},{8,10},{9,11},{10,... | collective-permute-start | bytes 245768 | tf_op jit(solution)/shard_map/ppermute | solution.py:40
  15.6 35.0 %all-to-all-start = ((bf16[8,64,1024]{2,1,0:T(8,128)(2,1)}), bf16[8,64,1024]{2,1,0:T(8,128)(2,1)S(1)}, u32[]{:S(2)}, u32[]{:S(2)}) async-start(bf16[8,64,1024]{2,1,0:T(8,128)(2,1)} %pad_maximum_fusion), calls=%async_computation | async-start | bytes 2097152 | tf_op jit(solution)/shard_map/all_to_all | solution.py:32
  24.9 14.4 %collective-permute-start.9 = (bf16[4,16,2304]{2,1,0:T(8,128)(2,1)S(1)}, bf16[4,16,2304]{2,1,0:T(8,128)(2,1)S(1)}, u32[]{:S(2)}, u32[]{:S(2)}) collective-permute-start(bf16[4,16,2304]{2,1,0:T(8,128)(2,1)S(1)} %reshape.36.own0), channel_id=1, source_target_pairs={{0,48},{1,49},{2,50},{3,51},{4,52},{5,53},{6,54},{7,55},{8,56},{9,... | collective-permute-start | bytes 884744 | tf_op jit(solution)/shard_map/ppermute | solution.py:40
  28.0 11.3 %collective-permute-start.10 = (bf16[4,16,2304]{2,1,0:T(8,128)(2,1)S(1)}, bf16[4,16,2304]{2,1,0:T(8,128)(2,1)S(1)}, u32[]{:S(2)}, u32[]{:S(2)}) collective-permute-start(bf16[4,16,2304]{2,1,0:T(8,128)(2,1)S(1)} %reshape.36.own0), channel_id=1, source_target_pairs={{0,32},{1,33},{2,34},{3,35},{4,36},{5,37},{6,38},{7,39},{8,40},{9,... | collective-permute-start | bytes 884744 | tf_op jit(solution)/shard_map/ppermute | solution.py:40
  28.7 13.7 %collective-permute-start.11 = (bf16[4,16,2304]{2,1,0:T(8,128)(2,1)S(1)}, bf16[4,16,2304]{2,1,0:T(8,128)(2,1)S(1)}, u32[]{:S(2)}, u32[]{:S(2)}) collective-permute-start(bf16[4,16,2304]{2,1,0:T(8,128)(2,1)S(1)} %reshape.36.own0), channel_id=1, source_target_pairs={{0,16},{1,17},{2,18},{3,19},{4,20},{5,21},{6,22},{7,23},{8,24},{9,... | collective-permute-start | bytes 884744 | tf_op jit(solution)/shard_map/ppermute | solution.py:40
  36.1 15.7 %collective-permute-start.12 = (bf16[4,16,2304]{2,1,0:T(8,128)(2,1)S(1)}, bf16[4,16,2304]{2,1,0:T(8,128)(2,1)S(1)}, u32[]{:S(2)}, u32[]{:S(2)}) collective-permute-start(bf16[4,16,2304]{2,1,0:T(8,128)(2,1)S(1)} %reshape.36.own0), channel_id=1, source_target_pairs={{0,8},{1,9},{2,10},{3,11},{4,12},{5,13},{6,14},{7,15},{8,0},{9,1},... | collective-permute-start | bytes 884744 | tf_op jit(solution)/shard_map/ppermute | solution.py:40
  39.1 12.7 %collective-permute-start.8 = (bf16[64,1024]{1,0:T(8,128)(2,1)}, bf16[64,1024]{1,0:T(8,128)(2,1)}, u32[]{:S(2)}, u32[]{:S(2)}) collective-permute-start(bf16[64,1024]{1,0:T(8,128)(2,1)} %get-tuple-element.45), channel_id=1, source_target_pairs={{0,3},{1,0},{2,1},{3,2},{4,7},{5,4},{6,5},{7,6},{8,11},{9,8},{10,9... | collective-permute-start | bytes 393224 | tf_op jit(solution)/shard_map/ppermute | solution.py:40
  39.4 12.4 %collective-permute-start.13 = (bf16[4,16,2304]{2,1,0:T(8,128)(2,1)S(1)}, bf16[4,16,2304]{2,1,0:T(8,128)(2,1)S(1)}, u32[]{:S(2)}, u32[]{:S(2)}) collective-permute-start(bf16[4,16,2304]{2,1,0:T(8,128)(2,1)S(1)} %collective-permute-done.9.own1), channel_id=1, source_target_pairs={{0,8},{1,9},{2,10},{3,11},{4,12},{5,13},{6,14},{7,15},{8,0},{9,1},... | collective-permute-start | bytes 884744 | tf_op jit(solution)/shard_map/ppermute | solution.py:40
  39.4 12.4 %collective-permute-start.14 = (bf16[4,16,2304]{2,1,0:T(8,128)(2,1)S(1)}, bf16[4,16,2304]{2,1,0:T(8,128)(2,1)S(1)}, u32[]{:S(2)}, u32[]{:S(2)}) collective-permute-start(bf16[4,16,2304]{2,1,0:T(8,128)(2,1)S(1)} %collective-permute-done.10.own2), channel_id=1, source_target_pairs={{0,8},{1,9},{2,10},{3,11},{4,12},{5,13},{6,14},{7,15},{8,0},{9,1},... | collective-permute-start | bytes 884744 | tf_op jit(solution)/shard_map/ppermute | solution.py:40
  42.4 9.4 %collective-permute-start.15 = (bf16[4,16,2304]{2,1,0:T(8,128)(2,1)S(1)}, bf16[4,16,2304]{2,1,0:T(8,128)(2,1)}, u32[]{:S(2)}, u32[]{:S(2)}) collective-permute-start(bf16[4,16,2304]{2,1,0:T(8,128)(2,1)S(1)} %collective-permute-done.11.own3), channel_id=1, source_target_pairs={{0,8},{1,9},{2,10},{3,11},{4,12},{5,13},{6,14},{7,15},{8,0},{9,1},... | collective-permute-start | bytes 884744 | tf_op jit(solution)/shard_map/ppermute | solution.py:40
  70.7 10.5 %collective-permute-start.17 = (bf16[4,16,2304]{2,1,0:T(8,128)(2,1)}, bf16[4,16,2304]{2,1,0:T(8,128)(2,1)S(1)}, u32[]{:S(2)}, u32[]{:S(2)}) collective-permute-start(bf16[4,16,2304]{2,1,0:T(8,128)(2,1)} %get-tuple-element.55), channel_id=1, source_target_pairs={{0,16},{1,17},{2,18},{3,19},{4,20},{5,21},{6,22},{7,23},{8,24},{9,... | collective-permute-start | bytes 884744 | tf_op jit(solution)/shard_map/ppermute | solution.py:40
  72.2 16.4 %collective-permute-start.18 = (bf16[4,16,2304]{2,1,0:T(8,128)(2,1)}, bf16[4,16,2304]{2,1,0:T(8,128)(2,1)S(1)}, u32[]{:S(2)}, u32[]{:S(2)}) collective-permute-start(bf16[4,16,2304]{2,1,0:T(8,128)(2,1)} %get-tuple-element.56), channel_id=1, source_target_pairs={{0,32},{1,33},{2,34},{3,35},{4,36},{5,37},{6,38},{7,39},{8,40},{9,... | collective-permute-start | bytes 884744 | tf_op jit(solution)/shard_map/ppermute | solution.py:40
  75.1 13.6 %collective-permute-start.19 = (bf16[4,16,2304]{2,1,0:T(8,128)(2,1)}, bf16[4,16,2304]{2,1,0:T(8,128)(2,1)S(1)}, u32[]{:S(2)}, u32[]{:S(2)}) collective-permute-start(bf16[4,16,2304]{2,1,0:T(8,128)(2,1)} %get-tuple-element.57), channel_id=1, source_target_pairs={{0,48},{1,49},{2,50},{3,51},{4,52},{5,53},{6,54},{7,55},{8,56},{9,... | collective-permute-start | bytes 884744 | tf_op jit(solution)/shard_map/ppermute | solution.py:40
  76.5 40.0 %all-to-all-start.1 = ((bf16[8,64,1152]{2,1,0:T(8,128)(2,1)}), bf16[8,64,1152]{2,1,0:T(8,128)(2,1)S(1)}, u32[]{:S(2)}, u32[]{:S(2)}) async-start(bf16[8,64,1152]{2,1,0:T(8,128)(2,1)} %bitcast.20), calls=%async_computation.1 | async-start | bytes 2359296 | tf_op jit(solution)/shard_map/all_to_all | solution.py:32
  89.8 14.2 %collective-permute-start.20 = (bf16[4,80,128]{2,1,0:T(8,128)(2,1)S(1)}, bf16[4,80,128]{2,1,0:T(8,128)(2,1)S(1)}, u32[]{:S(2)}, u32[]{:S(2)}) collective-permute-start(bf16[4,80,128]{2,1,0:T(8,128)(2,1)S(1)} %get-tuple-element.59), channel_id=1, source_target_pairs={{0,1},{1,2},{2,3},{3,0},{4,5},{5,6},{6,7},{7,4},{8,9},{9,10},{10,1... | collective-permute-start | bytes 245768 | tf_op jit(solution)/shard_map/ppermute | solution.py:40
  91.1 13.0 %collective-permute-start.21 = (bf16[4,80,128]{2,1,0:T(8,128)(2,1)S(1)}, bf16[4,80,128]{2,1,0:T(8,128)(2,1)S(1)}, u32[]{:S(2)}, u32[]{:S(2)}) collective-permute-start(bf16[4,80,128]{2,1,0:T(8,128)(2,1)S(1)} %get-tuple-element.60), channel_id=1, source_target_pairs={{0,2},{1,3},{2,0},{3,1},{4,6},{5,7},{6,4},{7,5},{8,10},{9,11},{10,... | collective-permute-start | bytes 245768 | tf_op jit(solution)/shard_map/ppermute | solution.py:40
  93.7 10.4 %collective-permute-start.22 = (bf16[4,80,128]{2,1,0:T(8,128)(2,1)S(1)}, bf16[4,80,128]{2,1,0:T(8,128)(2,1)S(1)}, u32[]{:S(2)}, u32[]{:S(2)}) collective-permute-start(bf16[4,80,128]{2,1,0:T(8,128)(2,1)S(1)} %get-tuple-element.61), channel_id=1, source_target_pairs={{0,3},{1,0},{2,1},{3,2},{4,7},{5,4},{6,5},{7,6},{8,11},{9,8},{10,9... | collective-permute-start | bytes 245768 | tf_op jit(solution)/shard_map/ppermute | solution.py:40
  104.2 9.6 %collective-permute-start.23 = (bf16[64,1024]{1,0:T(8,128)(2,1)S(1)}, bf16[64,1024]{1,0:T(8,128)(2,1)S(1)}, u32[]{:S(2)}, u32[]{:S(2)}) collective-permute-start(bf16[64,1024]{1,0:T(8,128)(2,1)S(1)} %get-tuple-element.78), channel_id=1, source_target_pairs={{0,1},{1,2},{2,3},{3,0},{4,5},{5,6},{6,7},{7,4},{8,9},{9,10},{10,1... | collective-permute-start | bytes 393224 | tf_op jit(solution)/shard_map/ppermute | solution.py:40
  104.8 11.7 %collective-permute-start.24 = (bf16[64,1024]{1,0:T(8,128)(2,1)S(1)}, bf16[64,1024]{1,0:T(8,128)(2,1)S(1)}, u32[]{:S(2)}, u32[]{:S(2)}) collective-permute-start(bf16[64,1024]{1,0:T(8,128)(2,1)S(1)} %get-tuple-element.77), channel_id=1, source_target_pairs={{0,2},{1,3},{2,0},{3,1},{4,6},{5,7},{6,4},{7,5},{8,10},{9,11},{10,... | collective-permute-start | bytes 393224 | tf_op jit(solution)/shard_map/ppermute | solution.py:40
  105.7 10.7 %collective-permute-start.25 = (bf16[64,1024]{1,0:T(8,128)(2,1)S(1)}, bf16[64,1024]{1,0:T(8,128)(2,1)S(1)}, u32[]{:S(2)}, u32[]{:S(2)}) collective-permute-start(bf16[64,1024]{1,0:T(8,128)(2,1)S(1)} %get-tuple-element.76), channel_id=1, source_target_pairs={{0,3},{1,0},{2,1},{3,2},{4,7},{5,4},{6,5},{7,6},{8,11},{9,8},{10,9... | collective-permute-start | bytes 393224 | tf_op jit(solution)/shard_map/ppermute | solution.py:40
  107.8 11.2 %collective-permute-start.26 = (bf16[80,128]{1,0:T(8,128)(2,1)S(1)}, bf16[80,128]{1,0:T(8,128)(2,1)S(1)}, u32[]{:S(2)}, u32[]{:S(2)}) collective-permute-start(bf16[80,128]{1,0:T(8,128)(2,1)S(1)} %get-tuple-element.86), channel_id=1, source_target_pairs={{0,64},{1,65},{2,66},{3,67},{4,68},{5,69},{6,70},{7,71},{8,72},{9,... | collective-permute-start | bytes 61448 | tf_op jit(solution)/shard_map/ppermute | solution.py:40
  108.7 10.3 %collective-permute-start.27 = (bf16[80,128]{1,0:T(8,128)(2,1)S(1)}, bf16[80,128]{1,0:T(8,128)(2,1)S(1)}, u32[]{:S(2)}, u32[]{:S(2)}) collective-permute-start(bf16[80,128]{1,0:T(8,128)(2,1)S(1)} %get-tuple-element.85), channel_id=1, source_target_pairs={{0,128},{1,129},{2,130},{3,131},{4,132},{5,133},{6,134},{7,135},{8... | collective-permute-start | bytes 61448 | tf_op jit(solution)/shard_map/ppermute | solution.py:40
  (14 other events, 90.9 us)

commit v5 on v4

--- a/solution.py
+++ b/solution.py
@@ -59,10 +59,9 @@
     return (((place[0] + l) % 4) * 4 + (place[1] + k) % 4) * 32
 
 
-def ready_body(place, whole, out):
+def ready_body(style, whole, out):
     del whole
-    for index in range(4):
-        out[index] = place[index]
+    out[...] = style[...]
 
 
 def gradient_body(
@@ -193,12 +192,26 @@
         keep_copy(step).wait()
 
 
-def forward_body(place, whole, kernel_in, demod_in, out, products, kernel_t, images, demod, sems):
+def flip_body(kernel_in, out, kernel_t, sems):
+    def enter(t):
+        lanes = pl.ds(pl.multiple_of(t * 256, 256), 256)
+        return pltpu.make_async_copy(kernel_in.at[:, lanes], kernel_t.at[:, lanes], sems.at[t])
+
+    @pl.loop(0, 9)
+    def _(t):
+        enter(t).start()
+
+    @pl.loop(0, 9)
+    def _(t):
+        enter(t).wait()
+        part = pl.ds(pl.multiple_of(t * 256, 256), 256)
+        out[part, :] = jnp.transpose(kernel_t[:, part])
+
+
+def forward_body(place, whole, kernel, demod_in, out, products, images, demod, sems):
     copies = [
         pltpu.make_async_copy(source, target, sems.at[index])
-        for index, (source, target) in enumerate(
-            ((kernel_in, kernel_t), (whole, images), (demod_in, demod))
-        )
+        for index, (source, target) in enumerate(((whole, images), (demod_in, demod)))
     ]
     for copy in copies:
         copy.start()
@@ -208,8 +221,8 @@
     @pl.loop(0, 4)
     def _(step):
         lanes = pl.ds(pl.multiple_of(step * 256, 256), 256)
-        products[:, lanes] = lax.dot_general(
-            kernel_t[...], images[:, lanes], (((0,), (0,)), ((), ())), preferred_element_type=F32
+        products[:, lanes] = jnp.dot(
+            kernel[...], images[:, lanes], preferred_element_type=F32
         )
 
     @pl.loop(0, 8)
@@ -348,7 +361,7 @@
     kernels = own + [moved_by(one, "c", 1) for one in own]
 
     (ready,) = run(
-        ready_body, "ready", [((4,), jnp.int32)], pltpu.SMEM, [], 1, 12 * PRODUCT, place, whole,
+        ready_body, "ready", [((8, 512), F32)], VM, [], 1, 12 * PRODUCT, style, whole,
         far=(1,),
     )
     blocks = (4, 4, 16, 2304)
@@ -379,14 +392,25 @@
         ],
         32,
         2 * PRODUCT,
+        place,
         ready,
-        style,
         *cots,
         whole,
         *kernels,
         far=(6,),
     )
     received = moved_by(send, "c", 1)
+    halves = run(
+        pair_body, "pair_sum", [((4, 16, 2304), BF16)] * 4, VM, [], 8, 10**7, keep, received
+    )
+    halves, back = lax.optimization_barrier((halves, back))
+    back_parts = exchange(back.reshape(8, 64, 1152), "hx").reshape(2, 4, 64, 1152)
+    quarters = [halves[0]] + [moved_by(halves[k], "y", k) for k in (1, 2, 3)]
+    (kernel,) = run(
+        flip_body, "flip", [((2304, 512), BF16)], VM,
+        [VM((512, 2304), BF16), pltpu.SemaphoreType.DMA((9,))], 8, 10**7, kernel_t, far=(0,),
+    )
+    kernel, *quarters = lax.optimization_barrier((kernel, *quarters))
     (out,) = run(
         forward_body,
         "forward",
@@ -394,25 +418,18 @@
         VM,
         [
             VM((2304, 1024), F32),
-            VM((512, 2304), BF16),
             VM((512, 1024), BF16),
             VM((256, 128), F32),
-            pltpu.SemaphoreType.DMA((3,)),
+            pltpu.SemaphoreType.DMA((2,)),
         ],
         18,
         20 * PRODUCT,
         place,
         whole,
-        kernel_t,
+        kernel,
         demod,
-        far=(1, 2, 3),
-    )
-    halves = run(
-        pair_body, "pair_sum", [((4, 16, 2304), BF16)] * 4, VM, [], 8, 10**7, keep, received
-    )
-    halves, back = lax.optimization_barrier((halves, back))
-    back_parts = exchange(back.reshape(8, 64, 1152), "hx").reshape(2, 4, 64, 1152)
-    quarters = [halves[0]] + [moved_by(halves[k], "y", k) for k in (1, 2, 3)]
+        far=(1, 3),
+    )
     pieces = run(
         quarter_body, "quarter_sum", [((4, 80, 128), BF16)] * 4, VM, [VM((16, 2304), F32)],
         6, 10**7, place, *quarters,

time: 120 us -> 122 us (1.017)
  local copies, waits for them, and re-layouts: 5.98 us -> 8.72 us
    unnamed x21 -> x35, local copies, waits for them, and re-layouts: 1.75 us -> 3.28 us
    pallas_call x6 -> x7, Pallas kernels: 27.9 us -> 28 us  [run(): pl.pallas_call(body, out_shape=tuple((jax.ShapeDtypeStruct(*one) for one...]
  transfers between devices with their start and end apart: 31 -> 31, of which waited for: 9 -> 8; matrix products, arithmetic and copies ran while one was open for 4% -> 5% of each run, Pallas kernels for 10% -> 10%
where the time goes in v5:
time: 122 us
  starting transfers between devices  49.4 us (40%)
  waiting for transfers between devices  32.4 us (27%)
  Pallas kernels  28 us (23%)
  local copies, waits for them, and re-layouts  8.72 us (7%)
  other arithmetic  2.53 us (2%)
    ppermute x29, starting transfers between devices, moved_by(): return lax.ppermute(value, BOTH, pairs)  37.9 us
    pallas_call x7, Pallas kernels, run(): pl.pallas_call(body, out_shape=tuple((jax.ShapeDtypeStruct(*one) for one...  28 us
    ppermute x29, waiting for transfers between devices, moved_by(): return lax.ppermute(value, BOTH, pairs)  24.2 us
    all_to_all x2, starting transfers between devices, exchange(): lax.all_to_all(blocks, BOTH, 0, 0, axis_index_groups=groups, tiled=True)  11.5 us
    all_to_all x2, waiting for transfers between devices, exchange(): lax.all_to_all(blocks, BOTH, 0, 0, axis_index_groups=groups, tiled=True)  8.22 us
    unnamed x35, local copies, waits for them, and re-layouts  3.28 us
  transfers between devices with their start and end apart: 31, of which 8 were waited for; matrix products, arithmetic and copies ran while one was open for 5% of the time, Pallas kernels for 10%

profile of v5, /device:TPU:32, one launch (start us, length us, event | category | flops | bytes accessed | tf_op | source)
XLA Modules:
  0.0 122.1 jit_solution(3882391871277118918)
XLA Ops:
  1.5 1.9 %collective-permute-start = (bf16[9,1024]{1,0:T(8,128)(2,1)S(1)}, bf16[9,1024]{1,0:T(8,128)(2,1)S(1)}, u32[]{:S(2)}, u32[]{:S(2)}) collective-permute-start(bf16[9,1024]{1,0:T(8,128)(2,1)S(1)} %reshape.33), channel_id=1, source_target_pairs={{0,192},{1,193},{2,194},{3,195},{4,196},{5,197},{6,198},{7,199},{8... | collective-permute-start | bytes 55304 | tf_op jit(solution)/shard_map/ppermute | solution.py:40
  3.5 1.5 %collective-permute-start.1 = (bf16[9,1024]{1,0:T(8,128)(2,1)S(1)}, bf16[9,1024]{1,0:T(8,128)(2,1)S(1)}, u32[]{:S(2)}, u32[]{:S(2)}) collective-permute-start(bf16[9,1024]{1,0:T(8,128)(2,1)S(1)} %reshape.33), channel_id=1, source_target_pairs={{0,128},{1,129},{2,130},{3,131},{4,132},{5,133},{6,134},{7,135},{8... | collective-permute-start | bytes 55304 | tf_op jit(solution)/shard_map/ppermute | solution.py:40
  5.0 2.8 %collective-permute-start.2 = (bf16[9,1024]{1,0:T(8,128)(2,1)S(1)}, bf16[9,1024]{1,0:T(8,128)(2,1)S(1)}, u32[]{:S(2)}, u32[]{:S(2)}) collective-permute-start(bf16[9,1024]{1,0:T(8,128)(2,1)S(1)} %reshape.33), channel_id=1, source_target_pairs={{0,64},{1,65},{2,66},{3,67},{4,68},{5,69},{6,70},{7,71},{8,72},{9,... | collective-permute-start | bytes 55304 | tf_op jit(solution)/shard_map/ppermute | solution.py:40
  11.0 2.8 %collective-permute-start.3 = (bf16[40,1024]{1,0:T(8,128)(2,1)S(1)}, bf16[40,1024]{1,0:T(8,128)(2,1)S(1)}, u32[]{:S(2)}, u32[]{:S(2)}) collective-permute-start(bf16[40,1024]{1,0:T(8,128)(2,1)S(1)} %fusion.6), channel_id=1, source_target_pairs={{0,3},{1,0},{2,1},{3,2},{4,7},{5,4},{6,5},{7,6},{8,11},{9,8},{10,9... | collective-permute-start | bytes 245768 | tf_op jit(solution)/shard_map/ppermute | solution.py:40
  15.5 7.6 %all-to-all-start = ((bf16[8,64,1024]{2,1,0:T(8,128)(2,1)}), bf16[8,64,1024]{2,1,0:T(8,128)(2,1)S(1)}, u32[]{:S(2)}, u32[]{:S(2)}) async-start(bf16[8,64,1024]{2,1,0:T(8,128)(2,1)} %pad_maximum_fusion), calls=%async_computation | async-start | bytes 2097152 | tf_op jit(solution)/shard_map/all_to_all | solution.py:32
  24.9 3.1 %collective-permute-start.9 = (bf16[4,16,2304]{2,1,0:T(8,128)(2,1)S(1)}, bf16[4,16,2304]{2,1,0:T(8,128)(2,1)S(1)}, u32[]{:S(2)}, u32[]{:S(2)}) collective-permute-start(bf16[4,16,2304]{2,1,0:T(8,128)(2,1)S(1)} %reshape.36.own0), channel_id=1, source_target_pairs={{0,48},{1,49},{2,50},{3,51},{4,52},{5,53},{6,54},{7,55},{8,56},{9,... | collective-permute-start | bytes 884744 | tf_op jit(solution)/shard_map/ppermute | solution.py:40
  29.6 2.0 %collective-permute-start.6 = (bf16[64,1024]{1,0:T(8,128)(2,1)S(1)}, bf16[64,1024]{1,0:T(8,128)(2,1)S(1)}, u32[]{:S(2)}, u32[]{:S(2)}) collective-permute-start(bf16[64,1024]{1,0:T(8,128)(2,1)S(1)} %get-tuple-element.48), channel_id=1, source_target_pairs={{0,1},{1,2},{2,3},{3,0},{4,5},{5,6},{6,7},{7,4},{8,9},{9,10},{10,1... | collective-permute-start | bytes 393224 | tf_op jit(solution)/shard_map/ppermute | solution.py:40
  31.6 2.7 %collective-permute-start.7 = (bf16[64,1024]{1,0:T(8,128)(2,1)S(1)}, bf16[64,1024]{1,0:T(8,128)(2,1)S(1)}, u32[]{:S(2)}, u32[]{:S(2)}) collective-permute-start(bf16[64,1024]{1,0:T(8,128)(2,1)S(1)} %get-tuple-element.49), channel_id=1, source_target_pairs={{0,2},{1,3},{2,0},{3,1},{4,6},{5,7},{6,4},{7,5},{8,10},{9,11},{10,... | collective-permute-start | bytes 393224 | tf_op jit(solution)/shard_map/ppermute | solution.py:40
  36.5 2.3 %collective-permute-done.7.cot2 = bf16[64,1024]{1,0:T(8,128)(2,1)S(1)} collective-permute-done((bf16[64,1024]{1,0:T(8,128)(2,1)S(1)}, bf16[64,1024]{1,0:T(8,128)(2,1)S(1)}, u32[]{:S(2)}, u32[]{:S(2)}) %collective-permute-start.7) | collective-permute-done | bytes 131104 | tf_op jit(solution)/shard_map/ppermute | solution.py:40
  40.5 1.8 %collective-permute-done.11.own3 = bf16[4,16,2304]{2,1,0:T(8,128)(2,1)S(1)} collective-permute-done((bf16[4,16,2304]{2,1,0:T(8,128)(2,1)S(1)}, bf16[4,16,2304]{2,1,0:T(8,128)(2,1)S(1)}, u32[]{:S(2)}, u32[]{:S(2)}) %collective-permute-start.11) | collective-permute-done | bytes 294944 | tf_op jit(solution)/shard_map/ppermute | solution.py:40
  42.3 8.2 %all-to-all-done = bf16[8,64,1024]{2,1,0:T(8,128)(2,1)S(1)} async-done(((bf16[8,64,1024]{2,1,0:T(8,128)(2,1)}), bf16[8,64,1024]{2,1,0:T(8,128)(2,1)S(1)}, u32[]{:S(2)}, u32[]{:S(2)}) %all-to-all-start) | async-done | bytes 1048608 | tf_op jit(solution)/shard_map/all_to_all | solution.py:32
  52.2 14.1 %gradient.1 = (f32[256,128]{1,0:T(8,128)S(1)}, bf16[4,4,16,2304]{3,2,1,0:T(8,128)(2,1)S(1)}, f32[4,4,16,2304]{3,2,1,0:T(8,128)S(1)}, bf16[512,1152]{1,0:T(8,128)(2,1)S(1)}, bf16[512,2304]{1,0:T(8,128)(2,1)S(1)}) custom-call(s32[4]{0:T(128)S(1)} %pad_add_fusion.place, f32[8,512]{1,0:T(8,128)S(1)} %ready.1.style, bf16[64,1024]{1,0:T(8,128)(2,1)S(1)} %get-tuple-element.47.cot0, ...), custom_call_target="tpu_custom_call" | custom-call | flops 4831838208 | bytes 1048576 | tf_op jit(solution)/shard_map/gradient/pallas_call | solution.py:318
  66.5 2.8 %collective-permute-done.16.received = bf16[4,4,16,2304]{3,2,1,0:T(8,128)(2,1)S(1)} collective-permute-done((bf16[4,4,16,2304]{3,2,1,0:T(8,128)(2,1)S(1)}, bf16[4,4,16,2304]{3,2,1,0:T(8,128)(2,1)S(1)}, u32[]{:S(2)}, u32[]{:S(2)}) %collective-permute-start.16) | collective-permute-done | bytes 1179680 | tf_op jit(solution)/shard_map/ppermute | solution.py:40
  70.5 1.6 %collective-permute-start.17 = (bf16[4,16,2304]{2,1,0:T(8,128)(2,1)}, bf16[4,16,2304]{2,1,0:T(8,128)(2,1)}, u32[]{:S(2)}, u32[]{:S(2)}) collective-permute-start(bf16[4,16,2304]{2,1,0:T(8,128)(2,1)} %get-tuple-element.61), channel_id=1, source_target_pairs={{0,16},{1,17},{2,18},{3,19},{4,20},{5,21},{6,22},{7,23},{8,24},{9,... | collective-permute-start | bytes 884744 | tf_op jit(solution)/shard_map/ppermute | solution.py:40
  72.1 2.9 %collective-permute-start.18 = (bf16[4,16,2304]{2,1,0:T(8,128)(2,1)}, bf16[4,16,2304]{2,1,0:T(8,128)(2,1)}, u32[]{:S(2)}, u32[]{:S(2)}) collective-permute-start(bf16[4,16,2304]{2,1,0:T(8,128)(2,1)} %get-tuple-element.62), channel_id=1, source_target_pairs={{0,32},{1,33},{2,34},{3,35},{4,36},{5,37},{6,38},{7,39},{8,40},{9,... | collective-permute-start | bytes 884744 | tf_op jit(solution)/shard_map/ppermute | solution.py:40
  76.4 1.4 %flip.1.kernel = bf16[2304,512]{1,0:T(8,128)(2,1)S(1)} custom-call(bf16[512,2304]{1,0:T(8,128)(2,1)S(1)} %get-tuple-element.52.kernel_in), custom_call_target="tpu_custom_call" | custom-call | flops 10000000 | bytes 1048576 | tf_op jit(solution)/shard_map/flip/pallas_call | solution.py:318
  77.8 4.0 %all-to-all-start.1 = ((bf16[8,64,1152]{2,1,0:T(8,128)(2,1)}), bf16[8,64,1152]{2,1,0:T(8,128)(2,1)S(1)}, u32[]{:S(2)}, u32[]{:S(2)}) async-start(bf16[8,64,1152]{2,1,0:T(8,128)(2,1)} %bitcast.58), calls=%async_computation.1 | async-start | bytes 2359296 | tf_op jit(solution)/shard_map/all_to_all | solution.py:32
  81.8 6.9 %collective-permute-done.18.part2 = bf16[4,16,2304]{2,1,0:T(8,128)(2,1)} collective-permute-done((bf16[4,16,2304]{2,1,0:T(8,128)(2,1)}, bf16[4,16,2304]{2,1,0:T(8,128)(2,1)}, u32[]{:S(2)}, u32[]{:S(2)}) %collective-permute-start.18) | collective-permute-done | bytes 294944 | tf_op jit(solution)/shard_map/ppermute | solution.py:40
  89.7 1.8 %quarter_sum.1 = (bf16[4,80,128]{2,1,0:T(8,128)(2,1)S(1)}, bf16[4,80,128]{2,1,0:T(8,128)(2,1)S(1)}, bf16[4,80,128]{2,1,0:T(8,128)(2,1)S(1)}, bf16[4,80,128]{2,1,0:T(8,128)(2,1)S(1)}) custom-call(s32[4]{0:T(128)S(1)} %pad_add_fusion.place, bf16[4,16,2304]{2,1,0:T(8,128)(2,1)S(1)} %copy-done.6, bf16[4,16,2304]{2,1,0:T(8,128)(2,1)} %collective-permute-done.17.part1, ...), custom_call_target="tpu_custom_call" | custom-call | flops 10000000 | bytes 1048576 | tf_op jit(solution)/shard_map/quarter_sum/pallas_call | solution.py:318
  92.7 2.7 %collective-permute-start.21 = (bf16[4,80,128]{2,1,0:T(8,128)(2,1)S(1)}, bf16[4,80,128]{2,1,0:T(8,128)(2,1)S(1)}, u32[]{:S(2)}, u32[]{:S(2)}) collective-permute-start(bf16[4,80,128]{2,1,0:T(8,128)(2,1)S(1)} %get-tuple-element.70), channel_id=1, source_target_pairs={{0,2},{1,3},{2,0},{3,1},{4,6},{5,7},{6,4},{7,5},{8,10},{9,11},{10,... | collective-permute-start | bytes 245768 | tf_op jit(solution)/shard_map/ppermute | solution.py:40
  96.7 6.9 %forward.1 = bf16[4,64,1024]{2,1,0:T(8,128)(2,1)S(1)} custom-call(s32[4]{0:T(128)S(1)} %pad_add_fusion.place, bf16[512,1024]{1,0:T(8,128)(2,1)S(1)} %bitcast.61, bf16[2304,512]{1,0:T(8,128)(2,1)S(1)} %flip.1.kernel, f32[256,128]{1,0:T(8,128)S(1)} %copy-done.12), custom_call_target="tpu_custom_call" | custom-call | flops 48318382080 | bytes 1048576 | tf_op jit(solution)/shard_map/forward/pallas_call | solution.py:318
  105.4 2.1 %collective-permute-start.25 = (bf16[64,1024]{1,0:T(8,128)(2,1)S(1)}, bf16[64,1024]{1,0:T(8,128)(2,1)S(1)}, u32[]{:S(2)}, u32[]{:S(2)}) collective-permute-start(bf16[64,1024]{1,0:T(8,128)(2,1)S(1)} %get-tuple-element.86), channel_id=1, source_target_pairs={{0,3},{1,0},{2,1},{3,2},{4,7},{5,4},{6,5},{7,6},{8,11},{9,8},{10,9... | collective-permute-start | bytes 393224 | tf_op jit(solution)/shard_map/ppermute | solution.py:40
  109.3 8.2 %collective-permute-done.23.part1 = bf16[64,1024]{1,0:T(8,128)(2,1)S(1)} collective-permute-done((bf16[64,1024]{1,0:T(8,128)(2,1)S(1)}, bf16[64,1024]{1,0:T(8,128)(2,1)S(1)}, u32[]{:S(2)}, u32[]{:S(2)}) %collective-permute-start.23) | collective-permute-done | bytes 131104 | tf_op jit(solution)/shard_map/ppermute | solution.py:40
  117.6 2.5 %finish.1 = (bf16[4,64,1024]{2,1,0:T(8,128)(2,1)}, bf16[4,64,1024]{2,1,0:T(8,128)(2,1)}, f32[4,64]{1,0:T(4,128)}) custom-call(s32[4]{0:T(128)S(1)} %pad_add_fusion.place, bf16[64,1024]{1,0:T(8,128)(2,1)S(1)} %get-tuple-element.89.part0, bf16[64,1024]{1,0:T(8,128)(2,1)S(1)} %collective-permute-done.23.part1, ...), custom_call_target="tpu_custom_call" | custom-call | flops 10000000 | bytes 1048576 | tf_op jit(solution)/shard_map/finish/pallas_call | solution.py:318
  (103 shorter events, 26.3 us)
Async XLA Ops:
  1.5 9.4 %collective-permute-start = (bf16[9,1024]{1,0:T(8,128)(2,1)S(1)}, bf16[9,1024]{1,0:T(8,128)(2,1)S(1)}, u32[]{:S(2)}, u32[]{:S(2)}) collective-permute-start(bf16[9,1024]{1,0:T(8,128)(2,1)S(1)} %reshape.33), channel_id=1, source_target_pairs={{0,192},{1,193},{2,194},{3,195},{4,196},{5,197},{6,198},{7,199},{8... | collective-permute-start | bytes 55304 | tf_op jit(solution)/shard_map/ppermute | solution.py:40
  11.0 12.1 %collective-permute-start.3 = (bf16[40,1024]{1,0:T(8,128)(2,1)S(1)}, bf16[40,1024]{1,0:T(8,128)(2,1)S(1)}, u32[]{:S(2)}, u32[]{:S(2)}) collective-permute-start(bf16[40,1024]{1,0:T(8,128)(2,1)S(1)} %fusion.6), channel_id=1, source_target_pairs={{0,3},{1,0},{2,1},{3,2},{4,7},{5,4},{6,5},{7,6},{8,11},{9,8},{10,9... | collective-permute-start | bytes 245768 | tf_op jit(solution)/shard_map/ppermute | solution.py:40
  13.8 9.3 %collective-permute-start.4 = (bf16[40,1024]{1,0:T(8,128)(2,1)S(1)}, bf16[40,1024]{1,0:T(8,128)(2,1)S(1)}, u32[]{:S(2)}, u32[]{:S(2)}) collective-permute-start(bf16[40,1024]{1,0:T(8,128)(2,1)S(1)} %fusion.6), channel_id=1, source_target_pairs={{0,2},{1,3},{2,0},{3,1},{4,6},{5,7},{6,4},{7,5},{8,10},{9,11},{10,... | collective-permute-start | bytes 245768 | tf_op jit(solution)/shard_map/ppermute | solution.py:40
  14.6 8.5 %collective-permute-start.5 = (bf16[40,1024]{1,0:T(8,128)(2,1)S(1)}, bf16[40,1024]{1,0:T(8,128)(2,1)S(1)}, u32[]{:S(2)}, u32[]{:S(2)}) collective-permute-start(bf16[40,1024]{1,0:T(8,128)(2,1)S(1)} %fusion.6), channel_id=1, source_target_pairs={{0,1},{1,2},{2,3},{3,0},{4,5},{5,6},{6,7},{7,4},{8,9},{9,10},{10,1... | collective-permute-start | bytes 245768 | tf_op jit(solution)/shard_map/ppermute | solution.py:40
  15.5 35.0 %all-to-all-start = ((bf16[8,64,1024]{2,1,0:T(8,128)(2,1)}), bf16[8,64,1024]{2,1,0:T(8,128)(2,1)S(1)}, u32[]{:S(2)}, u32[]{:S(2)}) async-start(bf16[8,64,1024]{2,1,0:T(8,128)(2,1)} %pad_maximum_fusion), calls=%async_computation | async-start | bytes 2097152 | tf_op jit(solution)/shard_map/all_to_all | solution.py:32
  24.9 15.1 %collective-permute-start.9 = (bf16[4,16,2304]{2,1,0:T(8,128)(2,1)S(1)}, bf16[4,16,2304]{2,1,0:T(8,128)(2,1)S(1)}, u32[]{:S(2)}, u32[]{:S(2)}) collective-permute-start(bf16[4,16,2304]{2,1,0:T(8,128)(2,1)S(1)} %reshape.36.own0), channel_id=1, source_target_pairs={{0,48},{1,49},{2,50},{3,51},{4,52},{5,53},{6,54},{7,55},{8,56},{9,... | collective-permute-start | bytes 884744 | tf_op jit(solution)/shard_map/ppermute | solution.py:40
  28.0 12.0 %collective-permute-start.10 = (bf16[4,16,2304]{2,1,0:T(8,128)(2,1)S(1)}, bf16[4,16,2304]{2,1,0:T(8,128)(2,1)S(1)}, u32[]{:S(2)}, u32[]{:S(2)}) collective-permute-start(bf16[4,16,2304]{2,1,0:T(8,128)(2,1)S(1)} %reshape.36.own0), channel_id=1, source_target_pairs={{0,32},{1,33},{2,34},{3,35},{4,36},{5,37},{6,38},{7,39},{8,40},{9,... | collective-permute-start | bytes 884744 | tf_op jit(solution)/shard_map/ppermute | solution.py:40
  28.6 13.7 %collective-permute-start.11 = (bf16[4,16,2304]{2,1,0:T(8,128)(2,1)S(1)}, bf16[4,16,2304]{2,1,0:T(8,128)(2,1)S(1)}, u32[]{:S(2)}, u32[]{:S(2)}) collective-permute-start(bf16[4,16,2304]{2,1,0:T(8,128)(2,1)S(1)} %reshape.36.own0), channel_id=1, source_target_pairs={{0,16},{1,17},{2,18},{3,19},{4,20},{5,21},{6,22},{7,23},{8,24},{9,... | collective-permute-start | bytes 884744 | tf_op jit(solution)/shard_map/ppermute | solution.py:40
  36.5 14.8 %collective-permute-start.12 = (bf16[4,16,2304]{2,1,0:T(8,128)(2,1)S(1)}, bf16[4,16,2304]{2,1,0:T(8,128)(2,1)S(1)}, u32[]{:S(2)}, u32[]{:S(2)}) collective-permute-start(bf16[4,16,2304]{2,1,0:T(8,128)(2,1)S(1)} %reshape.36.own0), channel_id=1, source_target_pairs={{0,8},{1,9},{2,10},{3,11},{4,12},{5,13},{6,14},{7,15},{8,0},{9,1},... | collective-permute-start | bytes 884744 | tf_op jit(solution)/shard_map/ppermute | solution.py:40
  39.4 11.8 %collective-permute-start.8 = (bf16[64,1024]{1,0:T(8,128)(2,1)}, bf16[64,1024]{1,0:T(8,128)(2,1)}, u32[]{:S(2)}, u32[]{:S(2)}) collective-permute-start(bf16[64,1024]{1,0:T(8,128)(2,1)} %get-tuple-element.50), channel_id=1, source_target_pairs={{0,3},{1,0},{2,1},{3,2},{4,7},{5,4},{6,5},{7,6},{8,11},{9,8},{10,9... | collective-permute-start | bytes 393224 | tf_op jit(solution)/shard_map/ppermute | solution.py:40
  39.9 11.3 %collective-permute-start.13 = (bf16[4,16,2304]{2,1,0:T(8,128)(2,1)S(1)}, bf16[4,16,2304]{2,1,0:T(8,128)(2,1)S(1)}, u32[]{:S(2)}, u32[]{:S(2)}) collective-permute-start(bf16[4,16,2304]{2,1,0:T(8,128)(2,1)S(1)} %collective-permute-done.9.own1), channel_id=1, source_target_pairs={{0,8},{1,9},{2,10},{3,11},{4,12},{5,13},{6,14},{7,15},{8,0},{9,1},... | collective-permute-start | bytes 884744 | tf_op jit(solution)/shard_map/ppermute | solution.py:40
  40.0 11.3 %collective-permute-start.14 = (bf16[4,16,2304]{2,1,0:T(8,128)(2,1)S(1)}, bf16[4,16,2304]{2,1,0:T(8,128)(2,1)S(1)}, u32[]{:S(2)}, u32[]{:S(2)}) collective-permute-start(bf16[4,16,2304]{2,1,0:T(8,128)(2,1)S(1)} %collective-permute-done.10.own2), channel_id=1, source_target_pairs={{0,8},{1,9},{2,10},{3,11},{4,12},{5,13},{6,14},{7,15},{8,0},{9,1},... | collective-permute-start | bytes 884744 | tf_op jit(solution)/shard_map/ppermute | solution.py:40
  42.3 9.0 %collective-permute-start.15 = (bf16[4,16,2304]{2,1,0:T(8,128)(2,1)S(1)}, bf16[4,16,2304]{2,1,0:T(8,128)(2,1)S(1)}, u32[]{:S(2)}, u32[]{:S(2)}) collective-permute-start(bf16[4,16,2304]{2,1,0:T(8,128)(2,1)S(1)} %collective-permute-done.11.own3), channel_id=1, source_target_pairs={{0,8},{1,9},{2,10},{3,11},{4,12},{5,13},{6,14},{7,15},{8,0},{9,1},... | collective-permute-start | bytes 884744 | tf_op jit(solution)/shard_map/ppermute | solution.py:40
  70.5 11.3 %collective-permute-start.17 = (bf16[4,16,2304]{2,1,0:T(8,128)(2,1)}, bf16[4,16,2304]{2,1,0:T(8,128)(2,1)}, u32[]{:S(2)}, u32[]{:S(2)}) collective-permute-start(bf16[4,16,2304]{2,1,0:T(8,128)(2,1)} %get-tuple-element.61), channel_id=1, source_target_pairs={{0,16},{1,17},{2,18},{3,19},{4,20},{5,21},{6,22},{7,23},{8,24},{9,... | collective-permute-start | bytes 884744 | tf_op jit(solution)/shard_map/ppermute | solution.py:40
  72.1 16.6 %collective-permute-start.18 = (bf16[4,16,2304]{2,1,0:T(8,128)(2,1)}, bf16[4,16,2304]{2,1,0:T(8,128)(2,1)}, u32[]{:S(2)}, u32[]{:S(2)}) collective-permute-start(bf16[4,16,2304]{2,1,0:T(8,128)(2,1)} %get-tuple-element.62), channel_id=1, source_target_pairs={{0,32},{1,33},{2,34},{3,35},{4,36},{5,37},{6,38},{7,39},{8,40},{9,... | collective-permute-start | bytes 884744 | tf_op jit(solution)/shard_map/ppermute | solution.py:40
  75.0 13.7 %collective-permute-start.19 = (bf16[4,16,2304]{2,1,0:T(8,128)(2,1)}, bf16[4,16,2304]{2,1,0:T(8,128)(2,1)}, u32[]{:S(2)}, u32[]{:S(2)}) collective-permute-start(bf16[4,16,2304]{2,1,0:T(8,128)(2,1)} %get-tuple-element.63), channel_id=1, source_target_pairs={{0,48},{1,49},{2,50},{3,51},{4,52},{5,53},{6,54},{7,55},{8,56},{9,... | collective-permute-start | bytes 884744 | tf_op jit(solution)/shard_map/ppermute | solution.py:40
  77.8 39.7 %all-to-all-start.1 = ((bf16[8,64,1152]{2,1,0:T(8,128)(2,1)}), bf16[8,64,1152]{2,1,0:T(8,128)(2,1)S(1)}, u32[]{:S(2)}, u32[]{:S(2)}) async-start(bf16[8,64,1152]{2,1,0:T(8,128)(2,1)} %bitcast.58), calls=%async_computation.1 | async-start | bytes 2359296 | tf_op jit(solution)/shard_map/all_to_all | solution.py:32
  91.5 12.2 %collective-permute-start.20 = (bf16[4,80,128]{2,1,0:T(8,128)(2,1)S(1)}, bf16[4,80,128]{2,1,0:T(8,128)(2,1)S(1)}, u32[]{:S(2)}, u32[]{:S(2)}) collective-permute-start(bf16[4,80,128]{2,1,0:T(8,128)(2,1)S(1)} %get-tuple-element.69), channel_id=1, source_target_pairs={{0,1},{1,2},{2,3},{3,0},{4,5},{5,6},{6,7},{7,4},{8,9},{9,10},{10,1... | collective-permute-start | bytes 245768 | tf_op jit(solution)/shard_map/ppermute | solution.py:40
  92.7 11.0 %collective-permute-start.21 = (bf16[4,80,128]{2,1,0:T(8,128)(2,1)S(1)}, bf16[4,80,128]{2,1,0:T(8,128)(2,1)S(1)}, u32[]{:S(2)}, u32[]{:S(2)}) collective-permute-start(bf16[4,80,128]{2,1,0:T(8,128)(2,1)S(1)} %get-tuple-element.70), channel_id=1, source_target_pairs={{0,2},{1,3},{2,0},{3,1},{4,6},{5,7},{6,4},{7,5},{8,10},{9,11},{10,... | collective-permute-start | bytes 245768 | tf_op jit(solution)/shard_map/ppermute | solution.py:40
  103.8 13.7 %collective-permute-start.23 = (bf16[64,1024]{1,0:T(8,128)(2,1)S(1)}, bf16[64,1024]{1,0:T(8,128)(2,1)S(1)}, u32[]{:S(2)}, u32[]{:S(2)}) collective-permute-start(bf16[64,1024]{1,0:T(8,128)(2,1)S(1)} %get-tuple-element.88), channel_id=1, source_target_pairs={{0,1},{1,2},{2,3},{3,0},{4,5},{5,6},{6,7},{7,4},{8,9},{9,10},{10,1... | collective-permute-start | bytes 393224 | tf_op jit(solution)/shard_map/ppermute | solution.py:40
  104.5 13.0 %collective-permute-start.24 = (bf16[64,1024]{1,0:T(8,128)(2,1)S(1)}, bf16[64,1024]{1,0:T(8,128)(2,1)S(1)}, u32[]{:S(2)}, u32[]{:S(2)}) collective-permute-start(bf16[64,1024]{1,0:T(8,128)(2,1)S(1)} %get-tuple-element.87), channel_id=1, source_target_pairs={{0,2},{1,3},{2,0},{3,1},{4,6},{5,7},{6,4},{7,5},{8,10},{9,11},{10,... | collective-permute-start | bytes 393224 | tf_op jit(solution)/shard_map/ppermute | solution.py:40
  105.4 12.1 %collective-permute-start.25 = (bf16[64,1024]{1,0:T(8,128)(2,1)S(1)}, bf16[64,1024]{1,0:T(8,128)(2,1)S(1)}, u32[]{:S(2)}, u32[]{:S(2)}) collective-permute-start(bf16[64,1024]{1,0:T(8,128)(2,1)S(1)} %get-tuple-element.86), channel_id=1, source_target_pairs={{0,3},{1,0},{2,1},{3,2},{4,7},{5,4},{6,5},{7,6},{8,11},{9,8},{10,9... | collective-permute-start | bytes 393224 | tf_op jit(solution)/shard_map/ppermute | solution.py:40
  107.5 12.6 %collective-permute-start.26 = (bf16[80,128]{1,0:T(8,128)(2,1)S(1)}, bf16[80,128]{1,0:T(8,128)(2,1)S(1)}, u32[]{:S(2)}, u32[]{:S(2)}) collective-permute-start(bf16[80,128]{1,0:T(8,128)(2,1)S(1)} %get-tuple-element.96), channel_id=1, source_target_pairs={{0,64},{1,65},{2,66},{3,67},{4,68},{5,69},{6,70},{7,71},{8,72},{9,... | collective-permute-start | bytes 61448 | tf_op jit(solution)/shard_map/ppermute | solution.py:40
  108.4 11.7 %collective-permute-start.27 = (bf16[80,128]{1,0:T(8,128)(2,1)S(1)}, bf16[80,128]{1,0:T(8,128)(2,1)S(1)}, u32[]{:S(2)}, u32[]{:S(2)}) collective-permute-start(bf16[80,128]{1,0:T(8,128)(2,1)S(1)} %get-tuple-element.95), channel_id=1, source_target_pairs={{0,128},{1,129},{2,130},{3,131},{4,132},{5,133},{6,134},{7,135},{8... | collective-permute-start | bytes 61448 | tf_op jit(solution)/shard_map/ppermute | solution.py:40
  (21 other events, 108.2 us)

commit v6 on v4

--- a/solution.py
+++ b/solution.py
@@ -399,7 +399,7 @@
             VM((256, 128), F32),
             pltpu.SemaphoreType.DMA((3,)),
         ],
-        18,
+        54,
         20 * PRODUCT,
         place,
         whole,

time: 120 us -> 119 us (level)
  waiting for transfers between devices: 33.3 us -> 31.1 us
  Pallas kernels: 27.9 us -> 29.4 us
    ppermute x29, waiting for transfers between devices: 25 us -> 22.9 us  [moved_by(): return lax.ppermute(value, BOTH, pairs)]
    unnamed x21 -> x23, local copies, waits for them, and re-layouts: 1.75 us -> 0.1 us
    pallas_call x6, Pallas kernels: 27.9 us -> 29.4 us  [run(): pl.pallas_call(body, out_shape=tuple((jax.ShapeDtypeStruct(*one) for one...]
  transfers between devices with their start and end apart: 31 -> 31, of which waited for: 9 -> 9; matrix products, arithmetic and copies ran while one was open for 4% -> 5% of each run, Pallas kernels for 10% -> 12%
where the time goes in v6:
time: 119 us
  starting transfers between devices  49.4 us (42%)
  waiting for transfers between devices  31.1 us (26%)
  Pallas kernels  29.4 us (25%)
  local copies, waits for them, and re-layouts  5.44 us (5%)
  other arithmetic  2.54 us (2%)
    ppermute x29, starting transfers between devices, moved_by(): return lax.ppermute(value, BOTH, pairs)  37.9 us
    pallas_call x6, Pallas kernels, run(): pl.pallas_call(body, out_shape=tuple((jax.ShapeDtypeStruct(*one) for one...  29.4 us
    ppermute x29, waiting for transfers between devices, moved_by(): return lax.ppermute(value, BOTH, pairs)  22.9 us
    all_to_all x2, starting transfers between devices, exchange(): lax.all_to_all(blocks, BOTH, 0, 0, axis_index_groups=groups, tiled=True)  11.5 us
    all_to_all x2, waiting for transfers between devices, exchange(): lax.all_to_all(blocks, BOTH, 0, 0, axis_index_groups=groups, tiled=True)  8.22 us
  transfers between devices with their start and end apart: 31, of which 9 were waited for; matrix products, arithmetic and copies ran while one was open for 5% of the time, Pallas kernels for 12%

profile of v6, /device:TPU:32, one launch (start us, length us, event | category | flops | bytes accessed | tf_op | source)
XLA Modules:
  0.0 119.0 jit_solution(7301880056241893649)
XLA Ops:
  1.5 1.9 %collective-permute-start = (bf16[9,1024]{1,0:T(8,128)(2,1)S(1)}, bf16[9,1024]{1,0:T(8,128)(2,1)S(1)}, u32[]{:S(2)}, u32[]{:S(2)}) collective-permute-start(bf16[9,1024]{1,0:T(8,128)(2,1)S(1)} %reshape.33), channel_id=1, source_target_pairs={{0,192},{1,193},{2,194},{3,195},{4,196},{5,197},{6,198},{7,199},{8... | collective-permute-start | bytes 55304 | tf_op jit(solution)/shard_map/ppermute | solution.py:40
  3.5 1.5 %collective-permute-start.1 = (bf16[9,1024]{1,0:T(8,128)(2,1)S(1)}, bf16[9,1024]{1,0:T(8,128)(2,1)S(1)}, u32[]{:S(2)}, u32[]{:S(2)}) collective-permute-start(bf16[9,1024]{1,0:T(8,128)(2,1)S(1)} %reshape.33), channel_id=1, source_target_pairs={{0,128},{1,129},{2,130},{3,131},{4,132},{5,133},{6,134},{7,135},{8... | collective-permute-start | bytes 55304 | tf_op jit(solution)/shard_map/ppermute | solution.py:40
  5.0 2.8 %collective-permute-start.2 = (bf16[9,1024]{1,0:T(8,128)(2,1)S(1)}, bf16[9,1024]{1,0:T(8,128)(2,1)S(1)}, u32[]{:S(2)}, u32[]{:S(2)}) collective-permute-start(bf16[9,1024]{1,0:T(8,128)(2,1)S(1)} %reshape.33), channel_id=1, source_target_pairs={{0,64},{1,65},{2,66},{3,67},{4,68},{5,69},{6,70},{7,71},{8,72},{9,... | collective-permute-start | bytes 55304 | tf_op jit(solution)/shard_map/ppermute | solution.py:40
  11.0 2.8 %collective-permute-start.3 = (bf16[40,1024]{1,0:T(8,128)(2,1)S(1)}, bf16[40,1024]{1,0:T(8,128)(2,1)S(1)}, u32[]{:S(2)}, u32[]{:S(2)}) collective-permute-start(bf16[40,1024]{1,0:T(8,128)(2,1)S(1)} %fusion.6), channel_id=1, source_target_pairs={{0,3},{1,0},{2,1},{3,2},{4,7},{5,4},{6,5},{7,6},{8,11},{9,8},{10,9... | collective-permute-start | bytes 245768 | tf_op jit(solution)/shard_map/ppermute | solution.py:40
  15.5 7.6 %all-to-all-start = ((bf16[8,64,1024]{2,1,0:T(8,128)(2,1)}), bf16[8,64,1024]{2,1,0:T(8,128)(2,1)S(1)}, u32[]{:S(2)}, u32[]{:S(2)}) async-start(bf16[8,64,1024]{2,1,0:T(8,128)(2,1)} %pad_maximum_fusion), calls=%async_computation | async-start | bytes 2097152 | tf_op jit(solution)/shard_map/all_to_all | solution.py:32
  24.9 3.1 %collective-permute-start.9 = (bf16[4,16,2304]{2,1,0:T(8,128)(2,1)S(1)}, bf16[4,16,2304]{2,1,0:T(8,128)(2,1)S(1)}, u32[]{:S(2)}, u32[]{:S(2)}) collective-permute-start(bf16[4,16,2304]{2,1,0:T(8,128)(2,1)S(1)} %reshape.36.own0), channel_id=1, source_target_pairs={{0,48},{1,49},{2,50},{3,51},{4,52},{5,53},{6,54},{7,55},{8,56},{9,... | collective-permute-start | bytes 884744 | tf_op jit(solution)/shard_map/ppermute | solution.py:40
  29.6 2.0 %collective-permute-start.6 = (bf16[64,1024]{1,0:T(8,128)(2,1)S(1)}, bf16[64,1024]{1,0:T(8,128)(2,1)S(1)}, u32[]{:S(2)}, u32[]{:S(2)}) collective-permute-start(bf16[64,1024]{1,0:T(8,128)(2,1)S(1)} %get-tuple-element.43), channel_id=1, source_target_pairs={{0,1},{1,2},{2,3},{3,0},{4,5},{5,6},{6,7},{7,4},{8,9},{9,10},{10,1... | collective-permute-start | bytes 393224 | tf_op jit(solution)/shard_map/ppermute | solution.py:40
  31.6 2.7 %collective-permute-start.7 = (bf16[64,1024]{1,0:T(8,128)(2,1)S(1)}, bf16[64,1024]{1,0:T(8,128)(2,1)S(1)}, u32[]{:S(2)}, u32[]{:S(2)}) collective-permute-start(bf16[64,1024]{1,0:T(8,128)(2,1)S(1)} %get-tuple-element.44), channel_id=1, source_target_pairs={{0,2},{1,3},{2,0},{3,1},{4,6},{5,7},{6,4},{7,5},{8,10},{9,11},{10,... | collective-permute-start | bytes 393224 | tf_op jit(solution)/shard_map/ppermute | solution.py:40
  35.8 3.0 %collective-permute-done.7.cot2 = bf16[64,1024]{1,0:T(8,128)(2,1)S(1)} collective-permute-done((bf16[64,1024]{1,0:T(8,128)(2,1)S(1)}, bf16[64,1024]{1,0:T(8,128)(2,1)S(1)}, u32[]{:S(2)}, u32[]{:S(2)}) %collective-permute-start.7) | collective-permute-done | bytes 131104 | tf_op jit(solution)/shard_map/ppermute | solution.py:40
  39.8 2.5 %collective-permute-done.11.own3 = bf16[4,16,2304]{2,1,0:T(8,128)(2,1)S(1)} collective-permute-done((bf16[4,16,2304]{2,1,0:T(8,128)(2,1)S(1)}, bf16[4,16,2304]{2,1,0:T(8,128)(2,1)S(1)}, u32[]{:S(2)}, u32[]{:S(2)}) %collective-permute-start.11) | collective-permute-done | bytes 294944 | tf_op jit(solution)/shard_map/ppermute | solution.py:40
  42.3 8.2 %all-to-all-done = bf16[8,64,1024]{2,1,0:T(8,128)(2,1)S(1)} async-done(((bf16[8,64,1024]{2,1,0:T(8,128)(2,1)}), bf16[8,64,1024]{2,1,0:T(8,128)(2,1)S(1)}, u32[]{:S(2)}, u32[]{:S(2)}) %all-to-all-start) | async-done | bytes 1048608 | tf_op jit(solution)/shard_map/all_to_all | solution.py:32
  51.8 14.7 %gradient.1 = (f32[256,128]{1,0:T(8,128)S(1)}, bf16[4,4,16,2304]{3,2,1,0:T(8,128)(2,1)S(1)}, f32[4,4,16,2304]{3,2,1,0:T(8,128)S(1)}, bf16[512,1152]{1,0:T(8,128)(2,1)}, bf16[512,2304]{1,0:T(8,128)(2,1)S(1)}) custom-call(s32[4]{0:T(128)S(1)} %ready.1.place, f32[8,512]{1,0:T(8,128)S(1)} %broadcast_in_dim.7.style, bf16[64,1024]{1,0:T(8,128)(2,1)S(1)} %get-tuple-element.42.cot0, ...), custom_call_target="tpu_custom_call" | custom-call | flops 4831838208 | bytes 1048576 | tf_op jit(solution)/shard_map/gradient/pallas_call | solution.py:305
  66.6 2.8 %collective-permute-done.16.received = bf16[4,4,16,2304]{3,2,1,0:T(8,128)(2,1)S(1)} collective-permute-done((bf16[4,4,16,2304]{3,2,1,0:T(8,128)(2,1)S(1)}, bf16[4,4,16,2304]{3,2,1,0:T(8,128)(2,1)S(1)}, u32[]{:S(2)}, u32[]{:S(2)}) %collective-permute-start.16) | collective-permute-done | bytes 1179680 | tf_op jit(solution)/shard_map/ppermute | solution.py:40
  69.8 1.6 %collective-permute-start.17 = (bf16[4,16,2304]{2,1,0:T(8,128)(2,1)S(1)}, bf16[4,16,2304]{2,1,0:T(8,128)(2,1)S(1)}, u32[]{:S(2)}, u32[]{:S(2)}) collective-permute-start(bf16[4,16,2304]{2,1,0:T(8,128)(2,1)S(1)} %get-tuple-element.55), channel_id=1, source_target_pairs={{0,16},{1,17},{2,18},{3,19},{4,20},{5,21},{6,22},{7,23},{8,24},{9,... | collective-permute-start | bytes 884744 | tf_op jit(solution)/shard_map/ppermute | solution.py:40
  71.4 2.9 %collective-permute-start.18 = (bf16[4,16,2304]{2,1,0:T(8,128)(2,1)S(1)}, bf16[4,16,2304]{2,1,0:T(8,128)(2,1)S(1)}, u32[]{:S(2)}, u32[]{:S(2)}) collective-permute-start(bf16[4,16,2304]{2,1,0:T(8,128)(2,1)S(1)} %get-tuple-element.56), channel_id=1, source_target_pairs={{0,32},{1,33},{2,34},{3,35},{4,36},{5,37},{6,38},{7,39},{8,40},{9,... | collective-permute-start | bytes 884744 | tf_op jit(solution)/shard_map/ppermute | solution.py:40
  75.6 4.0 %all-to-all-start.1 = ((bf16[8,64,1152]{2,1,0:T(8,128)(2,1)}), bf16[8,64,1152]{2,1,0:T(8,128)(2,1)S(1)}, u32[]{:S(2)}, u32[]{:S(2)}) async-start(bf16[8,64,1152]{2,1,0:T(8,128)(2,1)} %bitcast.20), calls=%async_computation.1 | async-start | bytes 2359296 | tf_op jit(solution)/shard_map/all_to_all | solution.py:32
  80.1 7.5 %collective-permute-done.18.part2 = bf16[4,16,2304]{2,1,0:T(8,128)(2,1)S(1)} collective-permute-done((bf16[4,16,2304]{2,1,0:T(8,128)(2,1)S(1)}, bf16[4,16,2304]{2,1,0:T(8,128)(2,1)S(1)}, u32[]{:S(2)}, u32[]{:S(2)}) %collective-permute-start.18) | collective-permute-done | bytes 294944 | tf_op jit(solution)/shard_map/ppermute | solution.py:40
  90.0 2.6 %collective-permute-start.21 = (bf16[4,80,128]{2,1,0:T(8,128)(2,1)S(1)}, bf16[4,80,128]{2,1,0:T(8,128)(2,1)S(1)}, u32[]{:S(2)}, u32[]{:S(2)}) collective-permute-start(bf16[4,80,128]{2,1,0:T(8,128)(2,1)S(1)} %get-tuple-element.60), channel_id=1, source_target_pairs={{0,2},{1,3},{2,0},{3,1},{4,6},{5,7},{6,4},{7,5},{8,10},{9,11},{10,... | collective-permute-start | bytes 245768 | tf_op jit(solution)/shard_map/ppermute | solution.py:40
  92.6 1.5 %collective-permute-start.22 = (bf16[4,80,128]{2,1,0:T(8,128)(2,1)S(1)}, bf16[4,80,128]{2,1,0:T(8,128)(2,1)S(1)}, u32[]{:S(2)}, u32[]{:S(2)}) collective-permute-start(bf16[4,80,128]{2,1,0:T(8,128)(2,1)S(1)} %get-tuple-element.61), channel_id=1, source_target_pairs={{0,3},{1,0},{2,1},{3,2},{4,7},{5,4},{6,5},{7,6},{8,11},{9,8},{10,9... | collective-permute-start | bytes 245768 | tf_op jit(solution)/shard_map/ppermute | solution.py:40
  94.1 9.6 %forward.1 = bf16[4,64,1024]{2,1,0:T(8,128)(2,1)} custom-call(s32[4]{0:T(128)} %copy-done.3, bf16[512,1024]{1,0:T(8,128)(2,1)} %bitcast.60, bf16[512,2304]{1,0:T(8,128)(2,1)} %copy-done.5, f32[256,128]{1,0:T(8,128)} %copy-done.6), custom_call_target="tpu_custom_call" | custom-call | flops 48318382080 | bytes 1048576 | tf_op jit(solution)/shard_map/forward/pallas_call | solution.py:305
  106.6 2.1 %collective-permute-start.25 = (bf16[64,1024]{1,0:T(8,128)(2,1)S(1)}, bf16[64,1024]{1,0:T(8,128)(2,1)S(1)}, u32[]{:S(2)}, u32[]{:S(2)}) collective-permute-start(bf16[64,1024]{1,0:T(8,128)(2,1)S(1)} %get-tuple-element.76), channel_id=1, source_target_pairs={{0,3},{1,0},{2,1},{3,2},{4,7},{5,4},{6,5},{7,6},{8,11},{9,8},{10,9... | collective-permute-start | bytes 393224 | tf_op jit(solution)/shard_map/ppermute | solution.py:40
  110.5 2.3 %collective-permute-done.23.part1 = bf16[64,1024]{1,0:T(8,128)(2,1)S(1)} collective-permute-done((bf16[64,1024]{1,0:T(8,128)(2,1)S(1)}, bf16[64,1024]{1,0:T(8,128)(2,1)S(1)}, u32[]{:S(2)}, u32[]{:S(2)}) %collective-permute-start.23) | collective-permute-done | bytes 131104 | tf_op jit(solution)/shard_map/ppermute | solution.py:40
  112.8 2.7 %collective-permute-done.24.part2 = bf16[64,1024]{1,0:T(8,128)(2,1)S(1)} collective-permute-done((bf16[64,1024]{1,0:T(8,128)(2,1)S(1)}, bf16[64,1024]{1,0:T(8,128)(2,1)S(1)}, u32[]{:S(2)}, u32[]{:S(2)}) %collective-permute-start.24) | collective-permute-done | bytes 131104 | tf_op jit(solution)/shard_map/ppermute | solution.py:40
  115.7 2.5 %finish.1 = (bf16[4,64,1024]{2,1,0:T(8,128)(2,1)}, bf16[4,64,1024]{2,1,0:T(8,128)(2,1)}, f32[4,64]{1,0:T(4,128)}) custom-call(s32[4]{0:T(128)S(1)} %copy-done.4, bf16[64,1024]{1,0:T(8,128)(2,1)S(1)} %get-tuple-element.79.part0, bf16[64,1024]{1,0:T(8,128)(2,1)S(1)} %collective-permute-done.23.part1, bf16[64,1024]{1,0:T(8,128)(2,1)S(1)} %collective-permute-done.24.part2, ...), custom_call_target="tpu_custom_call" | custom-call | flops 10000000 | bytes 1048576 | tf_op jit(solution)/shard_map/finish/pallas_call | solution.py:305
  (90 shorter events, 22.9 us)
Async XLA Ops:
  1.5 9.4 %collective-permute-start = (bf16[9,1024]{1,0:T(8,128)(2,1)S(1)}, bf16[9,1024]{1,0:T(8,128)(2,1)S(1)}, u32[]{:S(2)}, u32[]{:S(2)}) collective-permute-start(bf16[9,1024]{1,0:T(8,128)(2,1)S(1)} %reshape.33), channel_id=1, source_target_pairs={{0,192},{1,193},{2,194},{3,195},{4,196},{5,197},{6,198},{7,199},{8... | collective-permute-start | bytes 55304 | tf_op jit(solution)/shard_map/ppermute | solution.py:40
  11.0 12.1 %collective-permute-start.3 = (bf16[40,1024]{1,0:T(8,128)(2,1)S(1)}, bf16[40,1024]{1,0:T(8,128)(2,1)S(1)}, u32[]{:S(2)}, u32[]{:S(2)}) collective-permute-start(bf16[40,1024]{1,0:T(8,128)(2,1)S(1)} %fusion.6), channel_id=1, source_target_pairs={{0,3},{1,0},{2,1},{3,2},{4,7},{5,4},{6,5},{7,6},{8,11},{9,8},{10,9... | collective-permute-start | bytes 245768 | tf_op jit(solution)/shard_map/ppermute | solution.py:40
  13.9 9.3 %collective-permute-start.4 = (bf16[40,1024]{1,0:T(8,128)(2,1)S(1)}, bf16[40,1024]{1,0:T(8,128)(2,1)S(1)}, u32[]{:S(2)}, u32[]{:S(2)}) collective-permute-start(bf16[40,1024]{1,0:T(8,128)(2,1)S(1)} %fusion.6), channel_id=1, source_target_pairs={{0,2},{1,3},{2,0},{3,1},{4,6},{5,7},{6,4},{7,5},{8,10},{9,11},{10,... | collective-permute-start | bytes 245768 | tf_op jit(solution)/shard_map/ppermute | solution.py:40
  14.7 8.5 %collective-permute-start.5 = (bf16[40,1024]{1,0:T(8,128)(2,1)S(1)}, bf16[40,1024]{1,0:T(8,128)(2,1)S(1)}, u32[]{:S(2)}, u32[]{:S(2)}) collective-permute-start(bf16[40,1024]{1,0:T(8,128)(2,1)S(1)} %fusion.6), channel_id=1, source_target_pairs={{0,1},{1,2},{2,3},{3,0},{4,5},{5,6},{6,7},{7,4},{8,9},{9,10},{10,1... | collective-permute-start | bytes 245768 | tf_op jit(solution)/shard_map/ppermute | solution.py:40
  15.5 35.0 %all-to-all-start = ((bf16[8,64,1024]{2,1,0:T(8,128)(2,1)}), bf16[8,64,1024]{2,1,0:T(8,128)(2,1)S(1)}, u32[]{:S(2)}, u32[]{:S(2)}) async-start(bf16[8,64,1024]{2,1,0:T(8,128)(2,1)} %pad_maximum_fusion), calls=%async_computation | async-start | bytes 2097152 | tf_op jit(solution)/shard_map/all_to_all | solution.py:32
  24.9 14.4 %collective-permute-start.9 = (bf16[4,16,2304]{2,1,0:T(8,128)(2,1)S(1)}, bf16[4,16,2304]{2,1,0:T(8,128)(2,1)S(1)}, u32[]{:S(2)}, u32[]{:S(2)}) collective-permute-start(bf16[4,16,2304]{2,1,0:T(8,128)(2,1)S(1)} %reshape.36.own0), channel_id=1, source_target_pairs={{0,48},{1,49},{2,50},{3,51},{4,52},{5,53},{6,54},{7,55},{8,56},{9,... | collective-permute-start | bytes 884744 | tf_op jit(solution)/shard_map/ppermute | solution.py:40
  28.0 11.3 %collective-permute-start.10 = (bf16[4,16,2304]{2,1,0:T(8,128)(2,1)S(1)}, bf16[4,16,2304]{2,1,0:T(8,128)(2,1)S(1)}, u32[]{:S(2)}, u32[]{:S(2)}) collective-permute-start(bf16[4,16,2304]{2,1,0:T(8,128)(2,1)S(1)} %reshape.36.own0), channel_id=1, source_target_pairs={{0,32},{1,33},{2,34},{3,35},{4,36},{5,37},{6,38},{7,39},{8,40},{9,... | collective-permute-start | bytes 884744 | tf_op jit(solution)/shard_map/ppermute | solution.py:40
  28.6 13.7 %collective-permute-start.11 = (bf16[4,16,2304]{2,1,0:T(8,128)(2,1)S(1)}, bf16[4,16,2304]{2,1,0:T(8,128)(2,1)S(1)}, u32[]{:S(2)}, u32[]{:S(2)}) collective-permute-start(bf16[4,16,2304]{2,1,0:T(8,128)(2,1)S(1)} %reshape.36.own0), channel_id=1, source_target_pairs={{0,16},{1,17},{2,18},{3,19},{4,20},{5,21},{6,22},{7,23},{8,24},{9,... | collective-permute-start | bytes 884744 | tf_op jit(solution)/shard_map/ppermute | solution.py:40
  35.8 15.9 %collective-permute-start.12 = (bf16[4,16,2304]{2,1,0:T(8,128)(2,1)S(1)}, bf16[4,16,2304]{2,1,0:T(8,128)(2,1)S(1)}, u32[]{:S(2)}, u32[]{:S(2)}) collective-permute-start(bf16[4,16,2304]{2,1,0:T(8,128)(2,1)S(1)} %reshape.36.own0), channel_id=1, source_target_pairs={{0,8},{1,9},{2,10},{3,11},{4,12},{5,13},{6,14},{7,15},{8,0},{9,1},... | collective-permute-start | bytes 884744 | tf_op jit(solution)/shard_map/ppermute | solution.py:40
  38.8 12.9 %collective-permute-start.8 = (bf16[64,1024]{1,0:T(8,128)(2,1)}, bf16[64,1024]{1,0:T(8,128)(2,1)}, u32[]{:S(2)}, u32[]{:S(2)}) collective-permute-start(bf16[64,1024]{1,0:T(8,128)(2,1)} %get-tuple-element.45), channel_id=1, source_target_pairs={{0,3},{1,0},{2,1},{3,2},{4,7},{5,4},{6,5},{7,6},{8,11},{9,8},{10,9... | collective-permute-start | bytes 393224 | tf_op jit(solution)/shard_map/ppermute | solution.py:40
  39.3 12.4 %collective-permute-start.13 = (bf16[4,16,2304]{2,1,0:T(8,128)(2,1)S(1)}, bf16[4,16,2304]{2,1,0:T(8,128)(2,1)S(1)}, u32[]{:S(2)}, u32[]{:S(2)}) collective-permute-start(bf16[4,16,2304]{2,1,0:T(8,128)(2,1)S(1)} %collective-permute-done.9.own1), channel_id=1, source_target_pairs={{0,8},{1,9},{2,10},{3,11},{4,12},{5,13},{6,14},{7,15},{8,0},{9,1},... | collective-permute-start | bytes 884744 | tf_op jit(solution)/shard_map/ppermute | solution.py:40
  39.3 12.4 %collective-permute-start.14 = (bf16[4,16,2304]{2,1,0:T(8,128)(2,1)S(1)}, bf16[4,16,2304]{2,1,0:T(8,128)(2,1)S(1)}, u32[]{:S(2)}, u32[]{:S(2)}) collective-permute-start(bf16[4,16,2304]{2,1,0:T(8,128)(2,1)S(1)} %collective-permute-done.10.own2), channel_id=1, source_target_pairs={{0,8},{1,9},{2,10},{3,11},{4,12},{5,13},{6,14},{7,15},{8,0},{9,1},... | collective-permute-start | bytes 884744 | tf_op jit(solution)/shard_map/ppermute | solution.py:40
  42.3 9.4 %collective-permute-start.15 = (bf16[4,16,2304]{2,1,0:T(8,128)(2,1)S(1)}, bf16[4,16,2304]{2,1,0:T(8,128)(2,1)}, u32[]{:S(2)}, u32[]{:S(2)}) collective-permute-start(bf16[4,16,2304]{2,1,0:T(8,128)(2,1)S(1)} %collective-permute-done.11.own3), channel_id=1, source_target_pairs={{0,8},{1,9},{2,10},{3,11},{4,12},{5,13},{6,14},{7,15},{8,0},{9,1},... | collective-permute-start | bytes 884744 | tf_op jit(solution)/shard_map/ppermute | solution.py:40
  69.8 10.4 %collective-permute-start.17 = (bf16[4,16,2304]{2,1,0:T(8,128)(2,1)S(1)}, bf16[4,16,2304]{2,1,0:T(8,128)(2,1)S(1)}, u32[]{:S(2)}, u32[]{:S(2)}) collective-permute-start(bf16[4,16,2304]{2,1,0:T(8,128)(2,1)S(1)} %get-tuple-element.55), channel_id=1, source_target_pairs={{0,16},{1,17},{2,18},{3,19},{4,20},{5,21},{6,22},{7,23},{8,24},{9,... | collective-permute-start | bytes 884744 | tf_op jit(solution)/shard_map/ppermute | solution.py:40
  71.4 16.2 %collective-permute-start.18 = (bf16[4,16,2304]{2,1,0:T(8,128)(2,1)S(1)}, bf16[4,16,2304]{2,1,0:T(8,128)(2,1)S(1)}, u32[]{:S(2)}, u32[]{:S(2)}) collective-permute-start(bf16[4,16,2304]{2,1,0:T(8,128)(2,1)S(1)} %get-tuple-element.56), channel_id=1, source_target_pairs={{0,32},{1,33},{2,34},{3,35},{4,36},{5,37},{6,38},{7,39},{8,40},{9,... | collective-permute-start | bytes 884744 | tf_op jit(solution)/shard_map/ppermute | solution.py:40
  74.3 13.3 %collective-permute-start.19 = (bf16[4,16,2304]{2,1,0:T(8,128)(2,1)S(1)}, bf16[4,16,2304]{2,1,0:T(8,128)(2,1)S(1)}, u32[]{:S(2)}, u32[]{:S(2)}) collective-permute-start(bf16[4,16,2304]{2,1,0:T(8,128)(2,1)S(1)} %get-tuple-element.57), channel_id=1, source_target_pairs={{0,48},{1,49},{2,50},{3,51},{4,52},{5,53},{6,54},{7,55},{8,56},{9,... | collective-permute-start | bytes 884744 | tf_op jit(solution)/shard_map/ppermute | solution.py:40
  75.6 39.9 %all-to-all-start.1 = ((bf16[8,64,1152]{2,1,0:T(8,128)(2,1)}), bf16[8,64,1152]{2,1,0:T(8,128)(2,1)S(1)}, u32[]{:S(2)}, u32[]{:S(2)}) async-start(bf16[8,64,1152]{2,1,0:T(8,128)(2,1)} %bitcast.20), calls=%async_computation.1 | async-start | bytes 2359296 | tf_op jit(solution)/shard_map/all_to_all | solution.py:32
  88.8 15.0 %collective-permute-start.20 = (bf16[4,80,128]{2,1,0:T(8,128)(2,1)S(1)}, bf16[4,80,128]{2,1,0:T(8,128)(2,1)S(1)}, u32[]{:S(2)}, u32[]{:S(2)}) collective-permute-start(bf16[4,80,128]{2,1,0:T(8,128)(2,1)S(1)} %get-tuple-element.59), channel_id=1, source_target_pairs={{0,1},{1,2},{2,3},{3,0},{4,5},{5,6},{6,7},{7,4},{8,9},{9,10},{10,1... | collective-permute-start | bytes 245768 | tf_op jit(solution)/shard_map/ppermute | solution.py:40
  90.0 13.8 %collective-permute-start.21 = (bf16[4,80,128]{2,1,0:T(8,128)(2,1)S(1)}, bf16[4,80,128]{2,1,0:T(8,128)(2,1)S(1)}, u32[]{:S(2)}, u32[]{:S(2)}) collective-permute-start(bf16[4,80,128]{2,1,0:T(8,128)(2,1)S(1)} %get-tuple-element.60), channel_id=1, source_target_pairs={{0,2},{1,3},{2,0},{3,1},{4,6},{5,7},{6,4},{7,5},{8,10},{9,11},{10,... | collective-permute-start | bytes 245768 | tf_op jit(solution)/shard_map/ppermute | solution.py:40
  92.6 11.2 %collective-permute-start.22 = (bf16[4,80,128]{2,1,0:T(8,128)(2,1)S(1)}, bf16[4,80,128]{2,1,0:T(8,128)(2,1)S(1)}, u32[]{:S(2)}, u32[]{:S(2)}) collective-permute-start(bf16[4,80,128]{2,1,0:T(8,128)(2,1)S(1)} %get-tuple-element.61), channel_id=1, source_target_pairs={{0,3},{1,0},{2,1},{3,2},{4,7},{5,4},{6,5},{7,6},{8,11},{9,8},{10,9... | collective-permute-start | bytes 245768 | tf_op jit(solution)/shard_map/ppermute | solution.py:40
  105.7 9.9 %collective-permute-start.24 = (bf16[64,1024]{1,0:T(8,128)(2,1)S(1)}, bf16[64,1024]{1,0:T(8,128)(2,1)S(1)}, u32[]{:S(2)}, u32[]{:S(2)}) collective-permute-start(bf16[64,1024]{1,0:T(8,128)(2,1)S(1)} %get-tuple-element.77), channel_id=1, source_target_pairs={{0,2},{1,3},{2,0},{3,1},{4,6},{5,7},{6,4},{7,5},{8,10},{9,11},{10,... | collective-permute-start | bytes 393224 | tf_op jit(solution)/shard_map/ppermute | solution.py:40
  106.6 8.9 %collective-permute-start.25 = (bf16[64,1024]{1,0:T(8,128)(2,1)S(1)}, bf16[64,1024]{1,0:T(8,128)(2,1)S(1)}, u32[]{:S(2)}, u32[]{:S(2)}) collective-permute-start(bf16[64,1024]{1,0:T(8,128)(2,1)S(1)} %get-tuple-element.76), channel_id=1, source_target_pairs={{0,3},{1,0},{2,1},{3,2},{4,7},{5,4},{6,5},{7,6},{8,11},{9,8},{10,9... | collective-permute-start | bytes 393224 | tf_op jit(solution)/shard_map/ppermute | solution.py:40
  108.7 9.4 %collective-permute-start.26 = (bf16[80,128]{1,0:T(8,128)(2,1)S(1)}, bf16[80,128]{1,0:T(8,128)(2,1)S(1)}, u32[]{:S(2)}, u32[]{:S(2)}) collective-permute-start(bf16[80,128]{1,0:T(8,128)(2,1)S(1)} %get-tuple-element.86), channel_id=1, source_target_pairs={{0,64},{1,65},{2,66},{3,67},{4,68},{5,69},{6,70},{7,71},{8,72},{9,... | collective-permute-start | bytes 61448 | tf_op jit(solution)/shard_map/ppermute | solution.py:40
  109.6 8.5 %collective-permute-start.27 = (bf16[80,128]{1,0:T(8,128)(2,1)S(1)}, bf16[80,128]{1,0:T(8,128)(2,1)S(1)}, u32[]{:S(2)}, u32[]{:S(2)}) collective-permute-start(bf16[80,128]{1,0:T(8,128)(2,1)S(1)} %get-tuple-element.85), channel_id=1, source_target_pairs={{0,128},{1,129},{2,130},{3,131},{4,132},{5,133},{6,134},{7,135},{8... | collective-permute-start | bytes 61448 | tf_op jit(solution)/shard_map/ppermute | solution.py:40
  (15 other events, 137.2 us)
